TPU v7x, 128 devices: a whole 4x4x4 slice. The times are simulated.
128 devices in a mesh: space: 16 (over y, z), member: 8 (over x, core).
Axes of the slice: x: 4, y: 4, z: 4, core: 2. Of those that a mesh axis runs over, the one named last changes fastest.
Arguments:
- state_field: bfloat16 [8, 96, 1024, 256], P('member', None, 'space'), may hold values from -2.5 to 2.5
- context_field: bfloat16 [96, 1024, 256], P('member', 'space'), may hold values from -6 to 6
- noise_latent: bfloat16 [8, 1, 8, 1024, 256], P('member', None, None, 'space'), may hold values from -6 to 6
- gate_kernel: bfloat16 [192, 200, 3, 3], replicated, may hold values from -0.125 to 0.125
- candidate_kernel: bfloat16 [96, 200, 3, 3], replicated, may hold values from -0.125 to 0.125
- active_tiles: int32 [16, 4], replicated, may hold values from 0 to 1, as said below
- tile_offset: int32 [16, 4], replicated, may hold values from 0 to 3, as said below
Outputs:
- next_state: bfloat16 [8, 96, 1024, 256], P('member', None, 'space')
Inputs may be any that keep to these rules, and one draw needn't show every extreme that they name: `active_tiles`: each owner has between 1 and 3 active tiles, and some owner has exactly 3; its tile with tile_offset 0 is always active. Each row is a permutation of 0 .. 3; active tiles have tile_offset below 3. An active tile of owner s with tile_offset k is computed by owner (s + k) mod 16; each owner computes at most 2 tiles counting its own, and some owner computes exactly 2.
All inputs are finite; a program needn't handle non-finite values.
Results may differ from a plain program's by a relative error of at most 0.001.
Values may be sent and summed in bfloat16 or wider, within the bound.
No kernel may reach another device: no remote copies, remote signals or barrier semaphores. Data moves between devices by JAX's collectives and lax.ppermute only.
A program may use at most 128 MiB of HBM per device.

v0:
```python
import jax
import jax.numpy as jnp
from jax import lax
from jax.sharding import PartitionSpec as P

STATE_CH = 96
CONTEXT_CH = 96
NOISE_CH = 8
TILE = 64
STEPS = 1
REACH = 3
HALO = 2


def with_halo(x, sides, width):
    for axis, dim in sides:
        size, length = (lax.axis_size(axis), x.shape[dim])
        up = [(i, (i + 1) % size) for i in range(size - 1)]
        down = [(j, i) for i, j in up]
        last = lax.slice_in_dim(x, length - width, length, axis=dim)
        first = lax.slice_in_dim(x, 0, width, axis=dim)
        before = lax.ppermute(last, axis, up)
        after = lax.ppermute(first, axis, down)
        x = jnp.concatenate([before, x, after], axis=dim)
    return x


def shifted(x, axis, by):
    length = lax.axis_size(axis)
    return lax.ppermute(x, axis, [(i, (i + by) % length) for i in range(length)])


def convolve(inputs, kernel):
    return lax.conv_general_dilated(
        inputs,
        kernel,
        (1, 1),
        "VALID",
        dimension_numbers=("NCHW", "OIHW", "NCHW"),
        preferred_element_type=jnp.float32,
    )


def trimmed(values, margin):
    return values[:, :, margin : values.shape[2] - margin, margin : values.shape[3] - margin]


def recurrent_step(carried, context, noise_part, gate_kernel, candidate_kernel):
    joined = jnp.concatenate([carried, context, noise_part], axis=1)
    gate_terms = convolve(joined, gate_kernel)
    update = jax.nn.sigmoid(gate_terms[:, :STATE_CH])
    reset_gate = jax.nn.sigmoid(gate_terms[:, STATE_CH:])
    reset_state = (reset_gate * trimmed(carried, 1).astype(jnp.float32)).astype(jnp.bfloat16)
    joined = jnp.concatenate([reset_state, trimmed(context, 1), trimmed(noise_part, 1)], axis=1)
    proposal = jnp.tanh(convolve(joined, candidate_kernel))
    update = trimmed(update, 1)
    return (1.0 - update) * trimmed(carried, 2).astype(jnp.float32) + update * proposal


def advance(window, gate_kernel, candidate_kernel):
    carried = window[:, :STATE_CH]
    context = window[:, STATE_CH : STATE_CH + CONTEXT_CH]
    noises = window[:, STATE_CH + CONTEXT_CH :]
    carried = recurrent_step(
        carried, trimmed(context, 0), trimmed(noises, 0), gate_kernel, candidate_kernel
    ).astype(jnp.bfloat16)
    return carried


def tile_choice(active_tiles, tile_offset, owner_index, offset):
    row_active = lax.dynamic_index_in_dim(active_tiles, owner_index, 0, keepdims=False)
    row_offset = lax.dynamic_index_in_dim(tile_offset, owner_index, 0, keepdims=False)
    selected = (row_active == 1) & (row_offset == offset)
    tile_index = lax.iota(jnp.int32, row_active.shape[0])
    return (jnp.any(selected), jnp.sum(jnp.where(selected, tile_index, 0)))


def column_window(values, column):
    channels = values.shape[0]
    rows_here = values.shape[1]
    breadth = values.shape[2]
    start = column * TILE
    zero = jnp.int32(0)
    middle = lax.dynamic_slice(values, (zero, zero, start), (channels, rows_here, TILE))
    left = lax.dynamic_slice(
        values, (zero, zero, jnp.maximum(start - HALO, 0)), (channels, rows_here, HALO)
    )
    right = lax.dynamic_slice(
        values, (zero, zero, jnp.minimum(start + TILE, breadth - HALO)), (channels, rows_here, HALO)
    )
    left = jnp.where(column > 0, left, jnp.zeros_like(left))
    right = jnp.where(column < breadth // TILE - 1, right, jnp.zeros_like(right))
    return jnp.concatenate([left, middle, right], axis=2)


def shards(
    state_field,
    context_field,
    noise_latent,
    gate_kernel,
    candidate_kernel,
    active_tiles,
    tile_offset,
):
    owners = lax.axis_size("space")
    position = lax.axis_index("space")
    height = state_field.shape[2]
    breadth = state_field.shape[3]
    context_rows = lax.all_gather(context_field, "member", axis=0, tiled=True)
    groups = [
        state_field[0],
        context_rows,
        noise_latent[0].reshape(STEPS * NOISE_CH, height, breadth),
    ]
    edges = jnp.concatenate(
        [jnp.concatenate([group[:, :HALO], group[:, height - HALO :]], axis=1) for group in groups],
        axis=0,
    )
    rimmed_edges = with_halo(edges, (("space", 1),), HALO)
    above = rimmed_edges[:, :HALO]
    below = rimmed_edges[:, 3 * HALO :]
    columns = []
    windows = []
    for offset in range(REACH):
        in_use, column = tile_choice(active_tiles, tile_offset, position, offset)
        columns.append((in_use, column))
        pieces = []
        first = 0
        for group in groups:
            count = group.shape[0]
            pieces.append(
                jnp.concatenate(
                    [
                        column_window(above[first : first + count], column),
                        column_window(group, column),
                        column_window(below[first : first + count], column),
                    ],
                    axis=1,
                )
            )
            first = first + count
        windows.append(jnp.concatenate(pieces, axis=0))
    second = jnp.zeros_like(windows[0])
    for offset in range(1, REACH):
        arrived = shifted(windows[offset], "space", offset)
        source = (position - offset) % owners
        taken, unused_column = tile_choice(active_tiles, tile_offset, source, offset)
        second = jnp.where(taken, arrived, second)
    batch_tiles = jnp.stack([windows[0], second])
    results = advance(batch_tiles, gate_kernel, candidate_kernel)
    returned = [results[0]]
    for offset in range(1, REACH):
        returned.append(shifted(results[1], "space", -offset))
    updated = state_field[0]
    for offset in range(REACH):
        in_use, column = columns[offset]
        start = column * TILE
        current = lax.dynamic_slice(updated, (0, 0, start), (STATE_CH, TILE, TILE))
        updated = lax.dynamic_update_slice(
            updated, jnp.where(in_use, returned[offset], current), (0, 0, start)
        )
    return updated[None]


def solution(mesh):
    return jax.shard_map(
        shards,
        mesh=mesh,
        in_specs=(
            P("member", None, "space", None),
            P("member", "space", None),
            P("member", None, None, "space", None),
            P(),
            P(),
            P(),
            P(),
        ),
        out_specs=P("member", None, "space", None),
        check_vma=False,
    )
```

profile of v0, /device:TPU:64, one launch (start us, length us, event | category | flops | bytes accessed | tf_op | source)
XLA Modules:
  0.0 771.7 jit_solution(8043122561504480645)
XLA Ops:
  27.4 7.2 copy.151
  35.5 5.6 constant_dynamic-slice_fusion.18
  41.0 4.6 copy.171
  48.6 3.9 copy.164
  52.5 3.4 copy.157
  67.9 3.6 collective-permute-start
  73.8 11.5 %constant_dynamic-slice_fusion.11 = (bf16[96,64,2]{2,1,0:T(8,128)(2,1)}, bf16[96,64,2]{2,1,0:T(8,128)(2,1)}, bf16[96,64,2]{2,1,0:T(8,128)(2,1)}, bf16[96,64,2]{2...) fusion(bf16[96,64,256]{2,1,0:T(8,128)(2,1)} %all-gather.2.cloned.1.call-done, s32[]{:T(128)S(6)} %max.8, ...), kind=kLoop, calls=%fused_computation.88 | loop fusion | bytes 294936 | tf_op jit(solution)/shard_map/dynamic_slice | solution.py:85
  85.3 3.0 copy.194
  88.9 3.0 copy.192
  92.5 6.1 constant_dynamic-slice_fusion.10
  98.6 4.6 copy.193
  103.2 3.0 copy.191
  106.8 3.6 copy.189
  110.4 4.6 copy.190
  120.4 4.9 copy.187
  131.2 14.6 %maximum_maximum_fusion.1 = bf16[200,68,68]{0,1,2:T(8,128)(2,1)S(1)} fusion(bf16[8,2,2]{0,1,2:T(2,128)(2,1)S(1)} %get-tuple-element.102, bf16[8,2,64]{0,1,2:T(2,128)(2,1)S(1)} %get-tuple-element.107, bf16[8,2,2]{0,1,2:T(2,128)(2,1)S(1)} %get-tuple-element.101, bf16[8,64,68]{0,1,2:T(8,128)(2,1)S(1)} %copy-done.9, bf16[8,2,2]{0,1,2:T(2,128)(2,1)S(1)} %get-tuple-element.93, ...), kind=kLoop, calls=%fused_computation.40 | loop fusion | flops 46240000 | bytes 3699200 | tf_op jit(solution)/shard_map/concatenate | solution.py:142
  147.7 13.0 %maximum_maximum_fusion = bf16[200,68,68]{0,1,2:T(8,128)(2,1)S(1)} fusion(bf16[8,2,2]{0,1,2:T(2,128)(2,1)S(1)} %get-tuple-element.103, bf16[8,2,64]{0,1,2:T(2,128)(2,1)S(1)} %get-tuple-element.108, bf16[8,2,2]{0,1,2:T(2,128)(2,1)S(1)} %get-tuple-element.104, bf16[8,64,68]{0,1,2:T(8,128)(2,1)S(1)} %copy-done.8, bf16[8,2,2]{0,1,2:T(2,128)(2,1)S(1)} %get-tuple-element.94, ...), kind=kLoop, calls=%fused_computation.39 | loop fusion | flops 46240000 | bytes 3699200 | tf_op jit(solution)/shard_map/concatenate | solution.py:142
  160.7 3.3 collective-permute-start.2
  164.1 13.2 %maximum_bitcast_fusion.1 = bf16[1,200,68,68]{1,2,3,0:T(8,128)(2,1)S(1)} fusion(bf16[8,2,2]{0,1,2:T(2,128)(2,1)S(1)} %get-tuple-element.105, bf16[8,2,64]{0,1,2:T(2,128)(2,1)S(1)} %get-tuple-element.109, bf16[8,2,2]{0,1,2:T(2,128)(2,1)S(1)} %get-tuple-element.106, bf16[8,64,68]{0,1,2:T(8,128)(2,1)S(1)} %copy-done.7, ...), kind=kLoop, calls=%fused_computation.38 | loop fusion | flops 46240000 | bytes 3699200 | tf_op jit(solution)/shard_map/stack | solution.py:149
  177.2 59.4 %collective-permute-done.3 = bf16[200,68,68]{0,1,2:T(8,128)(2,1)S(1)} collective-permute-done((bf16[200,68,68]{0,1,2:T(8,128)(2,1)S(1)}, bf16[200,68,68]{0,1,2:T(8,128)(2,1)S(1)}, u32[]{:S(2)}, u32[]{:S(2)}) %collective-permute-start.3) | collective-permute-done | bytes 1849632 | tf_op jit(solution)/shard_map/ppermute | solution.py:30
  236.7 21.0 %collective-permute-done.2 = bf16[200,68,68]{0,1,2:T(8,128)(2,1)S(1)} collective-permute-done((bf16[200,68,68]{0,1,2:T(8,128)(2,1)S(1)}, bf16[200,68,68]{0,1,2:T(8,128)(2,1)S(1)}, u32[]{:S(2)}, u32[]{:S(2)}) %collective-permute-start.2) | collective-permute-done | bytes 1849632 | tf_op jit(solution)/shard_map/ppermute | solution.py:30
  264.4 317.3 %broadcast_select_fusion = f32[66,16,9,192]{3,1,2,0:T(8,128)S(1)} fusion(pred[16,9]{0,1:T(8,128)(4,1)S(1)} %copy-done.20, bf16[192,200,3,3]{1,0,3,2:T(8,128)(2,1)S(1)} %copy-done, bf16[200,68,2,8,11]{0,1,4,3,2:T(8,128)(2,1)S(1)} %fusion.1), kind=kOutput, calls=%fused_computation.32 | convolution fusion | flops 6570989568 | bytes 12777616 | tf_op jit(solution)/shard_map/conv_general_dilated | solution.py:34
  581.7 4.1 fusion.17
  588.8 4.3 maximum_bitcast_fusion
  593.2 8.0 %copy.195 = bf16[200,66,2,66]{0,2,3,1:T(2,128)(2,1)} copy(bf16[200,66,2,66]{0,1,3,2:T(8,128)(2,1)} %maximum_bitcast_fusion) | data formatting | bytes 6969600
  601.1 8.6 %pad.2.clone = bf16[200,66,2,72]{0,2,3,1:T(2,128)(2,1)} pad(bf16[200,66,2,66]{0,2,3,1:T(2,128)(2,1)} %copy.195, bf16[]{:T(256)} %constant.94.clone.1), padding=0_0x0_0x0_0x0_6 | pad | bytes 7286402 | tf_op jit(solution)/shard_map/concatenate | solution.py:54
  611.6 7.5 fusion.5
  619.2 12.4 %select_tanh_fusion = f32[64,16,9,96]{3,1,2,0:T(8,128)S(1)} fusion(pred[16,9]{0,1:T(8,128)(4,1)S(1)} %copy-done.19, bf16[96,200,3,3]{1,0,3,2:T(8,128)(2,1)S(1)} %copy-done.18, bf16[200,66,2,8,11]{0,2,4,3,1:T(2,128)(2,1)S(1)} %fusion.5), kind=kOutput, calls=%fused_computation.33 | convolution fusion | flops 3185934336 | bytes 8531088 | tf_op jit(solution)/shard_map/conv_general_dilated | solution.py:34
  638.6 36.7 %collective-permute-start.4 = (bf16[96,64,64]{0,1,2:T(8,128)(2,1)S(1)}, bf16[96,64,64]{0,1,2:T(8,128)(2,1)S(1)}, u32[]{:S(2)}, u32[]{:S(2)}) collective-permute-start(bf16[96,64,64]{0,1,2:T(8,128)(2,1)S(1)} %slice_bitcast_fusion.3), channel_id=1, source_target_pairs={{0,120},{8,0},{16,8},{24,16},{32,24},{40,32},{48,40},{56,48},{64,5... | collective-permute-start | bytes 2359304 | tf_op jit(solution)/shard_map/ppermute | solution.py:30
  676.5 34.2 %collective-permute-done.4 = bf16[96,64,64]{0,1,2:T(8,128)(2,1)S(1)} collective-permute-done((bf16[96,64,64]{0,1,2:T(8,128)(2,1)S(1)}, bf16[96,64,64]{0,1,2:T(8,128)(2,1)S(1)}, u32[]{:S(2)}, u32[]{:S(2)}) %collective-permute-start.4) | collective-permute-done | bytes 786464 | tf_op jit(solution)/shard_map/ppermute | solution.py:30
  713.8 41.8 %collective-permute-done.5 = bf16[96,64,64]{0,1,2:T(8,128)(2,1)S(1)} collective-permute-done((bf16[96,64,64]{0,1,2:T(8,128)(2,1)S(1)}, bf16[96,64,64]{0,1,2:T(8,128)(2,1)S(1)}, u32[]{:S(2)}, u32[]{:S(2)}) %collective-permute-start.5) | collective-permute-done | bytes 786464 | tf_op jit(solution)/shard_map/ppermute | solution.py:30
  757.6 7.0 copy.183
  (123 shorter events, 72.6 us)
Async XLA Ops:
  6.5 257.8 %copy-start = (bf16[192,200,3,3]{1,0,3,2:T(8,128)(2,1)S(1)}, bf16[192,200,3,3]{1,0,3,2:T(8,128)(2,1)}, u32[]{:S(2)}) copy-start(bf16[192,200,3,3]{1,0,3,2:T(8,128)(2,1)} %param.10) | copy-start | bytes 2073604
  6.5 56.2 %all-gather.2.cloned.1.call-start = ((), (), s32[]{:S(2)}) async-start(), calls=%async_computation | async-start | bytes 3538944 | tf_op jit(solution)/shard_map/all_gather | solution.py:109
  67.9 57.5 %collective-permute-start = (bf16[200,2,256]{0,1,2:T(2,128)(2,1)}, bf16[200,2,256]{0,1,2:T(2,128)(2,1)}, u32[]{:S(2)}, u32[]{:S(2)}) collective-permute-start(bf16[200,2,256]{0,1,2:T(2,128)(2,1)} %get-tuple-element.39), channel_id=1, source_target_pairs={{0,8},{8,16},{16,24},{24,32},{32,40},{40,48},{48,56},{56,64},{64,7... | collective-permute-start | bytes 614408 | tf_op jit(solution)/shard_map/ppermute | solution.py:22
  71.6 55.4 %collective-permute-start.1 = (bf16[200,2,256]{0,1,2:T(2,128)(2,1)}, bf16[200,2,256]{0,1,2:T(2,128)(2,1)}, u32[]{:S(2)}, u32[]{:S(2)}) collective-permute-start(bf16[200,2,256]{0,1,2:T(2,128)(2,1)} %get-tuple-element.40), channel_id=1, source_target_pairs={{8,0},{16,8},{24,16},{32,24},{40,32},{48,40},{56,48},{64,56},{72,6... | collective-permute-start | bytes 614408 | tf_op jit(solution)/shard_map/ppermute | solution.py:23
  120.4 10.7 %copy-start.9 = (bf16[8,64,68]{0,1,2:T(8,128)(2,1)S(1)}, bf16[8,64,68]{0,1,2:T(8,128)(2,1)}, u32[]{:S(2)}) copy-start(bf16[8,64,68]{0,1,2:T(8,128)(2,1)} %copy.176) | copy-start | bytes 208900
  125.4 22.3 %copy-start.8 = (bf16[8,64,68]{0,1,2:T(8,128)(2,1)S(1)}, bf16[8,64,68]{0,1,2:T(8,128)(2,1)}, u32[]{:S(2)}) copy-start(bf16[8,64,68]{0,1,2:T(8,128)(2,1)} %copy.169) | copy-start | bytes 208900
  125.4 22.3 %copy-start.11 = (bf16[96,64,64]{0,1,2:T(8,128)(2,1)S(1)}, bf16[96,64,64]{0,1,2:T(8,128)(2,1)}, u32[]{:S(2)}) copy-start(bf16[96,64,64]{0,1,2:T(8,128)(2,1)} %copy.190) | copy-start | bytes 2359300
  125.4 22.3 %copy-start.15 = (bf16[96,64,2]{0,1,2:T(8,128)(2,1)S(1)}, bf16[96,64,2]{0,1,2:T(8,128)(2,1)}, u32[]{:S(2)}) copy-start(bf16[96,64,2]{0,1,2:T(8,128)(2,1)} %get-tuple-element.19) | copy-start | bytes 73732
  125.4 22.3 %copy-start.16 = (bf16[96,64,2]{0,1,2:T(8,128)(2,1)S(1)}, bf16[96,64,2]{0,1,2:T(8,128)(2,1)}, u32[]{:S(2)}) copy-start(bf16[96,64,2]{0,1,2:T(8,128)(2,1)} %get-tuple-element.20) | copy-start | bytes 73732
  125.4 22.3 %copy-start.17 = (bf16[96,64,2]{0,1,2:T(8,128)(2,1)S(1)}, bf16[96,64,2]{0,1,2:T(8,128)(2,1)}, u32[]{:S(2)}) copy-start(bf16[96,64,2]{0,1,2:T(8,128)(2,1)} %broadcast_select_fusion.3) | copy-start | bytes 73732
  131.1 32.9 %copy-start.12 = (bf16[96,64,2]{0,1,2:T(8,128)(2,1)S(1)}, bf16[96,64,2]{0,1,2:T(8,128)(2,1)}, u32[]{:S(2)}) copy-start(bf16[96,64,2]{0,1,2:T(8,128)(2,1)} %copy.188) | copy-start | bytes 73732
  131.1 32.9 %copy-start.5 = (bf16[1,96,64,64]{1,2,3,0:T(8,128)(2,1)S(1)}, bf16[1,96,64,64]{1,2,3,0:T(8,128)(2,1)}, u32[]{:S(2)}) copy-start(bf16[1,96,64,64]{1,2,3,0:T(8,128)(2,1)} %copy.157) | copy-start | bytes 2359300
  131.2 32.9 %copy-start.7 = (bf16[8,64,68]{0,1,2:T(8,128)(2,1)S(1)}, bf16[8,64,68]{0,1,2:T(8,128)(2,1)}, u32[]{:S(2)}) copy-start(bf16[8,64,68]{0,1,2:T(8,128)(2,1)} %copy.162) | copy-start | bytes 208900
  131.2 32.9 %copy-start.10 = (bf16[96,64,64]{0,1,2:T(8,128)(2,1)S(1)}, bf16[96,64,64]{0,1,2:T(8,128)(2,1)}, u32[]{:S(2)}) copy-start(bf16[96,64,64]{0,1,2:T(8,128)(2,1)} %copy.187) | copy-start | bytes 2359300
  131.2 32.9 %copy-start.13 = (bf16[96,64,2]{0,1,2:T(8,128)(2,1)S(1)}, bf16[96,64,2]{0,1,2:T(8,128)(2,1)}, u32[]{:S(2)}) copy-start(bf16[96,64,2]{0,1,2:T(8,128)(2,1)} %get-tuple-element.21) | copy-start | bytes 73732
  131.2 32.9 %copy-start.14 = (bf16[96,64,2]{0,1,2:T(8,128)(2,1)S(1)}, bf16[96,64,2]{0,1,2:T(8,128)(2,1)}, u32[]{:S(2)}) copy-start(bf16[96,64,2]{0,1,2:T(8,128)(2,1)} %get-tuple-element.22) | copy-start | bytes 73732
  145.8 90.9 %collective-permute-start.3 = (bf16[200,68,68]{0,1,2:T(8,128)(2,1)S(1)}, bf16[200,68,68]{0,1,2:T(8,128)(2,1)S(1)}, u32[]{:S(2)}, u32[]{:S(2)}) collective-permute-start(bf16[200,68,68]{0,1,2:T(8,128)(2,1)S(1)} %maximum_maximum_fusion.1), channel_id=1, source_target_pairs={{0,8},{8,16},{16,24},{24,32},{32,40},{40,48},{48,56},{56,64},{64,7... | collective-permute-start | bytes 5548808 | tf_op jit(solution)/shard_map/ppermute | solution.py:30
  160.7 96.9 %collective-permute-start.2 = (bf16[200,68,68]{0,1,2:T(8,128)(2,1)S(1)}, bf16[200,68,68]{0,1,2:T(8,128)(2,1)S(1)}, u32[]{:S(2)}, u32[]{:S(2)}) collective-permute-start(bf16[200,68,68]{0,1,2:T(8,128)(2,1)S(1)} %maximum_maximum_fusion), channel_id=1, source_target_pairs={{0,16},{8,24},{16,32},{24,40},{32,48},{40,56},{48,64},{56,72},{64,... | collective-permute-start | bytes 5548808 | tf_op jit(solution)/shard_map/ppermute | solution.py:30
  259.3 328.2 %copy-start.2 = (bf16[1,200,68,68]{1,2,3,0:T(8,128)(2,1)}, bf16[1,200,68,68]{1,2,3,0:T(8,128)(2,1)S(1)}, u32[]{:S(2)}) copy-start(bf16[1,200,68,68]{1,2,3,0:T(8,128)(2,1)S(1)} %select_bitcast_fusion) | copy-start | bytes 5548804
  262.9 1.4 copy-start.20
  611.6 7.6 copy-start.18
  611.6 7.6 copy-start.19
  611.6 21.7 %slice-start = ((s8[4866048]{0:T(1024)(128)(4,1)}), s8[4194304]{0:T(1024)(128)(4,1)S(1)}, s32[]{:S(2)}) async-start(s8[4866048]{0:T(1024)(128)(4,1)} %bitcast.99), calls=%async_computation.1 | async-start | bytes 8388608
  619.1 14.1 %slice-start.1 = ((s8[4866048]{0:T(1024)(128)(4,1)}), s8[671744]{0:T(1024)(128)(4,1)S(1)}, s32[]{:S(2)}) async-start(s8[4866048]{0:T(1024)(128)(4,1)} %bitcast.99), calls=%async_computation.2 | async-start | bytes 1343488
  634.9 1.7 copy-start.3
  636.6 38.9 %copy-start.4 = (bf16[1,96,64,256]{1,2,3,0:T(8,128)(2,1)S(1)}, bf16[1,96,64,256]{1,2,3,0:T(8,128)(2,1)}, u32[]{:S(2)}) copy-start(bf16[1,96,64,256]{1,2,3,0:T(8,128)(2,1)} %copy.151) | copy-start | bytes 9437188
  636.6 38.9 %copy-start.6 = (bf16[1,96,64,64]{1,2,3,0:T(8,128)(2,1)S(1)}, bf16[1,96,64,64]{1,2,3,0:T(8,128)(2,1)}, u32[]{:S(2)}) copy-start(bf16[1,96,64,64]{1,2,3,0:T(8,128)(2,1)} %copy.157) | copy-start | bytes 2359300
  638.6 72.1 %collective-permute-start.4 = (bf16[96,64,64]{0,1,2:T(8,128)(2,1)S(1)}, bf16[96,64,64]{0,1,2:T(8,128)(2,1)S(1)}, u32[]{:S(2)}, u32[]{:S(2)}) collective-permute-start(bf16[96,64,64]{0,1,2:T(8,128)(2,1)S(1)} %slice_bitcast_fusion.3), channel_id=1, source_target_pairs={{0,120},{8,0},{16,8},{24,16},{32,24},{40,32},{48,40},{56,48},{64,5... | collective-permute-start | bytes 2359304 | tf_op jit(solution)/shard_map/ppermute | solution.py:30
  675.4 80.2 %collective-permute-start.5 = (bf16[96,64,64]{0,1,2:T(8,128)(2,1)S(1)}, bf16[96,64,64]{0,1,2:T(8,128)(2,1)S(1)}, u32[]{:S(2)}, u32[]{:S(2)}) collective-permute-start(bf16[96,64,64]{0,1,2:T(8,128)(2,1)S(1)} %slice_bitcast_fusion.3), channel_id=1, source_target_pairs={{0,112},{8,120},{16,0},{24,8},{32,16},{40,24},{48,32},{56,40},{64,... | collective-permute-start | bytes 2359304 | tf_op jit(solution)/shard_map/ppermute | solution.py:30
  755.6 9.1 %copy-start.1 = (bf16[192,200,3,3]{1,0,3,2:T(8,128)(2,1)S(1)}, bf16[192,200,3,3]{1,0,3,2:T(8,128)(2,1)}, u32[]{:S(2)}) copy-start(bf16[192,200,3,3]{1,0,3,2:T(8,128)(2,1)} %param.10) | copy-start | bytes 2073604
Sparse Core Ops, SparseCore 0:
  9.0 29.3 all-gather.1
where the time goes:
time: 776 us; the launch traced here: 772 us
  matrix products  330 us (43%)
  waiting for transfers between devices  157 us (20%)
  local copies, waits for them, and re-layouts  131 us (17%)
  other arithmetic  85.7 us (11%)
  starting transfers between devices  47.9 us (6%)
  between operations  20.2 us (3%)
    conv_general_dilated x2, matrix products, convolve(): lax.conv_general_dilated(inputs, kernel, (1, 1), 'VALID', dimension_numbe...  330 us
    ppermute x4, waiting for transfers between devices, shifted(): lax.ppermute(x, axis, [(i, (i + by) % length) for i in range(length)])  156 us
    unnamed x61, local copies, waits for them, and re-layouts  52.2 us
    ppermute x4, starting transfers between devices, shifted(): lax.ppermute(x, axis, [(i, (i + by) % length) for i in range(length)])  42 us
    concatenate x2, other arithmetic, shards(): windows.append(jnp.concatenate(pieces, axis=0))  27.6 us
    dynamic_slice x12, local copies, waits for them, and re-layouts, column_window(): lax.dynamic_slice(values, (zero, zero, start), (channels, rows_here, TILE))  25.9 us
    another operation x4, other arithmetic, shards(): batch_tiles = jnp.stack([windows[0], second])  17.5 us
  transfers between devices with their start and end apart: 7, of which 4 were waited for; matrix products, arithmetic and copies ran while one was open for 17% of the time, Pallas kernels for 0%

commit v1 on v0

v1 whole, which is shorter than its diff:
```python
import functools

import jax
import jax.numpy as jnp
from jax import lax
from jax.experimental import pallas as pl
from jax.experimental.pallas import tpu as pltpu
from jax.sharding import PartitionSpec as P

STATE_CH = 96
CONTEXT_CH = 96
NOISE_CH = 8
TILE = 64
REACH = 3
HALO = 2
ROWS = 64
COLS = 256
CHUNK = 16
STEPS = ROWS // CHUNK
SIDE_CH = CONTEXT_CH + 16
PIECE = CONTEXT_CH // 8
S3 = 3 * STATE_CH
C3 = 3 * SIDE_CH
BF16 = jnp.bfloat16
F32 = jnp.float32


def put_taps(ref, first, row):
    count = row.shape[0]
    edge = jnp.zeros((count, 1), row.dtype)
    ref[pl.ds(first, count), :] = jnp.concatenate([edge, row[:, : COLS - 1]], axis=1)
    ref[pl.ds(first + count, count), :] = row
    ref[pl.ds(first + 2 * count, count), :] = jnp.concatenate([row[:, 1:], edge], axis=1)


def logistic(x):
    return 0.5 * jnp.tanh(0.5 * x) + 0.5


def state_kernel(state, rim, weights, sums, first_sums, by_row, taps):
    step = pl.program_id(0)

    def sums_at(place):
        start = pl.multiple_of(place * S3, 16)
        return jnp.dot(weights[...], taps[pl.ds(start, 3 * S3), :], preferred_element_type=F32)

    @pl.when(step == 0)
    def _():
        chunk = jnp.transpose(state[:, :CHUNK, :], (1, 0, 2))
        for n in range(HALO):
            put_taps(taps, n * S3, rim[n])
            put_taps(taps, (HALO + ROWS + n) * S3, rim[HALO + n])
        for n in range(CHUNK):
            put_taps(taps, (HALO + n) * S3, chunk[n])
        for n in range(HALO):
            first_sums[n] = sums_at(n)

    here = pl.multiple_of(step * CHUNK, CHUNK)
    by_row[...] = jnp.transpose(state[:, pl.ds(here, CHUNK), :], (1, 0, 2))
    later = jnp.minimum(step + 1, STEPS - 1) * CHUNK
    chunk = jnp.transpose(state[:, pl.ds(pl.multiple_of(later, CHUNK), CHUNK), :], (1, 0, 2))
    for n in range(CHUNK):
        put_taps(taps, pl.multiple_of((HALO + later + n) * S3, 16), chunk[n])
        if n >= HALO:
            sums[n - HALO] = sums_at(here + n)
    for n in range(CHUNK - HALO, CHUNK):
        sums[n] = sums_at(here + n + HALO)


def side_kernel(
    pieces, noise, side_rim, by_row, rim, sums, first_sums, side_weights, reset_weights, active, offset,
    out, raw, taps, reset_taps, update, partial, rows_done, sems,
):
    step = pl.program_id(0)
    here = pl.multiple_of(step * CHUNK, CHUNK)

    def sums_at(place):
        start = pl.multiple_of(place * C3, 16)
        return jnp.dot(side_weights[...], taps[pl.ds(start, 3 * C3), :], preferred_element_type=F32)

    def gates(row_sums, state_sums, carried, slot):
        update[slot] = logistic(row_sums[:STATE_CH] + state_sums[:STATE_CH])
        reset = logistic(row_sums[STATE_CH : 2 * STATE_CH] + state_sums[STATE_CH:])
        partial[slot] = row_sums[2 * STATE_CH :]
        put_taps(reset_taps, slot * S3, (reset * carried.astype(F32)).astype(BF16))

    @pl.when(step == 0)
    def _():
        member = lax.axis_index("member")
        x, core = member // 2, member % 2
        copies = []
        for n, piece in enumerate(pieces):
            shift, rows, other = ((0, 0, ROWS), (3, 0, ROWS), (1, 0, ROWS), (2, 0, ROWS // 2), (2, ROWS // 2, ROWS // 2))[n % 5], None, n // 5
            place = 2 * lax.rem(x + shift[0], 4) + (core if other == 0 else 1 - core)
            target = raw.at[pl.ds(place * PIECE, PIECE), pl.ds(shift[1], shift[2]), :]
            copies.append(pltpu.make_async_copy(piece, target, sems.at[n]))
        for copy in copies:
            copy.start()
        raw[CONTEXT_CH : CONTEXT_CH + NOISE_CH] = noise[...]
        raw[CONTEXT_CH + NOISE_CH :] = jnp.zeros((SIDE_CH - CONTEXT_CH - NOISE_CH, ROWS, COLS), BF16)
        for n in range(HALO):
            put_taps(taps, n * C3, side_rim[n])
            put_taps(taps, (HALO + ROWS + n) * C3, side_rim[HALO + n])
        for copy in copies:
            copy.wait()
        chunk = jnp.transpose(raw[:, :CHUNK, :], (1, 0, 2))
        for n in range(CHUNK):
            put_taps(taps, (HALO + n) * C3, chunk[n])
        gates(sums_at(0), first_sums[0], rim[HALO - 1], 0)
        gates(sums_at(1), first_sums[1], by_row[0], 1)

    @pl.when(step > 0)
    def _():
        reset_taps[: 2 * S3] = reset_taps[CHUNK * S3 :]
        update[1] = update[CHUNK + 1]
        partial[1] = partial[CHUNK + 1]

    later = jnp.minimum(step + 1, STEPS - 1) * CHUNK
    chunk = jnp.transpose(raw[:, pl.ds(pl.multiple_of(later, CHUNK), CHUNK), :], (1, 0, 2))

    def gate_row(n):
        row = here + n + 1
        carried = by_row[jnp.minimum(row, ROWS - 1)]
        if n == CHUNK - 1:
            carried = jnp.where(step == STEPS - 1, rim[HALO], carried)
        gates(sums_at(here + n + 2), sums[n], carried, n + 2)

    for n in range(CHUNK):
        put_taps(taps, pl.multiple_of((HALO + later + n) * C3, 16), chunk[n])
        if n >= HALO:
            gate_row(n - HALO)
    for n in range(CHUNK - HALO, CHUNK):
        gate_row(n)

    owner = lax.axis_index("space")
    tile = lax.broadcasted_iota(jnp.int32, (1, COLS), 1) // TILE
    chosen = jnp.zeros((1, COLS), jnp.bool_)
    for n in range(COLS // TILE):
        used = (active[owner, n] == 1) & (offset[owner, n] < REACH)
        chosen = chosen | ((tile == n) & used)
    for n in range(CHUNK):
        terms = jnp.dot(reset_weights[...], reset_taps[n * S3 : (n + 3) * S3, :], preferred_element_type=F32)
        proposal = jnp.tanh(terms + partial[n + 1])
        old = by_row[here + n].astype(F32)
        new = (1.0 - update[n + 1]) * old + update[n + 1] * proposal
        rows_done[n] = jnp.where(chosen, new, old).astype(BF16)
    out[...] = jnp.transpose(rows_done[...], (1, 0, 2))


def whole(*shape):
    return pl.BlockSpec(shape, lambda i: (0,) * len(shape))


def state_part(state, rim, weights):
    return pl.pallas_call(
        state_kernel,
        grid=(STEPS,),
        in_specs=[whole(STATE_CH, ROWS, COLS), whole(2 * HALO, STATE_CH, COLS), whole(2 * STATE_CH, 3 * S3)],
        out_specs=[
            pl.BlockSpec((CHUNK, 2 * STATE_CH, COLS), lambda i: (i, 0, 0)),
            whole(HALO, 2 * STATE_CH, COLS),
            pl.BlockSpec((CHUNK, STATE_CH, COLS), lambda i: (i, 0, 0)),
        ],
        out_shape=[
            jax.ShapeDtypeStruct((ROWS, 2 * STATE_CH, COLS), F32),
            jax.ShapeDtypeStruct((HALO, 2 * STATE_CH, COLS), F32),
            jax.ShapeDtypeStruct((ROWS, STATE_CH, COLS), BF16),
        ],
        scratch_shapes=[pltpu.VMEM(((ROWS + 2 * HALO) * S3, COLS), BF16)],
        compiler_params=pltpu.CompilerParams(vmem_limit_bytes=50 * 2**20),
        cost_estimate=pl.CostEstimate(flops=11_000_000_000, bytes_accessed=20_000_000, transcendentals=0),
        name="state_part",
    )(state, rim, weights)


def side_part(pieces, noise, side_rim, by_row, rim, sums, first_sums, side_weights, reset_weights, active, offset):
    count = len(pieces)

    def kernel(*refs):
        side_kernel(refs[:count], *refs[count:])

    smem = pl.BlockSpec(memory_space=pltpu.SMEM)
    return pl.pallas_call(
        kernel,
        grid=(STEPS,),
        in_specs=[pl.BlockSpec(memory_space=pl.ANY)] * count
        + [
            whole(NOISE_CH, ROWS, COLS),
            whole(2 * HALO, SIDE_CH, COLS),
            whole(ROWS, STATE_CH, COLS),
            whole(2 * HALO, STATE_CH, COLS),
            pl.BlockSpec((CHUNK, 2 * STATE_CH, COLS), lambda i: (i, 0, 0)),
            whole(HALO, 2 * STATE_CH, COLS),
            whole(3 * STATE_CH, 3 * C3),
            whole(STATE_CH, 3 * S3),
            smem,
            smem,
        ],
        out_specs=pl.BlockSpec((STATE_CH, CHUNK, COLS), lambda i: (0, i, 0)),
        out_shape=jax.ShapeDtypeStruct((STATE_CH, ROWS, COLS), BF16),
        scratch_shapes=[
            pltpu.VMEM((SIDE_CH, ROWS, COLS), BF16),
            pltpu.VMEM(((ROWS + 2 * HALO) * C3, COLS), BF16),
            pltpu.VMEM(((CHUNK + 2) * S3, COLS), BF16),
            pltpu.VMEM((CHUNK + 2, STATE_CH, COLS), F32),
            pltpu.VMEM((CHUNK + 2, STATE_CH, COLS), F32),
            pltpu.VMEM((CHUNK, STATE_CH, COLS), BF16),
            pltpu.SemaphoreType.DMA((count,)),
        ],
        compiler_params=pltpu.CompilerParams(vmem_limit_bytes=56 * 2**20),
        cost_estimate=pl.CostEstimate(flops=17_000_000_000, bytes_accessed=20_000_000, transcendentals=0),
        name="side_part",
    )(*pieces, noise, side_rim, by_row, rim, sums, first_sums, side_weights, reset_weights, active, offset)


def tap_weights(kernel, first, count, padded):
    taps = jnp.transpose(kernel[:, first : first + count], (2, 3, 0, 1))
    taps = jnp.pad(taps, ((0, 0), (0, 0), (0, 0), (0, padded - count)))
    return jnp.concatenate([taps[a, b] for a in range(3) for b in range(3)], axis=1)


def along_x(by):
    return [(2 * x + core, 2 * ((x + by) % 4) + core) for x in range(4) for core in range(2)]


CORES = [(n, n ^ 1) for n in range(8)]


def gathered_pieces(context):
    half = ROWS // 2
    right = lax.ppermute(context, "member", along_x(1))
    left = lax.ppermute(context, "member", along_x(-1))
    right_far = lax.ppermute(right[:, :half], "member", along_x(1))
    left_far = lax.ppermute(left[:, half:], "member", along_x(-1))
    mine = [context, right, left, right_far, left_far]
    return mine + [lax.ppermute(piece, "member", CORES) for piece in mine]


def gathered_rim(rim):
    member = lax.axis_index("member")
    far = [lax.ppermute(rim, "member", along_x(by)) for by in (3, 2, 1)]
    mine = jnp.stack([rim] + far)
    other = lax.ppermute(mine, "member", CORES)
    x, core = member // 2, member % 2
    pair = jnp.where(core == 0, jnp.stack([mine, other], axis=1), jnp.stack([other, mine], axis=1))
    pair = jnp.concatenate([pair, pair], axis=0)
    pair = lax.dynamic_slice_in_dim(pair, lax.rem(4 - x, 4), 4, axis=0)
    return jnp.transpose(pair, (2, 0, 1, 3, 4)).reshape(2 * HALO, CONTEXT_CH, COLS)


def shards(state_field, context_field, noise_latent, gate_kernel, candidate_kernel, active_tiles, tile_offset):
    owners = lax.axis_size("space")
    state = state_field[0]
    noise = noise_latent[0, 0]
    pieces = gathered_pieces(context_field)

    def edge(first):
        rows = [a[:, first : first + HALO] for a in (state, context_field, noise)]
        return jnp.transpose(jnp.concatenate(rows, axis=0), (1, 0, 2))

    down = [(n, n + 1) for n in range(owners - 1)]
    up = [(n + 1, n) for n in range(owners - 1)]
    above = lax.ppermute(edge(ROWS - HALO), "space", down)
    below = lax.ppermute(edge(0), "space", up)
    rims = jnp.concatenate([above, below], axis=0)
    rim = rims[:, :STATE_CH]
    state_weights = tap_weights(gate_kernel, 0, STATE_CH, STATE_CH)
    sums, first_sums, by_row = state_part(state, rim, state_weights)
    side_kernels = jnp.concatenate([gate_kernel[:, STATE_CH:], candidate_kernel[:, STATE_CH:]], axis=0)
    side_weights = tap_weights(side_kernels, 0, CONTEXT_CH + NOISE_CH, SIDE_CH)
    reset_weights = tap_weights(candidate_kernel, 0, STATE_CH, STATE_CH)
    side_rim = jnp.concatenate(
        [
            gathered_rim(rims[:, STATE_CH : STATE_CH + PIECE]),
            rims[:, STATE_CH + PIECE :],
            jnp.zeros((2 * HALO, SIDE_CH - CONTEXT_CH - NOISE_CH, COLS), BF16),
        ],
        axis=1,
    )
    result = side_part(
        pieces, noise, side_rim, by_row, rim, sums, first_sums, side_weights, reset_weights, active_tiles, tile_offset
    )
    return result[None]


def solution(mesh):
    return jax.shard_map(
        shards,
        mesh=mesh,
        in_specs=(
            P("member", None, "space", None),
            P("member", "space", None),
            P("member", None, None, "space", None),
            P(),
            P(),
            P(),
            P(),
        ),
        out_specs=P("member", None, "space", None),
        check_vma=False,
    )
```

time: 776 us -> 84.8 us (0.11)
  the two profiles are of different devices: /device:TPU:64 before, /device:TPU:1 now
where the time goes in v1:
time: 84.8 us; the launch traced here: 84.5 us
  Pallas kernels  41.7 us (49%)
  starting transfers between devices  18.7 us (22%)
  local copies, waits for them, and re-layouts  11.9 us (14%)
  waiting for transfers between devices  10.5 us (12%)
  other arithmetic  1.16 us (1%)
    pallas_call x1, Pallas kernels, side_part(): pl.pallas_call(kernel, grid=(STEPS,), in_specs=[pl.BlockSpec(memory_space...  26.9 us
    pallas_call x1, Pallas kernels, state_part(): pl.pallas_call(state_kernel, grid=(STEPS,), in_specs=[whole(STATE_CH, ROW...  14.8 us
    unnamed x41, local copies, waits for them, and re-layouts  7.86 us
    ppermute x1, waiting for transfers between devices, shards(): below = lax.ppermute(edge(0), 'space', up)  4.2 us
    ppermute x5, starting transfers between devices, gathered_pieces(): return mine + [lax.ppermute(piece, 'member', CORES) for piece in mine]  3.92 us
    ppermute x1, starting transfers between devices, shards(): above = lax.ppermute(edge(ROWS - HALO), 'space', down)  3.55 us
    ppermute x1, waiting for transfers between devices, gathered_pieces(): left_far = lax.ppermute(left[:, half:], 'member', along_x(-1))  3.51 us
    ppermute x1, starting transfers between devices, gathered_pieces(): left = lax.ppermute(context, 'member', along_x(-1))  2.56 us
  transfers between devices with their start and end apart: 15, of which 5 were waited for; matrix products, arithmetic and copies ran while one was open for 14% of the time, Pallas kernels for 17%

profile of v1, /device:TPU:1, one launch (start us, length us, event | category | flops | bytes accessed | tf_op | source)
XLA Modules:
  0.0 84.5 jit_solution(11329649710264613910)
XLA Ops:
  0.0 1.4 %collective-permute-start.4 = (bf16[12,64,256]{2,1,0:T(8,128)(2,1)}, bf16[12,64,256]{2,1,0:T(8,128)(2,1)S(1)}, u32[]{:S(2)}, u32[]{:S(2)}) collective-permute-start(bf16[12,64,256]{2,1,0:T(8,128)(2,1)} %refs_0_.1), channel_id=1, source_target_pairs={{0,1},{1,0},{2,3},{3,2},{4,5},{5,4},{6,7},{7,6},{8,9},{9,8},{10,11... | collective-permute-start | bytes 1179656 | tf_op jit(solution)/shard_map/ppermute | solution.py:236
  1.4 2.6 %collective-permute-start.1 = (bf16[12,64,256]{2,1,0:T(8,128)(2,1)}, bf16[12,64,256]{2,1,0:T(8,128)(2,1)S(1)}, u32[]{:S(2)}, u32[]{:S(2)}) collective-permute-start(bf16[12,64,256]{2,1,0:T(8,128)(2,1)} %refs_0_.1), channel_id=1, source_target_pairs={{0,6},{1,7},{2,0},{3,1},{4,2},{5,3},{6,4},{7,5},{8,14},{9,15},{10,... | collective-permute-start | bytes 1179656 | tf_op jit(solution)/shard_map/ppermute | solution.py:232
  4.0 0.9 %fusion.4 = (bf16[12,2,256]{2,1,0:T(2,128)(2,1)S(1)}, bf16[12,2,256]{2,1,0:T(2,128)(2,1)S(1)}) fusion(bf16[12,64,256]{2,1,0:T(8,128)(2,1)} %refs_0_.1), kind=kLoop, calls=%fused_computation.46 | loop fusion | bytes 49152 | tf_op jit(solution)/shard_map/slice | solution.py:258
  4.9 1.1 %copy.33 = bf16[1,1,8,64,256]{4,2,3,1,0:T(8,128)(2,1)S(1)} copy(bf16[1,1,8,64,256]{4,3,2,1,0:T(8,128)(2,1)} %param.9) | data formatting | bytes 524288 | tf_op args[2]
  6.0 3.8 %copy.32 = bf16[1,96,64,256]{3,1,2,0:T(8,128)(2,1)S(1)} copy(bf16[1,96,64,256]{3,2,1,0:T(8,128)(2,1)} %param.7) | data formatting | bytes 6291456 | tf_op args[0]
  9.8 3.5 %collective-permute-start.9 = (bf16[2,116,256]{2,1,0:T(8,128)(2,1)S(1)}, bf16[2,116,256]{2,1,0:T(8,128)(2,1)S(1)}, u32[]{:S(2)}, u32[]{:S(2)}) collective-permute-start(bf16[2,116,256]{2,1,0:T(8,128)(2,1)S(1)} %maximum_bitcast_fusion.1), channel_id=1, source_target_pairs={{0,8},{8,16},{16,24},{24,32},{32,40},{40,48},{48,56},{56,64},{64,7... | collective-permute-start | bytes 356360 | tf_op jit(solution)/shard_map/ppermute | solution.py:263
  13.4 1.3 %collective-permute-start.10 = (bf16[2,116,256]{2,1,0:T(8,128)(2,1)S(1)}, bf16[2,116,256]{2,1,0:T(8,128)(2,1)S(1)}, u32[]{:S(2)}, u32[]{:S(2)}) collective-permute-start(bf16[2,116,256]{2,1,0:T(8,128)(2,1)S(1)} %maximum_bitcast_fusion.2), channel_id=1, source_target_pairs={{8,0},{16,8},{24,16},{32,24},{40,32},{48,40},{56,48},{64,56},{72,6... | collective-permute-start | bytes 356360 | tf_op jit(solution)/shard_map/ppermute | solution.py:264
  14.9 0.2 slice.147
  15.4 0.3 collective-permute-done.9
  15.8 4.2 %collective-permute-done.10 = bf16[2,116,256]{2,1,0:T(8,128)(2,1)S(1)} collective-permute-done((bf16[2,116,256]{2,1,0:T(8,128)(2,1)S(1)}, bf16[2,116,256]{2,1,0:T(8,128)(2,1)S(1)}, u32[]{:S(2)}, u32[]{:S(2)}) %collective-permute-start.10) | collective-permute-done | bytes 118816 | tf_op jit(solution)/shard_map/ppermute | solution.py:264
  20.0 0.6 collective-permute-start.12
  20.6 0.9 %collective-permute-start.11 = (bf16[4,12,256]{2,1,0:T(8,128)(2,1)S(1)}, bf16[4,12,256]{2,1,0:T(8,128)(2,1)S(1)}, u32[]{:S(2)}, u32[]{:S(2)}) collective-permute-start(bf16[4,12,256]{2,1,0:T(8,128)(2,1)S(1)} %get-tuple-element.36), channel_id=1, source_target_pairs={{0,6},{1,7},{2,0},{3,1},{4,2},{5,3},{6,4},{7,5},{8,14},{9,15},{10,... | collective-permute-start | bytes 73736 | tf_op jit(solution)/shard_map/ppermute | solution.py:241
  21.5 0.6 collective-permute-start.13
  22.3 0.7 copy.24.refs_18_
  22.9 0.7 copy.25.refs_19_
  23.7 0.8 concatenate.35.refs_17_
  24.5 1.2 %concatenate.34.refs_16_ = bf16[288,1008]{1,0:T(8,128)(2,1)} concatenate(bf16[288,112]{1,0:T(8,128)(2,1)S(1)} %get-tuple-element.21, bf16[288,112]{1,0:T(8,128)(2,1)S(1)} %get-tuple-element.14, bf16[288,112]{1,0:T(8,128)(2,1)S(1)} %get-tuple-element.15, bf16[288,112]{1,0:T(8,128)(2,1)S(1)} %get-tuple-element.16, bf16[288,112]{1,0:T(8,128)(2,1)S(1)} %get-tuple-element.17, ...), dimensions={1} | concatenate | bytes 1161216 | tf_op jit(solution)/shard_map/concatenate | solution.py:219
  25.7 0.2 concatenate.32.weights
  26.0 0.7 collective-permute-start
  26.8 2.4 %collective-permute-start.14 = (bf16[4,4,12,256]{3,2,1,0:T(8,128)(2,1)S(1)}, bf16[4,4,12,256]{3,2,1,0:T(8,128)(2,1)S(1)}, u32[]{:S(2)}, u32[]{:S(2)}) collective-permute-start(bf16[4,4,12,256]{3,2,1,0:T(8,128)(2,1)S(1)} %get-tuple-element.47), channel_id=1, source_target_pairs={{0,1},{1,0},{2,3},{3,2},{4,5},{5,4},{6,7},{7,6},{8,9},{9,8},{10,11... | collective-permute-start | bytes 294920 | tf_op jit(solution)/shard_map/ppermute | solution.py:243
  29.1 14.8 %state_part.1 = (f32[64,192,256]{2,1,0:T(8,128)}, f32[2,192,256]{2,1,0:T(8,128)S(1)}, bf16[64,96,256]{2,1,0:T(8,128)(2,1)S(1)}) custom-call(bf16[96,64,256]{2,1,0:T(8,128)(2,1)} %bitcast.85, bf16[4,96,256]{2,1,0:T(8,128)(2,1)S(1)} %slice.176.rim.refs_13_, bf16[192,864]{1,0:T(8,128)(2,1)S(1)} %concatenate.32.weights), custom_call_target="tpu_custom_call" | custom-call | flops 11000000512 | bytes 20000000 | tf_op jit(solution)/shard_map/state_part/pallas_call | solution.py:155
  43.9 0.7 copy-done.2
  44.7 2.1 %collective-permute-start.3 = (bf16[12,32,256]{2,1,0:T(8,128)(2,1)S(1)}, bf16[12,32,256]{2,1,0:T(8,128)(2,1)S(1)}, u32[]{:S(2)}, u32[]{:S(2)}) collective-permute-start(bf16[12,32,256]{2,1,0:T(8,128)(2,1)S(1)} %slice.169), channel_id=1, source_target_pairs={{0,6},{1,7},{2,0},{3,1},{4,2},{5,3},{6,4},{7,5},{8,14},{9,15},{10,... | collective-permute-start | bytes 589832 | tf_op jit(solution)/shard_map/ppermute | solution.py:234
  46.9 0.4 collective-permute-start.6
  47.9 3.5 %collective-permute-done.3.refs_4_ = bf16[12,32,256]{2,1,0:T(8,128)(2,1)S(1)} collective-permute-done((bf16[12,32,256]{2,1,0:T(8,128)(2,1)S(1)}, bf16[12,32,256]{2,1,0:T(8,128)(2,1)S(1)}, u32[]{:S(2)}, u32[]{:S(2)}) %collective-permute-start.3) | collective-permute-done | bytes 196640 | tf_op jit(solution)/shard_map/ppermute | solution.py:234
  51.4 0.8 collective-permute-start.8
  52.1 2.2 %collective-permute-done.2.refs_3_ = bf16[12,32,256]{2,1,0:T(8,128)(2,1)S(1)} collective-permute-done((bf16[12,32,256]{2,1,0:T(8,128)(2,1)S(1)}, bf16[12,32,256]{2,1,0:T(8,128)(2,1)S(1)}, u32[]{:S(2)}, u32[]{:S(2)}) %collective-permute-start.2) | collective-permute-done | bytes 196640 | tf_op jit(solution)/shard_map/ppermute | solution.py:233
  54.3 1.1 %collective-permute-start.7 = (bf16[12,32,256]{2,1,0:T(8,128)(2,1)S(1)}, bf16[12,32,256]{2,1,0:T(8,128)(2,1)S(1)}, u32[]{:S(2)}, u32[]{:S(2)}) collective-permute-start(bf16[12,32,256]{2,1,0:T(8,128)(2,1)S(1)} %collective-permute-done.2.refs_3_), channel_id=1, source_target_pairs={{0,1},{1,0},{2,3},{3,2},{4,5},{5,4},{6,7},{7,6},{8,9},{9,8},{10,11... | collective-permute-start | bytes 589832 | tf_op jit(solution)/shard_map/ppermute | solution.py:236
  55.5 0.8 maximum_maximum_fusion.refs_11_
  56.3 0.2 collective-permute-done.7.refs_8_
  56.6 0.4 copy-done.10
  57.4 26.9 %side_part.1 = bf16[96,64,256]{2,1,0:T(8,128)(2,1)} custom-call(bf16[12,64,256]{2,1,0:T(8,128)(2,1)} %refs_0_.1, bf16[12,64,256]{2,1,0:T(8,128)(2,1)} %copy-done.6, bf16[12,64,256]{2,1,0:T(8,128)(2,1)} %copy-done.5, bf16[12,32,256]{2,1,0:T(8,128)(2,1)} %copy-done.14, bf16[12,32,256]{2,1,0:T(8,128)(2,1)} %copy-done.13, bf16[12,64,256]{2,1,0:T(8,128)(2,1)} %copy-done.10, ...), custom_call_target="tpu_custom_call" | custom-call | flops 16999999488 | bytes 20000000 | tf_op jit(solution)/shard_map/side_part/pallas_call | solution.py:183
  (71 shorter events, 1.9 us)
Async XLA Ops:
  0.0 56.2 %collective-permute-start.4 = (bf16[12,64,256]{2,1,0:T(8,128)(2,1)}, bf16[12,64,256]{2,1,0:T(8,128)(2,1)S(1)}, u32[]{:S(2)}, u32[]{:S(2)}) collective-permute-start(bf16[12,64,256]{2,1,0:T(8,128)(2,1)} %refs_0_.1), channel_id=1, source_target_pairs={{0,1},{1,0},{2,3},{3,2},{4,5},{5,4},{6,7},{7,6},{8,9},{9,8},{10,11... | collective-permute-start | bytes 1179656 | tf_op jit(solution)/shard_map/ppermute | solution.py:236
  1.4 43.2 %collective-permute-start.1 = (bf16[12,64,256]{2,1,0:T(8,128)(2,1)}, bf16[12,64,256]{2,1,0:T(8,128)(2,1)S(1)}, u32[]{:S(2)}, u32[]{:S(2)}) collective-permute-start(bf16[12,64,256]{2,1,0:T(8,128)(2,1)} %refs_0_.1), channel_id=1, source_target_pairs={{0,6},{1,7},{2,0},{3,1},{4,2},{5,3},{6,4},{7,5},{8,14},{9,15},{10,... | collective-permute-start | bytes 1179656 | tf_op jit(solution)/shard_map/ppermute | solution.py:232
  6.0 8.7 %copy-start.4 = (bf16[96,200,3,3]{1,0,3,2:T(8,128)(2,1)S(1)}, bf16[96,200,3,3]{1,0,3,2:T(8,128)(2,1)}, u32[]{:S(2)}) copy-start(bf16[96,200,3,3]{1,0,3,2:T(8,128)(2,1)} %param.11) | copy-start | bytes 1036804
  6.0 8.9 %copy-start.3 = (bf16[192,200,3,3]{1,0,3,2:T(8,128)(2,1)S(1)}, bf16[192,200,3,3]{1,0,3,2:T(8,128)(2,1)}, u32[]{:S(2)}) copy-start(bf16[192,200,3,3]{1,0,3,2:T(8,128)(2,1)} %param.10) | copy-start | bytes 2073604
  9.8 6.0 %collective-permute-start.9 = (bf16[2,116,256]{2,1,0:T(8,128)(2,1)S(1)}, bf16[2,116,256]{2,1,0:T(8,128)(2,1)S(1)}, u32[]{:S(2)}, u32[]{:S(2)}) collective-permute-start(bf16[2,116,256]{2,1,0:T(8,128)(2,1)S(1)} %maximum_bitcast_fusion.1), channel_id=1, source_target_pairs={{0,8},{8,16},{16,24},{24,32},{32,40},{40,48},{48,56},{56,64},{64,7... | collective-permute-start | bytes 356360 | tf_op jit(solution)/shard_map/ppermute | solution.py:263
  13.4 6.6 %collective-permute-start.10 = (bf16[2,116,256]{2,1,0:T(8,128)(2,1)S(1)}, bf16[2,116,256]{2,1,0:T(8,128)(2,1)S(1)}, u32[]{:S(2)}, u32[]{:S(2)}) collective-permute-start(bf16[2,116,256]{2,1,0:T(8,128)(2,1)S(1)} %maximum_bitcast_fusion.2), channel_id=1, source_target_pairs={{8,0},{16,8},{24,16},{32,24},{40,32},{48,40},{56,48},{64,56},{72,6... | collective-permute-start | bytes 356360 | tf_op jit(solution)/shard_map/ppermute | solution.py:264
  14.9 7.4 %copy-start.7 = (s32[16,4]{0,1:T(4,128)S(1)}, s32[16,4]{0,1:T(4,128)}, u32[]{:S(2)}) copy-start(s32[16,4]{0,1:T(4,128)} %param.12) | copy-start | bytes 772
  14.9 8.0 %copy-start.8 = (s32[16,4]{0,1:T(4,128)S(1)}, s32[16,4]{0,1:T(4,128)}, u32[]{:S(2)}) copy-start(s32[16,4]{0,1:T(4,128)} %param.13) | copy-start | bytes 772
  15.3 10.7 %copy-start.9 = (bf16[12,64,256]{2,1,0:T(8,128)(2,1)S(1)}, bf16[12,64,256]{2,1,0:T(8,128)(2,1)}, u32[]{:S(2)}) copy-start(bf16[12,64,256]{2,1,0:T(8,128)(2,1)} %refs_0_.1) | copy-start | bytes 1179652
  20.0 6.0 %collective-permute-start.12 = (bf16[4,12,256]{2,1,0:T(8,128)(2,1)S(1)}, bf16[4,12,256]{2,1,0:T(8,128)(2,1)S(1)}, u32[]{:S(2)}, u32[]{:S(2)}) collective-permute-start(bf16[4,12,256]{2,1,0:T(8,128)(2,1)S(1)} %get-tuple-element.36), channel_id=1, source_target_pairs={{0,4},{1,5},{2,6},{3,7},{4,0},{5,1},{6,2},{7,3},{8,12},{9,13},{10,... | collective-permute-start | bytes 73736 | tf_op jit(solution)/shard_map/ppermute | solution.py:241
  20.6 6.1 %collective-permute-start.11 = (bf16[4,12,256]{2,1,0:T(8,128)(2,1)S(1)}, bf16[4,12,256]{2,1,0:T(8,128)(2,1)S(1)}, u32[]{:S(2)}, u32[]{:S(2)}) collective-permute-start(bf16[4,12,256]{2,1,0:T(8,128)(2,1)S(1)} %get-tuple-element.36), channel_id=1, source_target_pairs={{0,6},{1,7},{2,0},{3,1},{4,2},{5,3},{6,4},{7,5},{8,14},{9,15},{10,... | collective-permute-start | bytes 73736 | tf_op jit(solution)/shard_map/ppermute | solution.py:241
  21.5 5.3 %collective-permute-start.13 = (bf16[4,12,256]{2,1,0:T(8,128)(2,1)S(1)}, bf16[4,12,256]{2,1,0:T(8,128)(2,1)S(1)}, u32[]{:S(2)}, u32[]{:S(2)}) collective-permute-start(bf16[4,12,256]{2,1,0:T(8,128)(2,1)S(1)} %get-tuple-element.36), channel_id=1, source_target_pairs={{0,2},{1,3},{2,4},{3,5},{4,6},{5,7},{6,0},{7,1},{8,10},{9,11},{10,... | collective-permute-start | bytes 73736 | tf_op jit(solution)/shard_map/ppermute | solution.py:241
  26.0 17.9 %copy-start = (bf16[4,96,256]{2,1,0:T(8,128)(2,1)}, bf16[4,96,256]{2,1,0:T(8,128)(2,1)S(1)}, u32[]{:S(2)}) copy-start(bf16[4,96,256]{2,1,0:T(8,128)(2,1)S(1)} %slice.176.rim.refs_13_) | copy-start | bytes 589828
  26.0 20.8 %collective-permute-start = (bf16[12,64,256]{2,1,0:T(8,128)(2,1)S(1)}, bf16[12,64,256]{2,1,0:T(8,128)(2,1)S(1)}, u32[]{:S(2)}, u32[]{:S(2)}) collective-permute-start(bf16[12,64,256]{2,1,0:T(8,128)(2,1)S(1)} %copy-done.9), channel_id=1, source_target_pairs={{0,2},{1,3},{2,4},{3,5},{4,6},{5,7},{6,0},{7,1},{8,10},{9,11},{10,... | collective-permute-start | bytes 1179656 | tf_op jit(solution)/shard_map/ppermute | solution.py:231
  26.8 20.6 %collective-permute-start.14 = (bf16[4,4,12,256]{3,2,1,0:T(8,128)(2,1)S(1)}, bf16[4,4,12,256]{3,2,1,0:T(8,128)(2,1)S(1)}, u32[]{:S(2)}, u32[]{:S(2)}) collective-permute-start(bf16[4,4,12,256]{3,2,1,0:T(8,128)(2,1)S(1)} %get-tuple-element.47), channel_id=1, source_target_pairs={{0,1},{1,0},{2,3},{3,2},{4,5},{5,4},{6,7},{7,6},{8,9},{9,8},{10,11... | collective-permute-start | bytes 294920 | tf_op jit(solution)/shard_map/ppermute | solution.py:243
  43.9 0.7 copy-start.2
  44.6 11.9 %copy-start.1 = (bf16[64,96,256]{2,1,0:T(8,128)(2,1)}, bf16[64,96,256]{2,1,0:T(8,128)(2,1)S(1)}, u32[]{:S(2)}) copy-start(bf16[64,96,256]{2,1,0:T(8,128)(2,1)S(1)} %get-tuple-element.8.refs_12_) | copy-start | bytes 9437188
  44.7 11.9 %copy-start.5 = (bf16[12,64,256]{2,1,0:T(8,128)(2,1)}, bf16[12,64,256]{2,1,0:T(8,128)(2,1)S(1)}, u32[]{:S(2)}) copy-start(bf16[12,64,256]{2,1,0:T(8,128)(2,1)S(1)} %collective-permute-done.1.refs_2_) | copy-start | bytes 1179652
  44.7 6.7 %collective-permute-start.3 = (bf16[12,32,256]{2,1,0:T(8,128)(2,1)S(1)}, bf16[12,32,256]{2,1,0:T(8,128)(2,1)S(1)}, u32[]{:S(2)}, u32[]{:S(2)}) collective-permute-start(bf16[12,32,256]{2,1,0:T(8,128)(2,1)S(1)} %slice.169), channel_id=1, source_target_pairs={{0,6},{1,7},{2,0},{3,1},{4,2},{5,3},{6,4},{7,5},{8,14},{9,15},{10,... | collective-permute-start | bytes 589832 | tf_op jit(solution)/shard_map/ppermute | solution.py:234
  46.8 9.7 %copy-start.6 = (bf16[12,64,256]{2,1,0:T(8,128)(2,1)}, bf16[12,64,256]{2,1,0:T(8,128)(2,1)S(1)}, u32[]{:S(2)}) copy-start(bf16[12,64,256]{2,1,0:T(8,128)(2,1)S(1)} %collective-permute-done.refs_1_) | copy-start | bytes 1179652
  46.9 7.5 %collective-permute-start.2 = (bf16[12,32,256]{2,1,0:T(8,128)(2,1)S(1)}, bf16[12,32,256]{2,1,0:T(8,128)(2,1)S(1)}, u32[]{:S(2)}, u32[]{:S(2)}) collective-permute-start(bf16[12,32,256]{2,1,0:T(8,128)(2,1)S(1)} %slice.168), channel_id=1, source_target_pairs={{0,2},{1,3},{2,4},{3,5},{4,6},{5,7},{6,0},{7,1},{8,10},{9,11},{10,... | collective-permute-start | bytes 589832 | tf_op jit(solution)/shard_map/ppermute | solution.py:233
  46.9 9.3 %collective-permute-start.6 = (bf16[12,64,256]{2,1,0:T(8,128)(2,1)S(1)}, bf16[12,64,256]{2,1,0:T(8,128)(2,1)S(1)}, u32[]{:S(2)}, u32[]{:S(2)}) collective-permute-start(bf16[12,64,256]{2,1,0:T(8,128)(2,1)S(1)} %collective-permute-done.1.refs_2_), channel_id=1, source_target_pairs={{0,1},{1,0},{2,3},{3,2},{4,5},{5,4},{6,7},{7,6},{8,9},{9,8},{10,11... | collective-permute-start | bytes 1179656 | tf_op jit(solution)/shard_map/ppermute | solution.py:236
  47.3 9.2 %collective-permute-start.5 = (bf16[12,64,256]{2,1,0:T(8,128)(2,1)S(1)}, bf16[12,64,256]{2,1,0:T(8,128)(2,1)S(1)}, u32[]{:S(2)}, u32[]{:S(2)}) collective-permute-start(bf16[12,64,256]{2,1,0:T(8,128)(2,1)S(1)} %collective-permute-done.refs_1_), channel_id=1, source_target_pairs={{0,1},{1,0},{2,3},{3,2},{4,5},{5,4},{6,7},{7,6},{8,9},{9,8},{10,11... | collective-permute-start | bytes 1179656 | tf_op jit(solution)/shard_map/ppermute | solution.py:236
  51.4 5.2 %copy-start.13 = (bf16[12,32,256]{2,1,0:T(8,128)(2,1)}, bf16[12,32,256]{2,1,0:T(8,128)(2,1)S(1)}, u32[]{:S(2)}) copy-start(bf16[12,32,256]{2,1,0:T(8,128)(2,1)S(1)} %collective-permute-done.3.refs_4_) | copy-start | bytes 589828
  51.4 4.9 %collective-permute-start.8 = (bf16[12,32,256]{2,1,0:T(8,128)(2,1)S(1)}, bf16[12,32,256]{2,1,0:T(8,128)(2,1)S(1)}, u32[]{:S(2)}, u32[]{:S(2)}) collective-permute-start(bf16[12,32,256]{2,1,0:T(8,128)(2,1)S(1)} %collective-permute-done.3.refs_4_), channel_id=1, source_target_pairs={{0,1},{1,0},{2,3},{3,2},{4,5},{5,4},{6,7},{7,6},{8,9},{9,8},{10,11... | collective-permute-start | bytes 589832 | tf_op jit(solution)/shard_map/ppermute | solution.py:236
  54.3 2.3 %copy-start.14 = (bf16[12,32,256]{2,1,0:T(8,128)(2,1)}, bf16[12,32,256]{2,1,0:T(8,128)(2,1)S(1)}, u32[]{:S(2)}) copy-start(bf16[12,32,256]{2,1,0:T(8,128)(2,1)S(1)} %collective-permute-done.2.refs_3_) | copy-start | bytes 589828
  54.3 2.2 %collective-permute-start.7 = (bf16[12,32,256]{2,1,0:T(8,128)(2,1)S(1)}, bf16[12,32,256]{2,1,0:T(8,128)(2,1)S(1)}, u32[]{:S(2)}, u32[]{:S(2)}) collective-permute-start(bf16[12,32,256]{2,1,0:T(8,128)(2,1)S(1)} %collective-permute-done.2.refs_3_), channel_id=1, source_target_pairs={{0,1},{1,0},{2,3},{3,2},{4,5},{5,4},{6,7},{7,6},{8,9},{9,8},{10,11... | collective-permute-start | bytes 589832 | tf_op jit(solution)/shard_map/ppermute | solution.py:236
  56.2 0.8 copy-start.10
  56.2 0.8 copy-start.15
  56.3 0.9 %copy-start.11 = (bf16[12,64,256]{2,1,0:T(8,128)(2,1)}, bf16[12,64,256]{2,1,0:T(8,128)(2,1)S(1)}, u32[]{:S(2)}) copy-start(bf16[12,64,256]{2,1,0:T(8,128)(2,1)S(1)} %collective-permute-done.6.refs_7_) | copy-start | bytes 1179652
  56.5 0.7 copy-start.16
  56.5 0.9 %copy-start.12 = (bf16[12,64,256]{2,1,0:T(8,128)(2,1)}, bf16[12,64,256]{2,1,0:T(8,128)(2,1)S(1)}, u32[]{:S(2)}) copy-start(bf16[12,64,256]{2,1,0:T(8,128)(2,1)S(1)} %collective-permute-done.5.refs_6_) | copy-start | bytes 1179652

commit v2 on v1

v2 whole, which is shorter than its diff:
```python
import functools

import jax
import jax.numpy as jnp
from jax import lax
from jax.experimental import pallas as pl
from jax.experimental.pallas import tpu as pltpu
from jax.sharding import PartitionSpec as P

STATE_CH = 96
CONTEXT_CH = 96
NOISE_CH = 8
TILE = 64
REACH = 3
HALO = 2
ROWS = 64
COLS = 256
CHUNK = 16
STEPS = ROWS // CHUNK
SIDE_CH = CONTEXT_CH + 16
PIECE = CONTEXT_CH // 8
EDGE_CH = STATE_CH + 32
S3 = 3 * STATE_CH
C3 = 3 * SIDE_CH
BF16 = jnp.bfloat16
F32 = jnp.float32


def put_taps(ref, first, row):
    count = row.shape[0]
    edge = jnp.zeros((count, 1), row.dtype)
    ref[pl.ds(first, count), :] = jnp.concatenate([edge, row[:, : COLS - 1]], axis=1)
    ref[pl.ds(first + count, count), :] = row
    ref[pl.ds(first + 2 * count, count), :] = jnp.concatenate([row[:, 1:], edge], axis=1)


def logistic(x):
    return 0.5 * jnp.tanh(0.5 * x) + 0.5


def edge_kernel(state_top, state_low, noise_top, noise_low, context_top, context_low, top, low):
    def fill(ref, first, state, noise, context):
        def rows(a):
            return jnp.transpose(a[...], (1, 0, 2))[first : first + HALO]

        ref[:, :STATE_CH] = rows(state)
        ref[:, STATE_CH:] = jnp.zeros((HALO, EDGE_CH - STATE_CH, COLS), BF16)
        ref[:, STATE_CH : STATE_CH + NOISE_CH] = rows(noise)
        ref[:, STATE_CH + 16 : STATE_CH + 16 + PIECE] = rows(context)

    fill(top, 0, state_top, noise_top, context_top)
    fill(low, CHUNK - HALO, state_low, noise_low, context_low)


def edges(state, noise, context):
    def block(channels, n):
        return pl.BlockSpec((channels, CHUNK, COLS), lambda i: (0, n, 0))

    last = ROWS // CHUNK - 1
    shape = jax.ShapeDtypeStruct((HALO, EDGE_CH, COLS), BF16)
    return pl.pallas_call(
        edge_kernel,
        grid=(1,),
        in_specs=[block(count, n) for count in (STATE_CH, NOISE_CH, PIECE) for n in (0, last)],
        out_specs=[whole(HALO, EDGE_CH, COLS)] * 2,
        out_shape=[shape, shape],
        compiler_params=pltpu.CompilerParams(vmem_limit_bytes=60 * 2**20),
        cost_estimate=pl.CostEstimate(flops=0, bytes_accessed=4_000_000, transcendentals=0),
        name="edges",
    )(state, state, noise, noise, context, context)


def joined_taps(kernel, first, count, padded):
    parts = []
    for tap in range(9):
        parts.append(kernel[tap, :, first : first + count])
        if padded > count:
            parts.append(jnp.zeros((kernel.shape[1], padded - count), BF16))
    return jnp.concatenate(parts, axis=1)


def inside(row, is_inside):
    return jnp.where(is_inside, row, jnp.zeros_like(row))


def state_kernel(first, count, *refs):
    state, following, kernel = refs[:3]
    last = first + count == STEPS
    if last:
        above, below, top = refs[3:6]
        sums, by_row, rim_sums, taps, weights, sums_buf, sems, rim_taps = refs[8:]
    else:
        sums, by_row, taps, weights, sums_buf, sems = refs[3:]
    turn = pl.program_id(0)
    half = CHUNK // 2

    def sums_copy(part, n):
        start = pl.multiple_of((first + part) * CHUNK + n * half, half)
        source = sums_buf.at[part, pl.ds(n * half, half)]
        return pltpu.make_async_copy(source, sums.at[pl.ds(start, half)], sems.at[part, n])

    def sums_at(ref, place):
        return jnp.dot(weights[...], ref[place * S3 : (place + 3) * S3, :], preferred_element_type=F32)

    here = jnp.transpose(state[...], (1, 0, 2))
    by_row[...] = here

    @pl.when(turn == 0)
    def _():
        weights[...] = joined_taps(kernel, 0, STATE_CH, STATE_CH)
        for n in range(CHUNK):
            put_taps(taps, n * S3, here[n])
        if last:
            not_first = lax.axis_index("space") > 0
            for n in range(HALO):
                put_taps(rim_taps, n * S3, inside(above[n, :STATE_CH], not_first))
                put_taps(rim_taps, (HALO + n) * S3, top[n, :STATE_CH])
            for n in range(HALO):
                rim_sums[n] = sums_at(rim_taps, n)

    rows = jnp.transpose(following[...], (1, 0, 2))
    for n in range(CHUNK):
        sums_buf[turn, n] = sums_at(taps, n)
        if n == half - 1:
            sums_copy(turn, 0).start()
        row = rows[n]
        if n < HALO:
            if last:
                not_last = lax.axis_index("space") < lax.axis_size("space") - 1
                row = jnp.where(turn == count - 1, inside(below[n, :STATE_CH], not_last), row)
            put_taps(taps, (CHUNK + n) * S3, row)
        put_taps(taps, n * S3, row)
    sums_copy(turn, 1).start()

    @pl.when(turn == count - 1)
    def _():
        for part in range(count):
            for n in range(2):
                sums_copy(part, n).wait()


def state_part(first, count, state, kernel, rims=None, before=None):
    last = first + count == STEPS
    extra = [*rims, *before] if last else []
    any_space = pl.BlockSpec(memory_space=pl.ANY)
    shapes = [
        jax.ShapeDtypeStruct((ROWS, 2 * STATE_CH, COLS), F32),
        jax.ShapeDtypeStruct((ROWS, STATE_CH, COLS), BF16),
    ]
    specs = [any_space, pl.BlockSpec((CHUNK, STATE_CH, COLS), lambda i: (first + i, 0, 0))]
    scratch = [
        pltpu.VMEM(((CHUNK + HALO) * S3, COLS), BF16),
        pltpu.VMEM((2 * STATE_CH, 3 * S3), BF16),
        pltpu.VMEM((count, CHUNK, 2 * STATE_CH, COLS), F32),
        pltpu.SemaphoreType.DMA((count, 2)),
    ]
    if last:
        shapes.append(jax.ShapeDtypeStruct((HALO, 2 * STATE_CH, COLS), F32))
        specs.append(whole(HALO, 2 * STATE_CH, COLS))
        scratch.append(pltpu.VMEM((2 * HALO * S3, COLS), BF16))
    return pl.pallas_call(
        functools.partial(state_kernel, first, count),
        grid=(count,),
        in_specs=[
            pl.BlockSpec((STATE_CH, CHUNK, COLS), lambda i: (0, first + i, 0)),
            pl.BlockSpec((STATE_CH, CHUNK, COLS), lambda i: (0, jnp.minimum(first + i + 1, STEPS - 1), 0)),
            whole(*kernel.shape),
        ]
        + ([whole(HALO, EDGE_CH, COLS)] * 3 + [any_space] * 2 if last else []),
        out_specs=specs,
        out_shape=shapes,
        scratch_shapes=scratch,
        input_output_aliases={6: 0, 7: 1} if last else {},
        compiler_params=pltpu.CompilerParams(vmem_limit_bytes=60 * 2**20),
        cost_estimate=pl.CostEstimate(flops=3_000_000_000 * count, bytes_accessed=5_000_000 * count, transcendentals=0),
        name="state_part_%d" % first,
    )(state, state, kernel, *extra)


LAG = 3
MAIN = 256
REST = S3 - MAIN


def side_kernel(
    mine, others, noise, mine_rim, other_rim, above, below, sums, by_row, rim_sums, gate_kernel, candidate_kernel,
    active, offset, out, raw, w_side, w_reset, w_rest, sums_buf, rows_buf, rim_sums_buf, taps, rim_taps, reset_taps,
    rest_taps, update, partial, rows_done, context_rim, gate_buf, candidate_buf, piece_sems, sums_sems, sems,
):
    step = pl.program_id(0)
    half = ROWS // 2
    member = lax.axis_index("member")
    x, core = member // 2, member % 2

    def piece_copies(part):
        copies = []
        for n in range(8):
            piece = (mine if n < 4 else others)[n % 4]
            side = core if n < 4 else 1 - core
            near = 3 - 2 * side
            place = 2 * lax.rem(x + (0, near, 4 - near, 2)[n % 4], 4) + side
            rows = pl.ds(part * half, half)
            target = raw.at[pl.ds(place * PIECE, PIECE), rows, :]
            copies.append(pltpu.make_async_copy(piece.at[:, rows, :], target, piece_sems.at[part, n]))
        copies.append(
            pltpu.make_async_copy(
                noise.at[:, pl.ds(part * half, half), :],
                raw.at[pl.ds(CONTEXT_CH, NOISE_CH), pl.ds(part * half, half), :],
                piece_sems.at[part, 8],
            )
        )
        return copies

    def sums_copy(n):
        slot = lax.rem(n, 2)
        rows = pl.ds(pl.multiple_of(n * CHUNK, CHUNK), CHUNK)
        return pltpu.make_async_copy(sums.at[rows], sums_buf.at[slot], sums_sems.at[slot])

    def sums_at(ref, place):
        return jnp.dot(w_side[...], ref[place * C3 : (place + 3) * C3, :], preferred_element_type=F32)

    not_first = lax.axis_index("space") > 0
    not_last = lax.axis_index("space") < lax.axis_size("space") - 1

    def gates(row_sums, state_sums, carried, slots):
        reset = logistic(row_sums[STATE_CH : 2 * STATE_CH] + state_sums[STATE_CH:])
        reset_row = (reset * carried.astype(F32)).astype(BF16)
        kept = logistic(row_sums[:STATE_CH] + state_sums[:STATE_CH])
        edge = jnp.zeros((STATE_CH, 1), BF16)
        right = jnp.concatenate([reset_row[:, 1:], edge], axis=1)
        first = slots[0] % 4 * MAIN
        reset_taps[first : first + STATE_CH] = jnp.concatenate([edge, reset_row[:, : COLS - 1]], axis=1)
        reset_taps[first + STATE_CH : first + 2 * STATE_CH] = reset_row
        reset_taps[first + 2 * STATE_CH : first + MAIN] = right[: MAIN - 2 * STATE_CH]
        for slot in slots:
            rest_taps[slot * REST : (slot + 1) * REST] = right[MAIN - 2 * STATE_CH :]
            update[slot] = kept

    def candidate_terms(slot, side_terms):
        first = slot % 4 * MAIN
        terms = jnp.dot(w_reset[...], reset_taps[first : first + MAIN, :], preferred_element_type=F32)
        partial[slot + 1] = terms[:STATE_CH]
        if slot > 0:
            partial[slot] += terms[STATE_CH : 2 * STATE_CH] + side_terms
        return terms[2 * STATE_CH :]

    @pl.when(step == 0)
    def _():
        raw[CONTEXT_CH + NOISE_CH :] = jnp.zeros((SIDE_CH - CONTEXT_CH - NOISE_CH, ROWS, COLS), BF16)
        first_half = piece_copies(0)
        for copy in first_half:
            copy.start()
        rest = [
            pltpu.make_async_copy(a, b, sems.at[n])
            for n, (a, b) in enumerate(
                ((gate_kernel, gate_buf), (candidate_kernel, candidate_buf), (rim_sums, rim_sums_buf), (by_row, rows_buf))
            )
        ]
        for copy in rest:
            copy.start()
        sums_copy(0).start()
        for copy in piece_copies(1):
            copy.start()
        for copy in rest[:2]:
            copy.wait()
        channels = CONTEXT_CH + NOISE_CH
        w_side[: 2 * STATE_CH] = joined_taps(gate_buf, STATE_CH, channels, SIDE_CH)
        w_side[2 * STATE_CH :] = joined_taps(candidate_buf, STATE_CH, channels, SIDE_CH)
        for a in range(3):
            left, middle, right = (candidate_buf[3 * a + n, :, :STATE_CH] for n in range(3))
            w_reset[a * STATE_CH : (a + 1) * STATE_CH] = jnp.concatenate(
                [left, middle, right[:, : MAIN - 2 * STATE_CH]], axis=1
            )
        w_rest[...] = jnp.concatenate(
            [candidate_buf[3 * a + 2, :, MAIN - 2 * STATE_CH : STATE_CH] for a in range(3)], axis=1
        )
        for n in range(2 * HALO):
            parts = []
            for place in range(4):
                turned = lax.rem(place + 4 - x, 4)
                a, b = mine_rim[turned, n].astype(F32), other_rim[turned, n].astype(F32)
                parts += [jnp.where(core == 0, a, b), jnp.where(core == 0, b, a)]
            context_rim[n] = inside(jnp.concatenate(parts, axis=0), not_first if n < HALO else not_last).astype(BF16)
        for copy in first_half:
            copy.wait()
        chunk = jnp.transpose(raw[:, :CHUNK, :], (1, 0, 2))
        for n in range(HALO):
            noise_rim = inside(above[n, STATE_CH : STATE_CH + 16], not_first)
            put_taps(rim_taps, n * C3, jnp.concatenate([context_rim[n], noise_rim], axis=0))
            put_taps(rim_taps, (HALO + n) * C3, chunk[n])
        for n in range(CHUNK):
            put_taps(taps, n * C3, chunk[n])
        for copy in rest[2:]:
            copy.wait()
        gates(sums_at(rim_taps, 0), rim_sums_buf[0], inside(above[1, :STATE_CH], not_first), (0,))
        candidate_terms(0, None)
        row_sums = sums_at(rim_taps, 1)
        gates(row_sums, rim_sums_buf[1], rows_buf[0], (1,))
        candidate_terms(1, row_sums[2 * STATE_CH :])

    @pl.when(step == 1)
    def _():
        for copy in piece_copies(1):
            copy.wait()

    @pl.when(step + 1 < STEPS)
    def _():
        sums_copy(step + 1).start()

    sums_copy(step).wait()
    state_sums = sums_buf.at[lax.rem(step, 2)]
    here = pl.multiple_of(step * CHUNK, CHUNK)
    owner = lax.axis_index("space")
    tile = lax.broadcasted_iota(jnp.int32, (1, COLS), 1) // TILE
    chosen = jnp.zeros((1, COLS), jnp.bool_)
    for n in range(COLS // TILE):
        used = (active[n, owner] == 1) & (offset[n, owner] < REACH)
        chosen = chosen | ((tile == n) & used)
    later = jnp.minimum(step + 1, STEPS - 1) * CHUNK
    chunk = jnp.transpose(raw[:, pl.ds(pl.multiple_of(later, CHUNK), CHUNK), :], (1, 0, 2))

    def candidate(n, side_terms):
        slot = n + 1
        terms = candidate_terms(slot + 1, side_terms)
        rest = jnp.dot(w_rest[...], rest_taps[n * REST : (n + 3) * REST, :], preferred_element_type=F32)
        proposal = jnp.tanh(partial[slot] + terms + rest)
        old = rows_buf[here + n].astype(F32)
        new = (1.0 - update[slot]) * old + update[slot] * proposal
        rows_done[n] = jnp.where(chosen, new, old).astype(BF16)

    waiting = []
    for n in range(CHUNK):
        row_sums = sums_at(taps, n)
        carried = rows_buf[jnp.minimum(here + n + 1, ROWS - 1)]
        if n == CHUNK - 1:
            carried = jnp.where(step == STEPS - 1, inside(below[0, :STATE_CH], not_last), carried)
        if len(waiting) == LAG:
            candidate(n - LAG, waiting.pop(0))
        gates(row_sums, state_sums[n], carried, (n + 2,) if n < CHUNK - HALO else (n + 2, n + 2 - CHUNK))
        waiting.append(row_sums[2 * STATE_CH :])
        row = chunk[n]
        if n < HALO:
            noise_rim = inside(below[n, STATE_CH : STATE_CH + 16], not_last)
            row = jnp.where(step == STEPS - 1, jnp.concatenate([context_rim[HALO + n], noise_rim], axis=0), row)
            put_taps(taps, (CHUNK + n) * C3, row)
        put_taps(taps, n * C3, row)
    for n in range(CHUNK - LAG, CHUNK):
        candidate(n, waiting.pop(0))
    for n in range(1, 3):
        partial[n] = partial[CHUNK + n]
    out[...] = jnp.transpose(rows_done[...], (1, 0, 2))


def whole(*shape):
    return pl.BlockSpec(shape, lambda i: (0,) * len(shape))


def side_part(
    mine, others, noise, mine_rim, other_rim, above, below, sums, by_row, rim_sums, gate_kernel, candidate_kernel,
    active, offset,
):
    def kernel(*refs):
        side_kernel(refs[:4], refs[4:8], *refs[8:])

    smem = pl.BlockSpec(memory_space=pltpu.SMEM)
    any_space = pl.BlockSpec(memory_space=pl.ANY)
    rim_spec = whole(*mine_rim.shape)
    return pl.pallas_call(
        kernel,
        grid=(STEPS,),
        in_specs=[any_space] * 9
        + [rim_spec, rim_spec, whole(HALO, EDGE_CH, COLS), whole(HALO, EDGE_CH, COLS)]
        + [any_space] * 5
        + [smem, smem],
        out_specs=pl.BlockSpec((STATE_CH, CHUNK, COLS), lambda i: (0, i, 0)),
        out_shape=jax.ShapeDtypeStruct((STATE_CH, ROWS, COLS), BF16),
        scratch_shapes=[
            pltpu.VMEM((SIDE_CH, ROWS, COLS), BF16),
            pltpu.VMEM((3 * STATE_CH, 3 * C3), BF16),
            pltpu.VMEM((3 * STATE_CH, MAIN), BF16),
            pltpu.VMEM((STATE_CH, 3 * REST), BF16),
            pltpu.VMEM((2, CHUNK, 2 * STATE_CH, COLS), F32),
            pltpu.VMEM((ROWS, STATE_CH, COLS), BF16),
            pltpu.VMEM((HALO, 2 * STATE_CH, COLS), F32),
            pltpu.VMEM(((CHUNK + HALO) * C3, COLS), BF16),
            pltpu.VMEM((2 * HALO * C3, COLS), BF16),
            pltpu.VMEM((4 * MAIN, COLS), BF16),
            pltpu.VMEM(((CHUNK + HALO) * REST, COLS), BF16),
            pltpu.VMEM((CHUNK + HALO, STATE_CH, COLS), F32),
            pltpu.VMEM((CHUNK + HALO + 1, STATE_CH, COLS), F32),
            pltpu.VMEM((CHUNK, STATE_CH, COLS), BF16),
            pltpu.VMEM((2 * HALO, CONTEXT_CH, COLS), BF16),
            pltpu.VMEM(gate_kernel.shape, BF16),
            pltpu.VMEM(candidate_kernel.shape, BF16),
            pltpu.SemaphoreType.DMA((2, 9)),
            pltpu.SemaphoreType.DMA((2,)),
            pltpu.SemaphoreType.DMA((4,)),
        ],
        compiler_params=pltpu.CompilerParams(vmem_limit_bytes=60 * 2**20),
        cost_estimate=pl.CostEstimate(flops=17_000_000_000, bytes_accessed=20_000_000, transcendentals=0),
        name="side_part",
    )(
        *mine, *others, noise, mine_rim, other_rim, above, below, sums, by_row, rim_sums, gate_kernel, candidate_kernel,
        active, offset,
    )


def by_tap(kernel):
    return jnp.transpose(kernel, (2, 3, 0, 1)).reshape((9,) + kernel.shape[:2])


def along_x(by):
    return [(2 * x + core, 2 * ((x + by) % 4) + core) for x in range(4) for core in range(2)]


FORTH = [(2 * x + core, 2 * ((x + 1 - 2 * core) % 4) + core) for x in range(4) for core in range(2)]
BACK = [(b, a) for a, b in FORTH]
CORES = [(n, n ^ 1) for n in range(8)]


def shards(state_field, context_field, noise_latent, gate_kernel, candidate_kernel, active_tiles, tile_offset):
    owners = lax.axis_size("space")
    state = state_field[0]
    noise = noise_latent[0, 0]

    def to_core(a):
        return lax.ppermute(a, "member", CORES)

    forth = lax.ppermute(context_field, "member", FORTH)
    back = lax.ppermute(context_field, "member", BACK)
    top, low = edges(state, noise, context_field)
    above = lax.ppermute(low, "space", [(n, (n + 1) % owners) for n in range(owners)])
    below = lax.ppermute(top, "space", [((n + 1) % owners, n) for n in range(owners)])
    gate_kernel, candidate_kernel = by_tap(gate_kernel), by_tap(candidate_kernel)
    state, top = lax.optimization_barrier((state, top))
    before = state_part(0, 2, state, gate_kernel)

    before, forth, back, above, below = lax.optimization_barrier((before, forth, back, above, below))
    far = lax.ppermute(forth, "member", FORTH)
    others = [to_core(context_field), to_core(forth), to_core(back)]
    side = slice(STATE_CH + 16, STATE_CH + 16 + PIECE)
    rim = jnp.concatenate([above[:, side], below[:, side]], axis=0)
    rims = [rim] + [lax.ppermute(rim, "member", along_x(by)) for by in (3, 2, 1)]
    sums, by_row, rim_sums = state_part(2, 2, state, gate_kernel, (above, below, top), before)

    sums, rims, far = lax.optimization_barrier((sums, rims, far))
    others.append(to_core(far))
    mine_rim = jnp.stack(rims)
    mine = [context_field, forth, back, far]
    result = side_part(
        mine, others, noise, mine_rim, to_core(mine_rim), above, below, sums, by_row, rim_sums, gate_kernel,
        candidate_kernel, active_tiles.T, tile_offset.T,
    )
    return result[None]


def solution(mesh):
    return jax.shard_map(
        shards,
        mesh=mesh,
        in_specs=(
            P("member", None, "space", None),
            P("member", "space", None),
            P("member", None, None, "space", None),
            P(),
            P(),
            P(),
            P(),
        ),
        out_specs=P("member", None, "space", None),
        check_vma=False,
    )
```

time: 84.8 us -> 64.2 us (0.76)
  local copies, waits for them, and re-layouts: 11.9 us -> 0.78 us
  waiting for transfers between devices: 10.5 us -> 1.66 us
  Pallas kernels: 41.7 us -> 43.3 us
  other arithmetic: 1.16 us -> 0.04 us
    ppermute x15 -> x13, waiting for transfers between devices: 10.5 us -> 1.66 us  [the longest x5 1.64 us: to_core(): return lax.ppermute(a, 'member', CORES)]
    unnamed x41 -> x22, local copies, waits for them, and re-layouts: 7.86 us -> 0.78 us
    concatenate x5 -> x0, local copies, waits for them, and re-layouts: 2.33 us -> none  [the longest x3 2.25 us: tap_weights(): jnp.concatenate([taps[a, b] for a in range(3) for b in range(3)], axis=1)]
    pallas_call x2 -> x4, Pallas kernels: 41.7 us -> 43.3 us  [the longest x1 23.8 us: side_part(): pl.pallas_call(kernel, grid=(STEPS,), in_specs=[any_space] * 9 + [rim_spe...]
    slice x9 -> x2, local copies, waits for them, and re-layouts: 1.25 us -> 0.01 us  [shards(): rim = jnp.concatenate([above[:, side], below[:, side]], axis=0)]
    ppermute x15 -> x13, starting transfers between devices: 18.7 us -> 17.9 us  [the longest x1 4.57 us: shards(): lax.ppermute(top, 'space', [((n + 1) % owners, n) for n in range(owners)])]
  transfers between devices with their start and end apart: 15 -> 13, of which waited for: 5 -> 3; matrix products, arithmetic and copies ran while one was open for 14% -> 0% of each run, Pallas kernels for 17% -> 31%
where the time goes in v2:
time: 64.2 us; the launch traced here: 64 us
  Pallas kernels  43.3 us (67%)
  starting transfers between devices  17.9 us (28%)
  waiting for transfers between devices  1.66 us (3%)
  local copies, waits for them, and re-layouts  0.78 us (1%)
    pallas_call x1, Pallas kernels, side_part(): pl.pallas_call(kernel, grid=(STEPS,), in_specs=[any_space] * 9 + [rim_spe...  23.8 us
    pallas_call x2, Pallas kernels, state_part(): pl.pallas_call(functools.partial(state_kernel, first, count), grid=(count...  17.3 us
    ppermute x1, starting transfers between devices, shards(): lax.ppermute(top, 'space', [((n + 1) % owners, n) for n in range(owners)])  4.57 us
    ppermute x5, starting transfers between devices, to_core(): return lax.ppermute(a, 'member', CORES)  3.72 us
    ppermute x1, starting transfers between devices, shards(): forth = lax.ppermute(context_field, 'member', FORTH)  3.31 us
    ppermute x3, starting transfers between devices, shards(): lax.ppermute(rim, 'member', along_x(by))  2.46 us
    pallas_call x1, Pallas kernels, edges(): pl.pallas_call(edge_kernel, grid=(1,), in_specs=[block(count, n) for coun...  2.23 us
    ppermute x1, starting transfers between devices, shards(): far = lax.ppermute(forth, 'member', FORTH)  2.07 us
  transfers between devices with their start and end apart: 13, of which 3 were waited for; matrix products, arithmetic and copies ran while one was open for 0% of the time, Pallas kernels for 31%

profile of v2, /device:TPU:1, one launch (start us, length us, event | category | flops | bytes accessed | tf_op | source)
XLA Modules:
  0.0 64.0 jit_solution(14612367820896944555)
XLA Ops:
  0.0 3.3 %collective-permute-start = (bf16[12,64,256]{2,1,0:T(8,128)(2,1)}, bf16[12,64,256]{2,1,0:T(8,128)(2,1)S(1)}, u32[]{:S(2)}, u32[]{:S(2)}) collective-permute-start(bf16[12,64,256]{2,1,0:T(8,128)(2,1)} %refs_0_.1), channel_id=1, source_target_pairs={{0,2},{1,7},{2,4},{3,1},{4,6},{5,3},{6,0},{7,5},{8,10},{9,15},{10,... | collective-permute-start | bytes 1179656 | tf_op jit(solution)/shard_map/ppermute | solution.py:429
  3.3 0.0 collective-permute-start.1
  3.3 1.3 %collective-permute-start.8 = (bf16[12,64,256]{2,1,0:T(8,128)(2,1)}, bf16[12,64,256]{2,1,0:T(8,128)(2,1)S(1)}, u32[]{:S(2)}, u32[]{:S(2)}) collective-permute-start(bf16[12,64,256]{2,1,0:T(8,128)(2,1)} %refs_0_.1), channel_id=1, source_target_pairs={{0,1},{1,0},{2,3},{3,2},{4,5},{5,4},{6,7},{7,6},{8,9},{9,8},{10,11... | collective-permute-start | bytes 1179656 | tf_op jit(solution)/shard_map/ppermute | solution.py:427
  4.7 2.2 %edges.1 = (bf16[2,128,256]{2,1,0:T(8,128)(2,1)}, bf16[2,128,256]{2,1,0:T(8,128)(2,1)}) custom-call(bf16[96,64,256]{2,1,0:T(8,128)(2,1)} %bitcast.15, bf16[96,64,256]{2,1,0:T(8,128)(2,1)} %bitcast.16, bf16[8,64,256]{2,1,0:T(8,128)(2,1)} %bitcast.21, bf16[8,64,256]{2,1,0:T(8,128)(2,1)} %bitcast.22, bf16[12,64,256]{2,1,0:T(8,128)(2,1)} %refs_0_.1, ...), custom_call_target="tpu_custom_call" | custom-call | bytes 4000000 | tf_op jit(solution)/shard_map/edges/pallas_call | solution.py:61
  6.9 1.7 %collective-permute-start.2 = (bf16[2,128,256]{2,1,0:T(8,128)(2,1)}, bf16[2,128,256]{2,1,0:T(8,128)(2,1)S(1)}, u32[]{:S(2)}, u32[]{:S(2)}) collective-permute-start(bf16[2,128,256]{2,1,0:T(8,128)(2,1)} %get-tuple-element.30), channel_id=1, source_target_pairs={{0,8},{8,16},{16,24},{24,32},{32,40},{40,48},{48,56},{56,64},{64,7... | collective-permute-start | bytes 393224 | tf_op jit(solution)/shard_map/ppermute | solution.py:432
  8.6 4.6 %collective-permute-start.3 = (bf16[2,128,256]{2,1,0:T(8,128)(2,1)}, bf16[2,128,256]{2,1,0:T(8,128)(2,1)S(1)}, u32[]{:S(2)}, u32[]{:S(2)}) collective-permute-start(bf16[2,128,256]{2,1,0:T(8,128)(2,1)} %get-tuple-element.35.refs_5_), channel_id=1, source_target_pairs={{8,0},{16,8},{24,16},{32,24},{40,32},{48,40},{56,48},{64,56},{72,6... | collective-permute-start | bytes 393224 | tf_op jit(solution)/shard_map/ppermute | solution.py:433
  13.2 8.4 %state_part_0.1 = (f32[64,192,256]{2,1,0:T(8,128)}, bf16[64,96,256]{2,1,0:T(8,128)(2,1)}) custom-call(bf16[96,64,256]{2,1,0:T(8,128)(2,1)} %bitcast.17, bf16[96,64,256]{2,1,0:T(8,128)(2,1)} %bitcast.18, bf16[9,192,200]{2,1,0:T(8,128)(2,1)} %bitcast.24), custom_call_target="tpu_custom_call" | custom-call | flops 6000000000 | bytes 10000000 | tf_op jit(solution)/shard_map/state_part_0/pallas_call | solution.py:161
  21.6 0.0 collective-permute-done.2.refs_3_.refs_11_
  21.7 0.0 collective-permute-done.3.refs_4_.refs_12_
  21.7 0.0 collective-permute-done.refs_1_
  21.7 0.0 collective-permute-done.1.refs_2_
  21.8 1.4 %collective-permute-start.4 = (bf16[4,12,256]{2,1,0:T(8,128)(2,1)S(1)}, bf16[4,12,256]{2,1,0:T(8,128)(2,1)S(1)}, u32[]{:S(2)}, u32[]{:S(2)}) collective-permute-start(bf16[4,12,256]{2,1,0:T(8,128)(2,1)S(1)} %pad_maximum_fusion.1), channel_id=1, source_target_pairs={{0,6},{1,7},{2,0},{3,1},{4,2},{5,3},{6,4},{7,5},{8,14},{9,15},{10,... | collective-permute-start | bytes 73736 | tf_op jit(solution)/shard_map/ppermute | solution.py:443
  23.1 0.5 collective-permute-start.5
  23.6 0.6 collective-permute-start.6
  24.2 2.1 %collective-permute-start.7 = (bf16[12,64,256]{2,1,0:T(8,128)(2,1)S(1)}, bf16[12,64,256]{2,1,0:T(8,128)(2,1)S(1)}, u32[]{:S(2)}, u32[]{:S(2)}) collective-permute-start(bf16[12,64,256]{2,1,0:T(8,128)(2,1)S(1)} %collective-permute-done.refs_1_), channel_id=1, source_target_pairs={{0,2},{1,7},{2,4},{3,1},{4,6},{5,3},{6,0},{7,5},{8,10},{9,15},{10,... | collective-permute-start | bytes 1179656 | tf_op jit(solution)/shard_map/ppermute | solution.py:439
  26.3 8.9 %state_part_2.1 = (f32[64,192,256]{2,1,0:T(8,128)}, bf16[64,96,256]{2,1,0:T(8,128)(2,1)}, f32[2,192,256]{2,1,0:T(8,128)}) custom-call(bf16[96,64,256]{2,1,0:T(8,128)(2,1)} %bitcast.19, bf16[96,64,256]{2,1,0:T(8,128)(2,1)} %bitcast.20, bf16[9,192,200]{2,1,0:T(8,128)(2,1)} %bitcast.25, ...), custom_call_target="tpu_custom_call", output_to_operand_aliasing={{0}: (6, {}), {1}: (7, {})} | custom-call | flops 6000000000 | bytes 10000000 | tf_op jit(solution)/shard_map/state_part_2/pallas_call | solution.py:161
  35.2 0.0 collective-permute-done.4
  35.2 1.4 %collective-permute-start.9 = (bf16[12,64,256]{2,1,0:T(8,128)(2,1)S(1)}, bf16[12,64,256]{2,1,0:T(8,128)(2,1)S(1)}, u32[]{:S(2)}, u32[]{:S(2)}) collective-permute-start(bf16[12,64,256]{2,1,0:T(8,128)(2,1)S(1)} %collective-permute-done.refs_1_), channel_id=1, source_target_pairs={{0,1},{1,0},{2,3},{3,2},{4,5},{5,4},{6,7},{7,6},{8,9},{9,8},{10,11... | collective-permute-start | bytes 1179656 | tf_op jit(solution)/shard_map/ppermute | solution.py:427
  36.6 0.0 collective-permute-done.5
  36.6 0.1 collective-permute-start.10
  36.7 0.0 collective-permute-done.6
  36.7 0.0 collective-permute-done.7.refs_3_
  36.7 0.5 collective-permute-start.11
  37.3 0.4 collective-permute-start.12
  37.6 0.0 collective-permute-done.8.refs_4_
  37.6 0.3 collective-permute-done.9.refs_5_
  38.0 0.6 collective-permute-done.10.refs_6_
  38.5 0.7 %collective-permute-done.12.refs_10_ = bf16[4,4,12,256]{3,2,1,0:T(8,128)(2,1)S(1)} collective-permute-done((bf16[4,4,12,256]{3,2,1,0:T(8,128)(2,1)S(1)}, bf16[4,4,12,256]{3,2,1,0:T(8,128)(2,1)S(1)}, u32[]{:S(2)}, u32[]{:S(2)}) %collective-permute-start.12) | collective-permute-done | bytes 98336 | tf_op jit(solution)/shard_map/ppermute | solution.py:427
  39.3 0.0 collective-permute-done.11.refs_7_
  39.3 0.6 copy-done.10
  39.9 0.1 copy-done.9
  40.1 23.8 %side_part.1 = bf16[96,64,256]{2,1,0:T(8,128)(2,1)} custom-call(bf16[12,64,256]{2,1,0:T(8,128)(2,1)} %refs_0_.1, bf16[12,64,256]{2,1,0:T(8,128)(2,1)} %copy-done.3, bf16[12,64,256]{2,1,0:T(8,128)(2,1)} %copy-done.4, bf16[12,64,256]{2,1,0:T(8,128)(2,1)} %copy-done.6, bf16[12,64,256]{2,1,0:T(8,128)(2,1)} %copy-done.5, bf16[12,64,256]{2,1,0:T(8,128)(2,1)} %copy-done.7, ...), custom_call_target="tpu_custom_call" | custom-call | flops 16999999488 | bytes 20000000 | tf_op jit(solution)/shard_map/side_part/pallas_call | solution.py:368
  (24 shorter events, 0.1 us)
Async XLA Ops:
  0.0 21.7 %collective-permute-start = (bf16[12,64,256]{2,1,0:T(8,128)(2,1)}, bf16[12,64,256]{2,1,0:T(8,128)(2,1)S(1)}, u32[]{:S(2)}, u32[]{:S(2)}) collective-permute-start(bf16[12,64,256]{2,1,0:T(8,128)(2,1)} %refs_0_.1), channel_id=1, source_target_pairs={{0,2},{1,7},{2,4},{3,1},{4,6},{5,3},{6,0},{7,5},{8,10},{9,15},{10,... | collective-permute-start | bytes 1179656 | tf_op jit(solution)/shard_map/ppermute | solution.py:429
  3.3 18.4 %collective-permute-start.1 = (bf16[12,64,256]{2,1,0:T(8,128)(2,1)}, bf16[12,64,256]{2,1,0:T(8,128)(2,1)S(1)}, u32[]{:S(2)}, u32[]{:S(2)}) collective-permute-start(bf16[12,64,256]{2,1,0:T(8,128)(2,1)} %refs_0_.1), channel_id=1, source_target_pairs={{2,0},{7,1},{4,2},{1,3},{6,4},{3,5},{0,6},{5,7},{10,8},{15,9},{12,... | collective-permute-start | bytes 1179656 | tf_op jit(solution)/shard_map/ppermute | solution.py:430
  3.3 34.3 %collective-permute-start.8 = (bf16[12,64,256]{2,1,0:T(8,128)(2,1)}, bf16[12,64,256]{2,1,0:T(8,128)(2,1)S(1)}, u32[]{:S(2)}, u32[]{:S(2)}) collective-permute-start(bf16[12,64,256]{2,1,0:T(8,128)(2,1)} %refs_0_.1), channel_id=1, source_target_pairs={{0,1},{1,0},{2,3},{3,2},{4,5},{5,4},{6,7},{7,6},{8,9},{9,8},{10,11... | collective-permute-start | bytes 1179656 | tf_op jit(solution)/shard_map/ppermute | solution.py:427
  6.9 14.8 %collective-permute-start.2 = (bf16[2,128,256]{2,1,0:T(8,128)(2,1)}, bf16[2,128,256]{2,1,0:T(8,128)(2,1)S(1)}, u32[]{:S(2)}, u32[]{:S(2)}) collective-permute-start(bf16[2,128,256]{2,1,0:T(8,128)(2,1)} %get-tuple-element.30), channel_id=1, source_target_pairs={{0,8},{8,16},{16,24},{24,32},{32,40},{40,48},{48,56},{56,64},{64,7... | collective-permute-start | bytes 393224 | tf_op jit(solution)/shard_map/ppermute | solution.py:432
  8.6 13.1 %collective-permute-start.3 = (bf16[2,128,256]{2,1,0:T(8,128)(2,1)}, bf16[2,128,256]{2,1,0:T(8,128)(2,1)S(1)}, u32[]{:S(2)}, u32[]{:S(2)}) collective-permute-start(bf16[2,128,256]{2,1,0:T(8,128)(2,1)} %get-tuple-element.35.refs_5_), channel_id=1, source_target_pairs={{8,0},{16,8},{24,16},{32,24},{40,32},{48,40},{56,48},{64,56},{72,6... | collective-permute-start | bytes 393224 | tf_op jit(solution)/shard_map/ppermute | solution.py:433
  21.7 4.6 %copy-start = (bf16[2,128,256]{2,1,0:T(8,128)(2,1)}, bf16[2,128,256]{2,1,0:T(8,128)(2,1)S(1)}, u32[]{:S(2)}) copy-start(bf16[2,128,256]{2,1,0:T(8,128)(2,1)S(1)} %collective-permute-done.2.refs_3_.refs_11_) | copy-start | bytes 393220
  21.7 4.6 %copy-start.1 = (bf16[2,128,256]{2,1,0:T(8,128)(2,1)}, bf16[2,128,256]{2,1,0:T(8,128)(2,1)S(1)}, u32[]{:S(2)}) copy-start(bf16[2,128,256]{2,1,0:T(8,128)(2,1)S(1)} %collective-permute-done.3.refs_4_.refs_12_) | copy-start | bytes 393220
  21.7 13.5 %copy-start.3 = (bf16[12,64,256]{2,1,0:T(8,128)(2,1)}, bf16[12,64,256]{2,1,0:T(8,128)(2,1)S(1)}, u32[]{:S(2)}) copy-start(bf16[12,64,256]{2,1,0:T(8,128)(2,1)S(1)} %collective-permute-done.refs_1_) | copy-start | bytes 1179652
  21.7 14.9 %copy-start.4 = (bf16[12,64,256]{2,1,0:T(8,128)(2,1)}, bf16[12,64,256]{2,1,0:T(8,128)(2,1)S(1)}, u32[]{:S(2)}) copy-start(bf16[12,64,256]{2,1,0:T(8,128)(2,1)S(1)} %collective-permute-done.1.refs_2_) | copy-start | bytes 1179652
  21.8 13.4 %collective-permute-start.4 = (bf16[4,12,256]{2,1,0:T(8,128)(2,1)S(1)}, bf16[4,12,256]{2,1,0:T(8,128)(2,1)S(1)}, u32[]{:S(2)}, u32[]{:S(2)}) collective-permute-start(bf16[4,12,256]{2,1,0:T(8,128)(2,1)S(1)} %pad_maximum_fusion.1), channel_id=1, source_target_pairs={{0,6},{1,7},{2,0},{3,1},{4,2},{5,3},{6,4},{7,5},{8,14},{9,15},{10,... | collective-permute-start | bytes 73736 | tf_op jit(solution)/shard_map/ppermute | solution.py:443
  23.1 13.5 %collective-permute-start.5 = (bf16[4,12,256]{2,1,0:T(8,128)(2,1)S(1)}, bf16[4,12,256]{2,1,0:T(8,128)(2,1)S(1)}, u32[]{:S(2)}, u32[]{:S(2)}) collective-permute-start(bf16[4,12,256]{2,1,0:T(8,128)(2,1)S(1)} %pad_maximum_fusion.1), channel_id=1, source_target_pairs={{0,4},{1,5},{2,6},{3,7},{4,0},{5,1},{6,2},{7,3},{8,12},{9,13},{10,... | collective-permute-start | bytes 73736 | tf_op jit(solution)/shard_map/ppermute | solution.py:443
  23.6 13.1 %collective-permute-start.6 = (bf16[4,12,256]{2,1,0:T(8,128)(2,1)S(1)}, bf16[4,12,256]{2,1,0:T(8,128)(2,1)S(1)}, u32[]{:S(2)}, u32[]{:S(2)}) collective-permute-start(bf16[4,12,256]{2,1,0:T(8,128)(2,1)S(1)} %pad_maximum_fusion.1), channel_id=1, source_target_pairs={{0,2},{1,3},{2,4},{3,5},{4,6},{5,7},{6,0},{7,1},{8,10},{9,11},{10,... | collective-permute-start | bytes 73736 | tf_op jit(solution)/shard_map/ppermute | solution.py:443
  24.2 12.5 %collective-permute-start.7 = (bf16[12,64,256]{2,1,0:T(8,128)(2,1)S(1)}, bf16[12,64,256]{2,1,0:T(8,128)(2,1)S(1)}, u32[]{:S(2)}, u32[]{:S(2)}) collective-permute-start(bf16[12,64,256]{2,1,0:T(8,128)(2,1)S(1)} %collective-permute-done.refs_1_), channel_id=1, source_target_pairs={{0,2},{1,7},{2,4},{3,1},{4,6},{5,3},{6,0},{7,5},{8,10},{9,15},{10,... | collective-permute-start | bytes 1179656 | tf_op jit(solution)/shard_map/ppermute | solution.py:439
  35.2 2.8 %collective-permute-start.9 = (bf16[12,64,256]{2,1,0:T(8,128)(2,1)S(1)}, bf16[12,64,256]{2,1,0:T(8,128)(2,1)S(1)}, u32[]{:S(2)}, u32[]{:S(2)}) collective-permute-start(bf16[12,64,256]{2,1,0:T(8,128)(2,1)S(1)} %collective-permute-done.refs_1_), channel_id=1, source_target_pairs={{0,1},{1,0},{2,3},{3,2},{4,5},{5,4},{6,7},{7,6},{8,9},{9,8},{10,11... | collective-permute-start | bytes 1179656 | tf_op jit(solution)/shard_map/ppermute | solution.py:427
  36.6 1.9 %collective-permute-start.10 = (bf16[12,64,256]{2,1,0:T(8,128)(2,1)S(1)}, bf16[12,64,256]{2,1,0:T(8,128)(2,1)S(1)}, u32[]{:S(2)}, u32[]{:S(2)}) collective-permute-start(bf16[12,64,256]{2,1,0:T(8,128)(2,1)S(1)} %collective-permute-done.1.refs_2_), channel_id=1, source_target_pairs={{0,1},{1,0},{2,3},{3,2},{4,5},{5,4},{6,7},{7,6},{8,9},{9,8},{10,11... | collective-permute-start | bytes 1179656 | tf_op jit(solution)/shard_map/ppermute | solution.py:427
  36.7 2.6 %copy-start.6 = (bf16[12,64,256]{2,1,0:T(8,128)(2,1)}, bf16[12,64,256]{2,1,0:T(8,128)(2,1)S(1)}, u32[]{:S(2)}) copy-start(bf16[12,64,256]{2,1,0:T(8,128)(2,1)S(1)} %collective-permute-done.7.refs_3_) | copy-start | bytes 1179652
  36.7 2.5 %collective-permute-start.11 = (bf16[12,64,256]{2,1,0:T(8,128)(2,1)S(1)}, bf16[12,64,256]{2,1,0:T(8,128)(2,1)S(1)}, u32[]{:S(2)}, u32[]{:S(2)}) collective-permute-start(bf16[12,64,256]{2,1,0:T(8,128)(2,1)S(1)} %collective-permute-done.7.refs_3_), channel_id=1, source_target_pairs={{0,1},{1,0},{2,3},{3,2},{4,5},{5,4},{6,7},{7,6},{8,9},{9,8},{10,11... | collective-permute-start | bytes 1179656 | tf_op jit(solution)/shard_map/ppermute | solution.py:427
  37.2 2.0 %copy-start.2 = (bf16[4,4,12,256]{3,2,1,0:T(8,128)(2,1)}, bf16[4,4,12,256]{3,2,1,0:T(8,128)(2,1)S(1)}, u32[]{:S(2)}) copy-start(bf16[4,4,12,256]{3,2,1,0:T(8,128)(2,1)S(1)} %pad_maximum_fusion.refs_9_) | copy-start | bytes 294916
  37.3 2.0 %collective-permute-start.12 = (bf16[4,4,12,256]{3,2,1,0:T(8,128)(2,1)S(1)}, bf16[4,4,12,256]{3,2,1,0:T(8,128)(2,1)S(1)}, u32[]{:S(2)}, u32[]{:S(2)}) collective-permute-start(bf16[4,4,12,256]{3,2,1,0:T(8,128)(2,1)S(1)} %pad_maximum_fusion.refs_9_), channel_id=1, source_target_pairs={{0,1},{1,0},{2,3},{3,2},{4,5},{5,4},{6,7},{7,6},{8,9},{9,8},{10,11... | collective-permute-start | bytes 294920 | tf_op jit(solution)/shard_map/ppermute | solution.py:427
  37.6 1.7 %copy-start.5 = (bf16[12,64,256]{2,1,0:T(8,128)(2,1)}, bf16[12,64,256]{2,1,0:T(8,128)(2,1)S(1)}, u32[]{:S(2)}) copy-start(bf16[12,64,256]{2,1,0:T(8,128)(2,1)S(1)} %collective-permute-done.8.refs_4_) | copy-start | bytes 1179652
  38.0 1.3 %copy-start.7 = (bf16[12,64,256]{2,1,0:T(8,128)(2,1)}, bf16[12,64,256]{2,1,0:T(8,128)(2,1)S(1)}, u32[]{:S(2)}) copy-start(bf16[12,64,256]{2,1,0:T(8,128)(2,1)S(1)} %collective-permute-done.9.refs_5_) | copy-start | bytes 1179652
  38.5 0.8 %copy-start.8 = (bf16[12,64,256]{2,1,0:T(8,128)(2,1)}, bf16[12,64,256]{2,1,0:T(8,128)(2,1)S(1)}, u32[]{:S(2)}) copy-start(bf16[12,64,256]{2,1,0:T(8,128)(2,1)S(1)} %collective-permute-done.10.refs_6_) | copy-start | bytes 1179652
  39.3 0.7 %copy-start.10 = (bf16[4,4,12,256]{3,2,1,0:T(8,128)(2,1)}, bf16[4,4,12,256]{3,2,1,0:T(8,128)(2,1)S(1)}, u32[]{:S(2)}) copy-start(bf16[4,4,12,256]{3,2,1,0:T(8,128)(2,1)S(1)} %collective-permute-done.12.refs_10_) | copy-start | bytes 294916
  39.3 0.8 %copy-start.9 = (bf16[12,64,256]{2,1,0:T(8,128)(2,1)}, bf16[12,64,256]{2,1,0:T(8,128)(2,1)S(1)}, u32[]{:S(2)}) copy-start(bf16[12,64,256]{2,1,0:T(8,128)(2,1)S(1)} %collective-permute-done.11.refs_7_) | copy-start | bytes 1179652

commit v3 on v2

v3 whole, which is shorter than its diff:
```python
import functools

import jax
import jax.numpy as jnp
from jax import lax
from jax.experimental import pallas as pl
from jax.experimental.pallas import tpu as pltpu
from jax.sharding import PartitionSpec as P

STATE_CH = 96
CONTEXT_CH = 96
NOISE_CH = 8
TILE = 64
REACH = 3
HALO = 2
ROWS = 64
COLS = 256
CHUNK = 16
STEPS = ROWS // CHUNK
SIDE_CH = CONTEXT_CH + 16
PIECE = CONTEXT_CH // 8
EDGE_CH = STATE_CH + 32
RIM_CH = 16
S3 = 3 * STATE_CH
C3 = 3 * SIDE_CH
BF16 = jnp.bfloat16
F32 = jnp.float32


AHEAD = 4


def put_taps(ref, first, row):
    count = row.shape[0]
    edge = jnp.zeros((count, 1), row.dtype)
    ref[pl.ds(first, count), :] = jnp.concatenate([edge, row[:, : COLS - 1]], axis=1)
    ref[pl.ds(first + count, count), :] = row
    ref[pl.ds(first + 2 * count, count), :] = jnp.concatenate([row[:, 1:], edge], axis=1)


def logistic(x):
    return 0.5 * jnp.tanh(0.5 * x) + 0.5


def edge_kernel(state, noise, context, top, low, state_buf, noise_buf, context_buf, sems):
    copies = []
    for n, (source, buf) in enumerate(((state, state_buf), (noise, noise_buf), (context, context_buf))):
        for side, first in enumerate((0, ROWS - CHUNK)):
            rows = source.at[:, pl.ds(first, CHUNK), :]
            copies.append(pltpu.make_async_copy(rows, buf.at[side], sems.at[2 * n + side]))
    for copy in copies:
        copy.start()
    for copy in copies:
        copy.wait()
    for side, (ref, first) in enumerate(((top, 0), (low, CHUNK - HALO))):

        def rows(buf):
            return jnp.transpose(buf[side], (1, 0, 2))[first : first + HALO]

        ref[:, :STATE_CH] = rows(state_buf)
        ref[:, STATE_CH:] = jnp.zeros((HALO, EDGE_CH - STATE_CH, COLS), BF16)
        ref[:, STATE_CH : STATE_CH + NOISE_CH] = rows(noise_buf)
        ref[:, STATE_CH + 16 : STATE_CH + 16 + PIECE] = rows(context_buf)


def edges(state, noise, context):
    shape = jax.ShapeDtypeStruct((HALO, EDGE_CH, COLS), BF16)
    return pl.pallas_call(
        edge_kernel,
        in_specs=[pl.BlockSpec(memory_space=pltpu.HBM)] * 3,
        out_shape=[shape, shape],
        scratch_shapes=[pltpu.VMEM((2, count, CHUNK, COLS), BF16) for count in (STATE_CH, NOISE_CH, PIECE)]
        + [pltpu.SemaphoreType.DMA((6,))],
        compiler_params=pltpu.CompilerParams(vmem_limit_bytes=12 * 2**20),
        cost_estimate=pl.CostEstimate(flops=0, bytes_accessed=4_000_000, transcendentals=0),
        name="edges",
    )(*[pltpu.with_memory_space_constraint(a, pltpu.HBM) for a in (state, noise, context)])


def joined_taps(kernel, first, count, padded):
    parts = []
    for tap in range(9):
        parts.append(kernel[tap, :, first : first + count])
        if padded > count:
            parts.append(jnp.zeros((kernel.shape[1], padded - count), BF16))
    return jnp.concatenate(parts, axis=1)


def state_weights_kernel(gate, weights):
    weights[...] = joined_taps(gate, 0, STATE_CH, STATE_CH)


def side_weights_kernel(gate, candidate, w_side, w_reset, w_rest):
    channels = CONTEXT_CH + NOISE_CH
    w_side[: 2 * STATE_CH] = joined_taps(gate, STATE_CH, channels, SIDE_CH)
    w_side[2 * STATE_CH :] = joined_taps(candidate, STATE_CH, channels, SIDE_CH)
    for a in range(3):
        left, middle, right = (candidate[3 * a + n, :, :STATE_CH] for n in range(3))
        w_reset[a * STATE_CH : (a + 1) * STATE_CH] = jnp.concatenate(
            [left, middle, right[:, : MAIN - 2 * STATE_CH]], axis=1
        )
    w_rest[...] = jnp.concatenate([candidate[3 * a + 2, :, MAIN - 2 * STATE_CH : STATE_CH] for a in range(3)], axis=1)


def laid_out(kernel, name, shapes, *arrays):
    return pl.pallas_call(
        kernel,
        out_shape=[jax.ShapeDtypeStruct(shape, BF16) for shape in shapes],
        compiler_params=pltpu.CompilerParams(vmem_limit_bytes=12 * 2**20),
        cost_estimate=pl.CostEstimate(flops=0, bytes_accessed=3_000_000, transcendentals=0),
        name=name,
    )(*arrays)


def inside(row, is_inside):
    return jnp.where(is_inside, row, jnp.zeros_like(row))


def state_kernel(first, count, *refs):
    state, following, weights = refs[:3]
    last = first + count == STEPS
    if last:
        above, below, top = refs[3:6]
        sums, by_row, rim_sums, taps, sums_buf, sems, rim_taps = refs[8:]
    else:
        sums, by_row, taps, sums_buf, sems = refs[5 if first else 3 :]
    turn = pl.program_id(0)
    half = CHUNK // 2

    def sums_copy(part, n):
        start = pl.multiple_of((first + part) * CHUNK + n * half, half)
        source = sums_buf.at[part, pl.ds(n * half, half)]
        return pltpu.make_async_copy(source, sums.at[pl.ds(start, half)], sems.at[part, n])

    def sums_at(ref, place):
        return jnp.dot(weights[...], ref[place * S3 : (place + 3) * S3, :], preferred_element_type=F32)

    here = jnp.transpose(state[...], (1, 0, 2))
    by_row[...] = here

    @pl.when(turn == 0)
    def _():
        for n in range(AHEAD):
            put_taps(taps, n * S3, here[n])
        if last:
            not_first = lax.axis_index("space") > 0
            for n in range(HALO):
                put_taps(rim_taps, n * S3, inside(above[n, :STATE_CH], not_first))
                put_taps(rim_taps, (HALO + n) * S3, top[n, :STATE_CH])
            for n in range(HALO):
                rim_sums[n] = sums_at(rim_taps, n)

    rows = jnp.transpose(following[...], (1, 0, 2))
    for n in range(CHUNK):
        sums_buf[turn, n] = sums_at(taps, n)
        if n == half - 1:
            sums_copy(turn, 0).start()
        place = n + AHEAD
        if place < CHUNK:
            put_taps(taps, place * S3, here[place])
            continue
        row = rows[place - CHUNK]
        if place < CHUNK + HALO:
            if last:
                not_last = lax.axis_index("space") < lax.axis_size("space") - 1
                rim = inside(below[place - CHUNK, :STATE_CH], not_last)
                row = jnp.where(turn == count - 1, rim, row)
            put_taps(taps, place * S3, row)
        put_taps(taps, (place - CHUNK) * S3, row)
    sums_copy(turn, 1).start()

    @pl.when(turn == count - 1)
    def _():
        for part in range(count):
            for n in range(2):
                sums_copy(part, n).wait()


def state_part(first, count, state, weights, before=(), rims=()):
    last = first + count == STEPS
    extra = [*rims, *before]
    lead = 3 + len(rims)
    any_space = pl.BlockSpec(memory_space=pl.ANY)
    shapes = [
        pltpu.VMEM((ROWS, 2 * STATE_CH, COLS), F32),
        pltpu.VMEM((ROWS, STATE_CH, COLS), BF16),
    ]
    specs = [any_space, pl.BlockSpec((CHUNK, STATE_CH, COLS), lambda i: (first + i, 0, 0))]
    scratch = [
        pltpu.VMEM(((CHUNK + HALO) * S3, COLS), BF16),
        pltpu.VMEM((count, CHUNK, 2 * STATE_CH, COLS), F32),
        pltpu.SemaphoreType.DMA((count, 2)),
    ]
    if last:
        shapes.append(jax.ShapeDtypeStruct((HALO, 2 * STATE_CH, COLS), F32))
        specs.append(whole(HALO, 2 * STATE_CH, COLS))
        scratch.append(pltpu.VMEM((2 * HALO * S3, COLS), BF16))
    return pl.pallas_call(
        functools.partial(state_kernel, first, count),
        grid=(count,),
        in_specs=[
            pl.BlockSpec((STATE_CH, CHUNK, COLS), lambda i: (0, first + i, 0)),
            pl.BlockSpec((STATE_CH, CHUNK, COLS), lambda i: (0, jnp.minimum(first + i + 1, STEPS - 1), 0)),
            whole(*weights.shape),
        ]
        + [whole(HALO, EDGE_CH, COLS)] * len(rims)
        + [any_space] * len(before),
        out_specs=specs,
        out_shape=shapes,
        scratch_shapes=scratch,
        input_output_aliases={lead + n: n for n in range(len(before))},
        compiler_params=pltpu.CompilerParams(vmem_limit_bytes=20 * 2**20),
        cost_estimate=pl.CostEstimate(flops=3_000_000_000 * count, bytes_accessed=5_000_000 * count, transcendentals=0),
        name="state_part_%d" % first,
    )(state, state, weights, *extra)


LAG = 3
MAIN = 256
REST = S3 - MAIN


def side_kernel(
    context, forth, back, far, rims, others, other_far, noise, above, below, sums, by_row, rim_sums, w_side, w_reset, w_rest,
    active, offset, out, raw, sums_buf, rows_buf, rim_sums_buf, taps, rim_taps, reset_taps,
    rest_taps, update, partial, rows_done, rims_buf, context_rim, piece_sems, rim_sems, sums_sems, sems,
):
    step = pl.program_id(0)
    parts = ((0, CHUNK), (CHUNK, CHUNK), (2 * CHUNK, ROWS - 2 * CHUNK))
    member = lax.axis_index("member")
    x, core = member // 2, member % 2

    pieces = [(a, 0) for a in (context, forth, back, far)] + [(others, n * PIECE) for n in range(3)] + [(other_far, 0)]
    rim_pieces = [rims.at[0], far.at[PIECE], rims.at[1], rims.at[2]]
    rim_pieces += [other_far.at[PIECE + n] for n in (3, 0, 1, 2)]
    places = []
    for n in range(8):
        side = core if n < 4 else 1 - core
        near = 3 - 2 * side
        places.append(2 * lax.rem(x + (0, near, 4 - near, 2)[n % 4], 4) + side)

    def piece_copies(part):
        copies = []
        rows = pl.ds(*parts[part])
        for n, (piece, first) in enumerate(pieces):
            source = piece.at[pl.ds(first, PIECE), rows, :]
            target = raw.at[pl.ds(places[n] * PIECE, PIECE), rows, :]
            copies.append(pltpu.make_async_copy(source, target, piece_sems.at[part, n]))
        target = raw.at[pl.ds(CONTEXT_CH, NOISE_CH), rows, :]
        copies.append(pltpu.make_async_copy(noise.at[:, rows, :], target, piece_sems.at[part, 8]))
        return copies

    def sums_copy(n):
        slot = lax.rem(n, 2)
        rows = pl.ds(pl.multiple_of(n * CHUNK, CHUNK), CHUNK)
        return pltpu.make_async_copy(sums.at[rows], sums_buf.at[slot], sums_sems.at[slot])

    def sums_at(ref, place):
        return jnp.dot(w_side[...], ref[place * C3 : (place + 3) * C3, :], preferred_element_type=F32)

    not_first = lax.axis_index("space") > 0
    not_last = lax.axis_index("space") < lax.axis_size("space") - 1

    def gates(row_sums, state_sums, carried, slots):
        reset = logistic(row_sums[STATE_CH : 2 * STATE_CH] + state_sums[STATE_CH:])
        reset_row = (reset * carried.astype(F32)).astype(BF16)
        kept = logistic(row_sums[:STATE_CH] + state_sums[:STATE_CH])
        edge = jnp.zeros((STATE_CH, 1), BF16)
        right = jnp.concatenate([reset_row[:, 1:], edge], axis=1)
        first = slots[0] % 4 * MAIN
        reset_taps[first : first + STATE_CH] = jnp.concatenate([edge, reset_row[:, : COLS - 1]], axis=1)
        reset_taps[first + STATE_CH : first + 2 * STATE_CH] = reset_row
        reset_taps[first + 2 * STATE_CH : first + MAIN] = right[: MAIN - 2 * STATE_CH]
        for slot in slots:
            rest_taps[slot * REST : (slot + 1) * REST] = right[MAIN - 2 * STATE_CH :]
            update[slot] = kept

    def candidate_terms(slot, side_terms):
        first = slot % 4 * MAIN
        terms = jnp.dot(w_reset[...], reset_taps[first : first + MAIN, :], preferred_element_type=F32)
        partial[slot + 1] = terms[:STATE_CH]
        if slot > 0:
            partial[slot] += terms[STATE_CH : 2 * STATE_CH] + side_terms
        return terms[2 * STATE_CH :]

    @pl.when(step == 0)
    def _():
        raw[CONTEXT_CH + NOISE_CH :] = jnp.zeros((SIDE_CH - CONTEXT_CH - NOISE_CH, ROWS, COLS), BF16)
        first_half = piece_copies(0)
        for copy in first_half:
            copy.start()
        rest = [
            pltpu.make_async_copy(a, b, sems.at[n])
            for n, (a, b) in enumerate(((rim_sums, rim_sums_buf), (by_row, rows_buf)))
        ]
        rest += [
            pltpu.make_async_copy(piece, rims_buf.at[places[n]], rim_sems.at[n]) for n, piece in enumerate(rim_pieces)
        ]
        for copy in rest:
            copy.start()
        sums_copy(0).start()
        for part in (1, 2):
            for copy in piece_copies(part):
                copy.start()
        for copy in rest:
            copy.wait()
        for n in range(2 * HALO):
            first = n * RIM_CH
            joined = jnp.concatenate([rims_buf[m, first : first + PIECE].astype(F32) for m in range(8)], axis=0)
            context_rim[n] = inside(joined, not_first if n < HALO else not_last).astype(BF16)
        for copy in first_half:
            copy.wait()
        chunk = jnp.transpose(raw[:, :CHUNK, :], (1, 0, 2))[:AHEAD]
        for n in range(HALO):
            noise_rim = inside(above[n, STATE_CH : STATE_CH + 16], not_first)
            put_taps(rim_taps, n * C3, jnp.concatenate([context_rim[n], noise_rim], axis=0))
            put_taps(rim_taps, (HALO + n) * C3, chunk[n])
        for n in range(AHEAD):
            put_taps(taps, n * C3, chunk[n])
        for copy in piece_copies(1):
            copy.wait()
        gates(sums_at(rim_taps, 0), rim_sums_buf[0], inside(above[1, :STATE_CH], not_first), (0,))
        candidate_terms(0, None)
        row_sums = sums_at(rim_taps, 1)
        gates(row_sums, rim_sums_buf[1], rows_buf[0], (1,))
        candidate_terms(1, row_sums[2 * STATE_CH :])

    @pl.when(step == 1)
    def _():
        for copy in piece_copies(2):
            copy.wait()

    @pl.when(step + 1 < STEPS)
    def _():
        sums_copy(step + 1).start()

    sums_copy(step).wait()
    state_sums = sums_buf.at[lax.rem(step, 2)]
    here = pl.multiple_of(step * CHUNK, CHUNK)
    owner = lax.axis_index("space")
    tile = lax.broadcasted_iota(jnp.int32, (1, COLS), 1) // TILE
    chosen = jnp.zeros((1, COLS), jnp.bool_)
    for n in range(COLS // TILE):
        used = (active[n, owner] == 1) & (offset[n, owner] < REACH)
        chosen = chosen | ((tile == n) & used)
    later = pl.multiple_of(jnp.minimum(step + 1, STEPS - 1) * CHUNK, CHUNK)
    chunk = jnp.transpose(raw[:, pl.ds(here, CHUNK), :], (1, 0, 2))
    following = jnp.transpose(raw[:, pl.ds(later, CHUNK), :], (1, 0, 2))

    def candidate(n, side_terms):
        slot = n + 1
        terms = candidate_terms(slot + 1, side_terms)
        rest = jnp.dot(w_rest[...], rest_taps[n * REST : (n + 3) * REST, :], preferred_element_type=F32)
        proposal = jnp.tanh(partial[slot] + terms + rest)
        old = rows_buf[here + n].astype(F32)
        new = (1.0 - update[slot]) * old + update[slot] * proposal
        rows_done[n] = jnp.where(chosen, new, old).astype(BF16)

    waiting = []
    for n in range(CHUNK):
        row_sums = sums_at(taps, n)
        carried = rows_buf[jnp.minimum(here + n + 1, ROWS - 1)]
        if n == CHUNK - 1:
            carried = jnp.where(step == STEPS - 1, inside(below[0, :STATE_CH], not_last), carried)
        if len(waiting) == LAG:
            candidate(n - LAG, waiting.pop(0))
        gates(row_sums, state_sums[n], carried, (n + 2,) if n < CHUNK - HALO else (n + 2, n + 2 - CHUNK))
        waiting.append(row_sums[2 * STATE_CH :])
        place = n + AHEAD
        if place < CHUNK:
            put_taps(taps, place * C3, chunk[place])
            continue
        row = following[place - CHUNK]
        if place < CHUNK + HALO:
            noise_rim = inside(below[place - CHUNK, STATE_CH : STATE_CH + 16], not_last)
            rim = jnp.concatenate([context_rim[HALO + place - CHUNK], noise_rim], axis=0)
            row = jnp.where(step == STEPS - 1, rim, row)
            put_taps(taps, place * C3, row)
        put_taps(taps, (place - CHUNK) * C3, row)
    for n in range(CHUNK - LAG, CHUNK):
        candidate(n, waiting.pop(0))
    for n in range(1, 3):
        partial[n] = partial[CHUNK + n]
    out[...] = jnp.transpose(rows_done[...], (1, 0, 2))


def whole(*shape):
    return pl.BlockSpec(shape, lambda i: (0,) * len(shape))


def side_part(pieces, noise, above, below, sums, by_row, rim_sums, weights, active, offset):
    smem = pl.BlockSpec(memory_space=pltpu.SMEM)
    any_space = pl.BlockSpec(memory_space=pl.ANY)
    return pl.pallas_call(
        side_kernel,
        grid=(STEPS,),
        in_specs=[any_space] * (len(pieces) + 1)
        + [whole(HALO, EDGE_CH, COLS)] * 2
        + [any_space] * 3
        + [whole(*a.shape) for a in weights]
        + [smem, smem],
        out_specs=pl.BlockSpec((STATE_CH, CHUNK, COLS), lambda i: (0, i, 0)),
        out_shape=jax.ShapeDtypeStruct((STATE_CH, ROWS, COLS), BF16),
        scratch_shapes=[
            pltpu.VMEM((SIDE_CH, ROWS, COLS), BF16),
            pltpu.VMEM((2, CHUNK, 2 * STATE_CH, COLS), F32),
            pltpu.VMEM((ROWS, STATE_CH, COLS), BF16),
            pltpu.VMEM((HALO, 2 * STATE_CH, COLS), F32),
            pltpu.VMEM(((CHUNK + HALO) * C3, COLS), BF16),
            pltpu.VMEM((2 * HALO * C3, COLS), BF16),
            pltpu.VMEM((4 * MAIN, COLS), BF16),
            pltpu.VMEM(((CHUNK + HALO) * REST, COLS), BF16),
            pltpu.VMEM((CHUNK + HALO, STATE_CH, COLS), F32),
            pltpu.VMEM((CHUNK + HALO + 1, STATE_CH, COLS), F32),
            pltpu.VMEM((CHUNK, STATE_CH, COLS), BF16),
            pltpu.VMEM((8, 2 * HALO * RIM_CH, COLS), BF16),
            pltpu.VMEM((2 * HALO, CONTEXT_CH, COLS), BF16),
            pltpu.SemaphoreType.DMA((3, 9)),
            pltpu.SemaphoreType.DMA((8,)),
            pltpu.SemaphoreType.DMA((2,)),
            pltpu.SemaphoreType.DMA((2,)),
        ],
        compiler_params=pltpu.CompilerParams(vmem_limit_bytes=30 * 2**20),
        cost_estimate=pl.CostEstimate(flops=17_000_000_000, bytes_accessed=20_000_000, transcendentals=0),
        name="side_part",
    )(
        *pieces, noise, above, below, *[pltpu.with_memory_space_constraint(a, pltpu.VMEM) for a in (sums, by_row)],
        rim_sums, *weights, active, offset,
    )


def by_tap(kernel):
    return jnp.transpose(kernel, (2, 3, 0, 1)).reshape((9,) + kernel.shape[:2])


def along_x(by):
    return [(2 * x + core, 2 * ((x + by) % 4) + core) for x in range(4) for core in range(2)]


FORTH = [(2 * x + core, 2 * ((x + 1 - 2 * core) % 4) + core) for x in range(4) for core in range(2)]
BACK = [(b, a) for a, b in FORTH]
CORES = [(n, n ^ 1) for n in range(8)]


def shards(state_field, context_field, noise_latent, gate_kernel, candidate_kernel, active_tiles, tile_offset):
    owners = lax.axis_size("space")
    state = state_field[0]
    noise = noise_latent[0, 0]

    def to_core(a):
        return lax.ppermute(a, "member", CORES)

    forth = lax.ppermute(context_field, "member", FORTH)
    back = lax.ppermute(context_field, "member", BACK)
    top, low = edges(state, noise, context_field)
    above = lax.ppermute(low, "space", [(n, (n + 1) % owners) for n in range(owners)])
    below = lax.ppermute(top, "space", [((n + 1) % owners, n) for n in range(owners)])
    gate_kernel, candidate_kernel = by_tap(gate_kernel), by_tap(candidate_kernel)
    state, top = lax.optimization_barrier((state, top))
    (state_weights,) = laid_out(state_weights_kernel, "state_weights", [(2 * STATE_CH, 3 * S3)], gate_kernel)
    before = state_part(0, 2, state, state_weights)

    before, forth, back, above, below = lax.optimization_barrier((before, forth, back, above, below))
    side = slice(STATE_CH + 16, STATE_CH + 16 + RIM_CH)
    rim = jnp.concatenate([above[:, side], below[:, side]], axis=0).reshape(1, 2 * HALO * RIM_CH, COLS)
    far = lax.ppermute(jnp.concatenate([forth, rim], axis=0), "member", FORTH)
    rims = [rim, lax.ppermute(rim, "member", BACK), lax.ppermute(rim, "member", along_x(2))]
    others = to_core(jnp.concatenate([context_field, forth, back], axis=0))
    sums, by_row, rim_sums = state_part(2, 2, state, state_weights, before, (above, below, top))

    sums, rims, far = lax.optimization_barrier((sums, rims, far))
    rims = jnp.concatenate(rims, axis=0)
    other_far = to_core(jnp.concatenate([far, rims[1:], rims[:1]], axis=0))
    sums, gate_kernel, candidate_kernel = lax.optimization_barrier((sums, gate_kernel, candidate_kernel))
    shapes = [(3 * STATE_CH, 3 * C3), (3 * STATE_CH, MAIN), (STATE_CH, 3 * REST)]
    side_weights = laid_out(side_weights_kernel, "side_weights", shapes, gate_kernel, candidate_kernel)
    pieces = [context_field, forth, back, far, rims, others, other_far]
    result = side_part(
        pieces, noise, above, below, sums, by_row, rim_sums, side_weights, active_tiles.T, tile_offset.T
    )
    return result[None]


def solution(mesh):
    return jax.shard_map(
        shards,
        mesh=mesh,
        in_specs=(
            P("member", None, "space", None),
            P("member", "space", None),
            P("member", None, None, "space", None),
            P(),
            P(),
            P(),
            P(),
        ),
        out_specs=P("member", None, "space", None),
        check_vma=False,
    )
```

time: 64.2 us -> 56.9 us (0.89)
  Pallas kernels: 43.3 us -> 35.6 us
    pallas_call x2, Pallas kernels: 17.3 us -> 11.2 us  [state_part(): pl.pallas_call(functools.partial(state_kernel, first, count), grid=(count...]
    ppermute x1, starting transfers between devices: 0.01 us -> 2.04 us  [shards(): back = lax.ppermute(context_field, 'member', BACK)]
    ppermute x1, starting transfers between devices: 3.31 us -> 1.27 us  [shards(): forth = lax.ppermute(context_field, 'member', FORTH)]
    pallas_call x2 -> x4, Pallas kernels: 26 us -> 24.4 us  [the longest x1 22.1 us: side_part(): pl.pallas_call(side_kernel, grid=(STEPS,), in_specs=[any_space] * (len(pi...]
    ppermute x5 -> x2, waiting for transfers between devices: 1.64 us -> 1.09 us  [to_core(): return lax.ppermute(a, 'member', CORES)]
    ppermute x5 -> x2, starting transfers between devices: 3.72 us -> 3.9 us  [to_core(): return lax.ppermute(a, 'member', CORES)]
    ppermute x4 -> x3, starting transfers between devices: 4.53 us -> 4.35 us  [the longest x1 2.43 us: shards(): far = lax.ppermute(jnp.concatenate([forth, rim], axis=0), 'member', FORTH)]
  transfers between devices with their start and end apart: 13 -> 9, of which waited for: 3 -> 1; matrix products, arithmetic and copies ran while one was open for 0% -> 0% of each run, Pallas kernels for 31% -> 24%
where the time goes in v3:
time: 56.9 us; the launch traced here: 56.7 us
  Pallas kernels  35.6 us (63%)
  starting transfers between devices  18.1 us (32%)
  local copies, waits for them, and re-layouts  1.21 us (2%)
  waiting for transfers between devices  1.11 us (2%)
    pallas_call x1, Pallas kernels, side_part(): pl.pallas_call(side_kernel, grid=(STEPS,), in_specs=[any_space] * (len(pi...  22.1 us
    pallas_call x2, Pallas kernels, state_part(): pl.pallas_call(functools.partial(state_kernel, first, count), grid=(count...  11.2 us
    ppermute x1, starting transfers between devices, shards(): lax.ppermute(top, 'space', [((n + 1) % owners, n) for n in range(owners)])  4.65 us
    ppermute x2, starting transfers between devices, to_core(): return lax.ppermute(a, 'member', CORES)  3.9 us
    ppermute x1, starting transfers between devices, shards(): far = lax.ppermute(jnp.concatenate([forth, rim], axis=0), 'member', FORTH)  2.43 us
    ppermute x1, starting transfers between devices, shards(): back = lax.ppermute(context_field, 'member', BACK)  2.04 us
    ppermute x1, starting transfers between devices, shards(): lax.ppermute(low, 'space', [(n, (n + 1) % owners) for n in range(owners)])  1.9 us
    pallas_call x1, Pallas kernels, edges(): pl.pallas_call(edge_kernel, in_specs=[pl.BlockSpec(memory_space=pltpu.HBM...  1.78 us
  transfers between devices with their start and end apart: 9, of which 1 were waited for; matrix products, arithmetic and copies ran while one was open for 0% of the time, Pallas kernels for 24%

profile of v3, /device:TPU:1, one launch (start us, length us, event | category | flops | bytes accessed | tf_op | source)
XLA Modules:
  0.0 56.7 jit_solution(12005525978381344902)
XLA Ops:
  0.0 2.0 %collective-permute-start.1 = (bf16[12,64,256]{2,1,0:T(8,128)(2,1)}, bf16[12,64,256]{2,1,0:T(8,128)(2,1)S(1)}, u32[]{:S(2)}, u32[]{:S(2)}) collective-permute-start(bf16[12,64,256]{2,1,0:T(8,128)(2,1)} %context.3), channel_id=1, source_target_pairs={{2,0},{7,1},{4,2},{1,3},{6,4},{3,5},{0,6},{5,7},{10,8},{15,9},{12,... | collective-permute-start | bytes 1179656 | tf_op jit(solution)/shard_map/ppermute | solution.py:454
  2.0 1.3 %collective-permute-start = (bf16[12,64,256]{2,1,0:T(8,128)(2,1)}, bf16[12,64,256]{2,1,0:T(8,128)(2,1)S(1)}, u32[]{:S(2)}, u32[]{:S(2)}) collective-permute-start(bf16[12,64,256]{2,1,0:T(8,128)(2,1)} %context.3), channel_id=1, source_target_pairs={{0,2},{1,7},{2,4},{3,1},{4,6},{5,3},{6,0},{7,5},{8,10},{9,15},{10,... | collective-permute-start | bytes 1179656 | tf_op jit(solution)/shard_map/ppermute | solution.py:453
  3.3 1.8 %edges.1 = (bf16[2,128,256]{2,1,0:T(8,128)(2,1)S(1)}, bf16[2,128,256]{2,1,0:T(8,128)(2,1)S(1)}) custom-call(bf16[96,64,256]{2,1,0:T(8,128)(2,1)} %bitcast.12, bf16[8,64,256]{2,1,0:T(8,128)(2,1)} %bitcast.20, bf16[12,64,256]{2,1,0:T(8,128)(2,1)} %context.3), custom_call_target="tpu_custom_call" | custom-call | bytes 4000000 | tf_op jit(solution)/shard_map/edges/pallas_call | solution.py:68
  5.1 1.9 %collective-permute-start.2 = (bf16[2,128,256]{2,1,0:T(8,128)(2,1)S(1)}, bf16[2,128,256]{2,1,0:T(8,128)(2,1)S(1)}, u32[]{:S(2)}, u32[]{:S(2)}) collective-permute-start(bf16[2,128,256]{2,1,0:T(8,128)(2,1)S(1)} %get-tuple-element.35), channel_id=1, source_target_pairs={{0,8},{8,16},{16,24},{24,32},{32,40},{40,48},{48,56},{56,64},{64,7... | collective-permute-start | bytes 393224 | tf_op jit(solution)/shard_map/ppermute | solution.py:456
  7.0 4.7 %collective-permute-start.3 = (bf16[2,128,256]{2,1,0:T(8,128)(2,1)S(1)}, bf16[2,128,256]{2,1,0:T(8,128)(2,1)S(1)}, u32[]{:S(2)}, u32[]{:S(2)}) collective-permute-start(bf16[2,128,256]{2,1,0:T(8,128)(2,1)S(1)} %get-tuple-element.40.refs_5_), channel_id=1, source_target_pairs={{8,0},{16,8},{24,16},{32,24},{40,32},{48,40},{56,48},{64,56},{72,6... | collective-permute-start | bytes 393224 | tf_op jit(solution)/shard_map/ppermute | solution.py:457
  11.7 1.2 %copy-done.1 = bf16[192,200,3,3]{1,0,3,2:T(8,128)(2,1)S(1)} copy-done((bf16[192,200,3,3]{1,0,3,2:T(8,128)(2,1)S(1)}, bf16[192,200,3,3]{1,0,3,2:T(8,128)(2,1)}, u32[]{:S(2)}) %copy-start.1) | copy-done | bytes 691224
  12.8 0.1 state_weights.1.refs_2_
  13.0 5.5 %state_part_0.1 = (f32[64,192,256]{2,1,0:T(8,128)S(1)}, bf16[64,96,256]{2,1,0:T(8,128)(2,1)S(1)}) custom-call(bf16[96,64,256]{2,1,0:T(8,128)(2,1)S(1)} %bitcast.13, bf16[96,64,256]{2,1,0:T(8,128)(2,1)S(1)} %bitcast.14, bf16[192,864]{1,0:T(8,128)(2,1)S(1)} %state_weights.1.refs_2_), custom_call_target="tpu_custom_call" | custom-call | flops 6000000000 | bytes 10000000 | tf_op jit(solution)/shard_map/state_part_0/pallas_call | solution.py:198
  18.5 0.0 copy-start.3
  18.5 0.0 collective-permute-done.2.refs_3_.above
  18.5 0.0 collective-permute-done.3.refs_4_.below
  18.5 0.0 collective-permute-done.1.back
  18.6 0.0 collective-permute-done.forth
  18.6 1.6 %collective-permute-start.5 = (bf16[1,64,256]{2,1,0:T(8,128)(2,1)S(1)}, bf16[1,64,256]{2,1,0:T(8,128)(2,1)S(1)}, u32[]{:S(2)}, u32[]{:S(2)}) collective-permute-start(bf16[1,64,256]{2,1,0:T(8,128)(2,1)S(1)} %bitcast.24), channel_id=1, source_target_pairs={{0,4},{1,5},{2,6},{3,7},{4,0},{5,1},{6,2},{7,3},{8,12},{9,13},{10,... | collective-permute-start | bytes 98312 | tf_op jit(solution)/shard_map/ppermute | solution.py:467
  20.2 0.3 collective-permute-start.4
  20.6 2.4 %collective-permute-start.6 = (bf16[13,64,256]{2,1,0:T(8,128)(2,1)S(1)}, bf16[13,64,256]{2,1,0:T(8,128)(2,1)S(1)}, u32[]{:S(2)}, u32[]{:S(2)}) collective-permute-start(bf16[13,64,256]{2,1,0:T(8,128)(2,1)S(1)} %pad_maximum_fusion.2), channel_id=1, source_target_pairs={{0,2},{1,7},{2,4},{3,1},{4,6},{5,3},{6,0},{7,5},{8,10},{9,15},{10,... | collective-permute-start | bytes 1277960 | tf_op jit(solution)/shard_map/ppermute | solution.py:466
  23.0 0.1 pad_maximum_fusion
  23.1 1.2 %collective-permute-start.7 = (bf16[36,64,256]{2,1,0:T(8,128)(2,1)S(1)}, bf16[36,64,256]{2,1,0:T(8,128)(2,1)S(1)}, u32[]{:S(2)}, u32[]{:S(2)}) collective-permute-start(bf16[36,64,256]{2,1,0:T(8,128)(2,1)S(1)} %pad_maximum_fusion), channel_id=1, source_target_pairs={{0,1},{1,0},{2,3},{3,2},{4,5},{5,4},{6,7},{7,6},{8,9},{9,8},{10,11... | collective-permute-start | bytes 3538952 | tf_op jit(solution)/shard_map/ppermute | solution.py:451
  24.4 5.7 %state_part_2.1 = (f32[64,192,256]{2,1,0:T(8,128)S(1)}, bf16[64,96,256]{2,1,0:T(8,128)(2,1)S(1)}, f32[2,192,256]{2,1,0:T(8,128)S(1)}) custom-call(bf16[96,64,256]{2,1,0:T(8,128)(2,1)S(1)} %bitcast.15, bf16[96,64,256]{2,1,0:T(8,128)(2,1)S(1)} %bitcast.16, bf16[192,864]{1,0:T(8,128)(2,1)S(1)} %state_weights.1.refs_2_, ...), custom_call_target="tpu_custom_call", output_to_operand_aliasing={{0}: (6, {}), {1}: (7, {})} | custom-call | flops 6000000000 | bytes 10000000 | tf_op jit(solution)/shard_map/state_part_2/pallas_call | solution.py:198
  30.1 0.0 copy-start.2
  30.1 0.0 collective-permute-done.5
  30.1 0.0 collective-permute-done.4
  30.1 0.0 collective-permute-done.6.far
  30.1 0.0 copy-start.5
  30.2 0.0 copy-start.6
  30.2 0.0 copy-start.7
  30.2 0.1 pad_maximum_fusion.1
  30.3 2.7 %collective-permute-start.8 = (bf16[16,64,256]{2,1,0:T(8,128)(2,1)S(1)}, bf16[16,64,256]{2,1,0:T(8,128)(2,1)S(1)}, u32[]{:S(2)}, u32[]{:S(2)}) collective-permute-start(bf16[16,64,256]{2,1,0:T(8,128)(2,1)S(1)} %pad_maximum_fusion.1), channel_id=1, source_target_pairs={{0,1},{1,0},{2,3},{3,2},{4,5},{5,4},{6,7},{7,6},{8,9},{9,8},{10,11... | collective-permute-start | bytes 1572872 | tf_op jit(solution)/shard_map/ppermute | solution.py:451
  33.0 0.4 side_weights.1
  33.4 1.1 %collective-permute-done.8.other_far = bf16[16,64,256]{2,1,0:T(8,128)(2,1)S(1)} collective-permute-done((bf16[16,64,256]{2,1,0:T(8,128)(2,1)S(1)}, bf16[16,64,256]{2,1,0:T(8,128)(2,1)S(1)}, u32[]{:S(2)}, u32[]{:S(2)}) %collective-permute-start.8) | collective-permute-done | bytes 524320 | tf_op jit(solution)/shard_map/ppermute | solution.py:451
  34.5 0.0 collective-permute-done.7.others
  34.5 22.1 %side_part.1 = bf16[96,64,256]{2,1,0:T(8,128)(2,1)} custom-call(bf16[12,64,256]{2,1,0:T(8,128)(2,1)S(1)} %copy-done.3, bf16[12,64,256]{2,1,0:T(8,128)(2,1)S(1)} %collective-permute-done.forth, bf16[12,64,256]{2,1,0:T(8,128)(2,1)S(1)} %collective-permute-done.1.back, bf16[13,64,256]{2,1,0:T(8,128)(2,1)S(1)} %collective-permute-done.6.far, ...), custom_call_target="tpu_custom_call" | custom-call | flops 16999999488 | bytes 20000000 | tf_op jit(solution)/shard_map/side_part/pallas_call | solution.py:394
  (15 shorter events, 0.1 us)
Async XLA Ops:
  0.0 18.5 %collective-permute-start.1 = (bf16[12,64,256]{2,1,0:T(8,128)(2,1)}, bf16[12,64,256]{2,1,0:T(8,128)(2,1)S(1)}, u32[]{:S(2)}, u32[]{:S(2)}) collective-permute-start(bf16[12,64,256]{2,1,0:T(8,128)(2,1)} %context.3), channel_id=1, source_target_pairs={{2,0},{7,1},{4,2},{1,3},{6,4},{3,5},{0,6},{5,7},{10,8},{15,9},{12,... | collective-permute-start | bytes 1179656 | tf_op jit(solution)/shard_map/ppermute | solution.py:454
  2.0 16.5 %collective-permute-start = (bf16[12,64,256]{2,1,0:T(8,128)(2,1)}, bf16[12,64,256]{2,1,0:T(8,128)(2,1)S(1)}, u32[]{:S(2)}, u32[]{:S(2)}) collective-permute-start(bf16[12,64,256]{2,1,0:T(8,128)(2,1)} %context.3), channel_id=1, source_target_pairs={{0,2},{1,7},{2,4},{3,1},{4,6},{5,3},{6,0},{7,5},{8,10},{9,15},{10,... | collective-permute-start | bytes 1179656 | tf_op jit(solution)/shard_map/ppermute | solution.py:453
  3.3 9.7 %copy-start = (bf16[1,96,64,256]{3,2,1,0:T(8,128)(2,1)S(1)}, bf16[1,96,64,256]{3,2,1,0:T(8,128)(2,1)}, u32[]{:S(2)}) copy-start(bf16[1,96,64,256]{3,2,1,0:T(8,128)(2,1)} %param.7) | copy-start | bytes 9437188
  5.1 13.4 %collective-permute-start.2 = (bf16[2,128,256]{2,1,0:T(8,128)(2,1)S(1)}, bf16[2,128,256]{2,1,0:T(8,128)(2,1)S(1)}, u32[]{:S(2)}, u32[]{:S(2)}) collective-permute-start(bf16[2,128,256]{2,1,0:T(8,128)(2,1)S(1)} %get-tuple-element.35), channel_id=1, source_target_pairs={{0,8},{8,16},{16,24},{24,32},{32,40},{40,48},{48,56},{56,64},{64,7... | collective-permute-start | bytes 393224 | tf_op jit(solution)/shard_map/ppermute | solution.py:456
  7.0 11.5 %collective-permute-start.3 = (bf16[2,128,256]{2,1,0:T(8,128)(2,1)S(1)}, bf16[2,128,256]{2,1,0:T(8,128)(2,1)S(1)}, u32[]{:S(2)}, u32[]{:S(2)}) collective-permute-start(bf16[2,128,256]{2,1,0:T(8,128)(2,1)S(1)} %get-tuple-element.40.refs_5_), channel_id=1, source_target_pairs={{8,0},{16,8},{24,16},{32,24},{40,32},{48,40},{56,48},{64,56},{72,6... | collective-permute-start | bytes 393224 | tf_op jit(solution)/shard_map/ppermute | solution.py:457
  11.7 1.2 %copy-start.1 = (bf16[192,200,3,3]{1,0,3,2:T(8,128)(2,1)S(1)}, bf16[192,200,3,3]{1,0,3,2:T(8,128)(2,1)}, u32[]{:S(2)}) copy-start(bf16[192,200,3,3]{1,0,3,2:T(8,128)(2,1)} %param.10) | copy-start | bytes 2073604
  18.5 4.5 %copy-start.3 = (bf16[12,64,256]{2,1,0:T(8,128)(2,1)S(1)}, bf16[12,64,256]{2,1,0:T(8,128)(2,1)}, u32[]{:S(2)}) copy-start(bf16[12,64,256]{2,1,0:T(8,128)(2,1)} %context.3) | copy-start | bytes 1179652
  18.6 11.5 %collective-permute-start.5 = (bf16[1,64,256]{2,1,0:T(8,128)(2,1)S(1)}, bf16[1,64,256]{2,1,0:T(8,128)(2,1)S(1)}, u32[]{:S(2)}, u32[]{:S(2)}) collective-permute-start(bf16[1,64,256]{2,1,0:T(8,128)(2,1)S(1)} %bitcast.24), channel_id=1, source_target_pairs={{0,4},{1,5},{2,6},{3,7},{4,0},{5,1},{6,2},{7,3},{8,12},{9,13},{10,... | collective-permute-start | bytes 98312 | tf_op jit(solution)/shard_map/ppermute | solution.py:467
  20.2 9.9 %collective-permute-start.4 = (bf16[1,64,256]{2,1,0:T(8,128)(2,1)S(1)}, bf16[1,64,256]{2,1,0:T(8,128)(2,1)S(1)}, u32[]{:S(2)}, u32[]{:S(2)}) collective-permute-start(bf16[1,64,256]{2,1,0:T(8,128)(2,1)S(1)} %bitcast.25), channel_id=1, source_target_pairs={{2,0},{7,1},{4,2},{1,3},{6,4},{3,5},{0,6},{5,7},{10,8},{15,9},{12,... | collective-permute-start | bytes 98312 | tf_op jit(solution)/shard_map/ppermute | solution.py:467
  20.6 9.6 %collective-permute-start.6 = (bf16[13,64,256]{2,1,0:T(8,128)(2,1)S(1)}, bf16[13,64,256]{2,1,0:T(8,128)(2,1)S(1)}, u32[]{:S(2)}, u32[]{:S(2)}) collective-permute-start(bf16[13,64,256]{2,1,0:T(8,128)(2,1)S(1)} %pad_maximum_fusion.2), channel_id=1, source_target_pairs={{0,2},{1,7},{2,4},{3,1},{4,6},{5,3},{6,0},{7,5},{8,10},{9,15},{10,... | collective-permute-start | bytes 1277960 | tf_op jit(solution)/shard_map/ppermute | solution.py:466
  23.1 11.4 %collective-permute-start.7 = (bf16[36,64,256]{2,1,0:T(8,128)(2,1)S(1)}, bf16[36,64,256]{2,1,0:T(8,128)(2,1)S(1)}, u32[]{:S(2)}, u32[]{:S(2)}) collective-permute-start(bf16[36,64,256]{2,1,0:T(8,128)(2,1)S(1)} %pad_maximum_fusion), channel_id=1, source_target_pairs={{0,1},{1,0},{2,3},{3,2},{4,5},{5,4},{6,7},{7,6},{8,9},{9,8},{10,11... | collective-permute-start | bytes 3538952 | tf_op jit(solution)/shard_map/ppermute | solution.py:451
  24.4 8.6 %copy-start.4 = (bf16[96,200,3,3]{1,0,3,2:T(8,128)(2,1)S(1)}, bf16[96,200,3,3]{1,0,3,2:T(8,128)(2,1)}, u32[]{:S(2)}) copy-start(bf16[96,200,3,3]{1,0,3,2:T(8,128)(2,1)} %param.11) | copy-start | bytes 1036804
  30.1 2.9 %copy-start.2 = (bf16[192,200,3,3]{1,0,3,2:T(8,128)(2,1)S(1)}, bf16[192,200,3,3]{1,0,3,2:T(8,128)(2,1)}, u32[]{:S(2)}) copy-start(bf16[192,200,3,3]{1,0,3,2:T(8,128)(2,1)} %param.10) | copy-start | bytes 2073604
  30.1 4.4 %copy-start.5 = (bf16[1,1,8,64,256]{4,3,2,1,0:T(8,128)(2,1)S(1)}, bf16[1,1,8,64,256]{4,3,2,1,0:T(8,128)(2,1)}, u32[]{:S(2)}) copy-start(bf16[1,1,8,64,256]{4,3,2,1,0:T(8,128)(2,1)} %param.9) | copy-start | bytes 786436
  30.2 4.3 %copy-start.6 = (s32[16,4]{0,1:T(4,128)S(1)}, s32[16,4]{0,1:T(4,128)}, u32[]{:S(2)}) copy-start(s32[16,4]{0,1:T(4,128)} %param.12) | copy-start | bytes 772
  30.2 4.3 %copy-start.7 = (s32[16,4]{0,1:T(4,128)S(1)}, s32[16,4]{0,1:T(4,128)}, u32[]{:S(2)}) copy-start(s32[16,4]{0,1:T(4,128)} %param.13) | copy-start | bytes 772
  30.3 4.2 %collective-permute-start.8 = (bf16[16,64,256]{2,1,0:T(8,128)(2,1)S(1)}, bf16[16,64,256]{2,1,0:T(8,128)(2,1)S(1)}, u32[]{:S(2)}, u32[]{:S(2)}) collective-permute-start(bf16[16,64,256]{2,1,0:T(8,128)(2,1)S(1)} %pad_maximum_fusion.1), channel_id=1, source_target_pairs={{0,1},{1,0},{2,3},{3,2},{4,5},{5,4},{6,7},{7,6},{8,9},{9,8},{10,11... | collective-permute-start | bytes 1572872 | tf_op jit(solution)/shard_map/ppermute | solution.py:451

commit v4 on v3

--- a/solution.py
+++ b/solution.py
@@ -38,8 +38,8 @@
     ref[pl.ds(first + 2 * count, count), :] = jnp.concatenate([row[:, 1:], edge], axis=1)
 
 
-def logistic(x):
-    return 0.5 * jnp.tanh(0.5 * x) + 0.5
+def logistic_of_double(x):
+    return 0.5 * jnp.tanh(x) + 0.5
 
 
 def edge_kernel(state, noise, context, top, low, state_buf, noise_buf, context_buf, sems):
@@ -87,12 +87,12 @@
 
 
 def state_weights_kernel(gate, weights):
-    weights[...] = joined_taps(gate, 0, STATE_CH, STATE_CH)
+    weights[...] = joined_taps(gate, 0, STATE_CH, STATE_CH) * BF16(0.5)
 
 
 def side_weights_kernel(gate, candidate, w_side, w_reset, w_rest):
     channels = CONTEXT_CH + NOISE_CH
-    w_side[: 2 * STATE_CH] = joined_taps(gate, STATE_CH, channels, SIDE_CH)
+    w_side[: 2 * STATE_CH] = joined_taps(gate, STATE_CH, channels, SIDE_CH) * BF16(0.5)
     w_side[2 * STATE_CH :] = joined_taps(candidate, STATE_CH, channels, SIDE_CH)
     for a in range(3):
         left, middle, right = (candidate[3 * a + n, :, :STATE_CH] for n in range(3))
@@ -121,16 +121,10 @@
     last = first + count == STEPS
     if last:
         above, below, top = refs[3:6]
-        sums, by_row, rim_sums, taps, sums_buf, sems, rim_taps = refs[8:]
+        sums, by_row, rim_sums, taps, rim_taps = refs[8:]
     else:
-        sums, by_row, taps, sums_buf, sems = refs[5 if first else 3 :]
+        sums, by_row, taps = refs[5 if first else 3 :]
     turn = pl.program_id(0)
-    half = CHUNK // 2
-
-    def sums_copy(part, n):
-        start = pl.multiple_of((first + part) * CHUNK + n * half, half)
-        source = sums_buf.at[part, pl.ds(n * half, half)]
-        return pltpu.make_async_copy(source, sums.at[pl.ds(start, half)], sems.at[part, n])
 
     def sums_at(ref, place):
         return jnp.dot(weights[...], ref[place * S3 : (place + 3) * S3, :], preferred_element_type=F32)
@@ -152,9 +146,7 @@
 
     rows = jnp.transpose(following[...], (1, 0, 2))
     for n in range(CHUNK):
-        sums_buf[turn, n] = sums_at(taps, n)
-        if n == half - 1:
-            sums_copy(turn, 0).start()
+        sums[n] = sums_at(taps, n)
         place = n + AHEAD
         if place < CHUNK:
             put_taps(taps, place * S3, here[place])
@@ -167,13 +159,6 @@
                 row = jnp.where(turn == count - 1, rim, row)
             put_taps(taps, place * S3, row)
         put_taps(taps, (place - CHUNK) * S3, row)
-    sums_copy(turn, 1).start()
-
-    @pl.when(turn == count - 1)
-    def _():
-        for part in range(count):
-            for n in range(2):
-                sums_copy(part, n).wait()
 
 
 def state_part(first, count, state, weights, before=(), rims=()):
@@ -185,11 +170,9 @@
         pltpu.VMEM((ROWS, 2 * STATE_CH, COLS), F32),
         pltpu.VMEM((ROWS, STATE_CH, COLS), BF16),
     ]
-    specs = [any_space, pl.BlockSpec((CHUNK, STATE_CH, COLS), lambda i: (first + i, 0, 0))]
+    specs = [pl.BlockSpec((CHUNK, channels, COLS), lambda i: (first + i, 0, 0)) for channels in (2 * STATE_CH, STATE_CH)]
     scratch = [
         pltpu.VMEM(((CHUNK + HALO) * S3, COLS), BF16),
-        pltpu.VMEM((count, CHUNK, 2 * STATE_CH, COLS), F32),
-        pltpu.SemaphoreType.DMA((count, 2)),
     ]
     if last:
         shapes.append(jax.ShapeDtypeStruct((HALO, 2 * STATE_CH, COLS), F32))
@@ -222,8 +205,8 @@
 
 def side_kernel(
     context, forth, back, far, rims, others, other_far, noise, above, below, sums, by_row, rim_sums, w_side, w_reset, w_rest,
-    active, offset, out, raw, sums_buf, rows_buf, rim_sums_buf, taps, rim_taps, reset_taps,
-    rest_taps, update, partial, rows_done, rims_buf, context_rim, piece_sems, rim_sems, sums_sems, sems,
+    active, offset, out, raw, taps, rim_taps, reset_taps,
+    rest_taps, update, partial, rows_done, rims_buf, context_rim, piece_sems, rim_sems,
 ):
     step = pl.program_id(0)
     parts = ((0, CHUNK), (CHUNK, CHUNK), (2 * CHUNK, ROWS - 2 * CHUNK))
@@ -250,11 +233,6 @@
         copies.append(pltpu.make_async_copy(noise.at[:, rows, :], target, piece_sems.at[part, 8]))
         return copies
 
-    def sums_copy(n):
-        slot = lax.rem(n, 2)
-        rows = pl.ds(pl.multiple_of(n * CHUNK, CHUNK), CHUNK)
-        return pltpu.make_async_copy(sums.at[rows], sums_buf.at[slot], sums_sems.at[slot])
-
     def sums_at(ref, place):
         return jnp.dot(w_side[...], ref[place * C3 : (place + 3) * C3, :], preferred_element_type=F32)
 
@@ -262,9 +240,9 @@
     not_last = lax.axis_index("space") < lax.axis_size("space") - 1
 
     def gates(row_sums, state_sums, carried, slots):
-        reset = logistic(row_sums[STATE_CH : 2 * STATE_CH] + state_sums[STATE_CH:])
+        reset = logistic_of_double(row_sums[STATE_CH : 2 * STATE_CH] + state_sums[STATE_CH:])
         reset_row = (reset * carried.astype(F32)).astype(BF16)
-        kept = logistic(row_sums[:STATE_CH] + state_sums[:STATE_CH])
+        kept = logistic_of_double(row_sums[:STATE_CH] + state_sums[:STATE_CH])
         edge = jnp.zeros((STATE_CH, 1), BF16)
         right = jnp.concatenate([reset_row[:, 1:], edge], axis=1)
         first = slots[0] % 4 * MAIN
@@ -290,15 +268,10 @@
         for copy in first_half:
             copy.start()
         rest = [
-            pltpu.make_async_copy(a, b, sems.at[n])
-            for n, (a, b) in enumerate(((rim_sums, rim_sums_buf), (by_row, rows_buf)))
-        ]
-        rest += [
             pltpu.make_async_copy(piece, rims_buf.at[places[n]], rim_sems.at[n]) for n, piece in enumerate(rim_pieces)
         ]
         for copy in rest:
             copy.start()
-        sums_copy(0).start()
         for part in (1, 2):
             for copy in piece_copies(part):
                 copy.start()
@@ -319,10 +292,10 @@
             put_taps(taps, n * C3, chunk[n])
         for copy in piece_copies(1):
             copy.wait()
-        gates(sums_at(rim_taps, 0), rim_sums_buf[0], inside(above[1, :STATE_CH], not_first), (0,))
+        gates(sums_at(rim_taps, 0), rim_sums[0], inside(above[1, :STATE_CH], not_first), (0,))
         candidate_terms(0, None)
         row_sums = sums_at(rim_taps, 1)
-        gates(row_sums, rim_sums_buf[1], rows_buf[0], (1,))
+        gates(row_sums, rim_sums[1], by_row[0], (1,))
         candidate_terms(1, row_sums[2 * STATE_CH :])
 
     @pl.when(step == 1)
@@ -330,12 +303,6 @@
         for copy in piece_copies(2):
             copy.wait()
 
-    @pl.when(step + 1 < STEPS)
-    def _():
-        sums_copy(step + 1).start()
-
-    sums_copy(step).wait()
-    state_sums = sums_buf.at[lax.rem(step, 2)]
     here = pl.multiple_of(step * CHUNK, CHUNK)
     owner = lax.axis_index("space")
     tile = lax.broadcasted_iota(jnp.int32, (1, COLS), 1) // TILE
@@ -352,19 +319,19 @@
         terms = candidate_terms(slot + 1, side_terms)
         rest = jnp.dot(w_rest[...], rest_taps[n * REST : (n + 3) * REST, :], preferred_element_type=F32)
         proposal = jnp.tanh(partial[slot] + terms + rest)
-        old = rows_buf[here + n].astype(F32)
+        old = by_row[here + n].astype(F32)
         new = (1.0 - update[slot]) * old + update[slot] * proposal
         rows_done[n] = jnp.where(chosen, new, old).astype(BF16)
 
     waiting = []
     for n in range(CHUNK):
         row_sums = sums_at(taps, n)
-        carried = rows_buf[jnp.minimum(here + n + 1, ROWS - 1)]
+        carried = by_row[jnp.minimum(here + n + 1, ROWS - 1)]
         if n == CHUNK - 1:
             carried = jnp.where(step == STEPS - 1, inside(below[0, :STATE_CH], not_last), carried)
         if len(waiting) == LAG:
             candidate(n - LAG, waiting.pop(0))
-        gates(row_sums, state_sums[n], carried, (n + 2,) if n < CHUNK - HALO else (n + 2, n + 2 - CHUNK))
+        gates(row_sums, sums[n], carried, (n + 2,) if n < CHUNK - HALO else (n + 2, n + 2 - CHUNK))
         waiting.append(row_sums[2 * STATE_CH :])
         place = n + AHEAD
         if place < CHUNK:
@@ -396,16 +363,13 @@
         grid=(STEPS,),
         in_specs=[any_space] * (len(pieces) + 1)
         + [whole(HALO, EDGE_CH, COLS)] * 2
-        + [any_space] * 3
-        + [whole(*a.shape) for a in weights]
+        + [pl.BlockSpec((CHUNK, 2 * STATE_CH, COLS), lambda i: (i, 0, 0))]
+        + [whole(*a.shape) for a in (by_row, rim_sums, *weights)]
         + [smem, smem],
         out_specs=pl.BlockSpec((STATE_CH, CHUNK, COLS), lambda i: (0, i, 0)),
         out_shape=jax.ShapeDtypeStruct((STATE_CH, ROWS, COLS), BF16),
         scratch_shapes=[
             pltpu.VMEM((SIDE_CH, ROWS, COLS), BF16),
-            pltpu.VMEM((2, CHUNK, 2 * STATE_CH, COLS), F32),
-            pltpu.VMEM((ROWS, STATE_CH, COLS), BF16),
-            pltpu.VMEM((HALO, 2 * STATE_CH, COLS), F32),
             pltpu.VMEM(((CHUNK + HALO) * C3, COLS), BF16),
             pltpu.VMEM((2 * HALO * C3, COLS), BF16),
             pltpu.VMEM((4 * MAIN, COLS), BF16),
@@ -417,10 +381,8 @@
             pltpu.VMEM((2 * HALO, CONTEXT_CH, COLS), BF16),
             pltpu.SemaphoreType.DMA((3, 9)),
             pltpu.SemaphoreType.DMA((8,)),
-            pltpu.SemaphoreType.DMA((2,)),
-            pltpu.SemaphoreType.DMA((2,)),
         ],
-        compiler_params=pltpu.CompilerParams(vmem_limit_bytes=30 * 2**20),
+        compiler_params=pltpu.CompilerParams(vmem_limit_bytes=24 * 2**20),
         cost_estimate=pl.CostEstimate(flops=17_000_000_000, bytes_accessed=20_000_000, transcendentals=0),
         name="side_part",
     )(

time: 56.9 us -> 54.3 us (0.954)
  Pallas kernels: 35.6 us -> 32.1 us
  starting transfers between devices: 18.1 us -> 19 us
    pallas_call x2, Pallas kernels: 11.2 us -> 9.39 us  [state_part(): pl.pallas_call(functools.partial(state_kernel, first, count), grid=(count...]
    pallas_call x1, Pallas kernels: 22.1 us -> 20.4 us  [side_part(): pl.pallas_call(side_kernel, grid=(STEPS,), in_specs=[any_space] * (len(pi...]
    ppermute x2, starting transfers between devices: 3.9 us -> 4.83 us  [to_core(): return lax.ppermute(a, 'member', CORES)]
  transfers between devices with their start and end apart: 9 -> 9, of which waited for: 1 -> 1; matrix products, arithmetic and copies ran while one was open for 0% -> 1% of each run, Pallas kernels for 24% -> 22%
where the time goes in v4:
time: 54.3 us; the launch traced here: 54.1 us
  Pallas kernels  32.1 us (59%)
  starting transfers between devices  19 us (35%)
  local copies, waits for them, and re-layouts  1.21 us (2%)
  waiting for transfers between devices  1.11 us (2%)
    pallas_call x1, Pallas kernels, side_part(): pl.pallas_call(side_kernel, grid=(STEPS,), in_specs=[any_space] * (len(pi...  20.4 us
    pallas_call x2, Pallas kernels, state_part(): pl.pallas_call(functools.partial(state_kernel, first, count), grid=(count...  9.39 us
    ppermute x2, starting transfers between devices, to_core(): return lax.ppermute(a, 'member', CORES)  4.83 us
    ppermute x1, starting transfers between devices, shards(): lax.ppermute(top, 'space', [((n + 1) % owners, n) for n in range(owners)])  4.65 us
    ppermute x1, starting transfers between devices, shards(): far = lax.ppermute(jnp.concatenate([forth, rim], axis=0), 'member', FORTH)  2.43 us
    ppermute x1, starting transfers between devices, shards(): back = lax.ppermute(context_field, 'member', BACK)  2.04 us
    ppermute x1, starting transfers between devices, shards(): lax.ppermute(low, 'space', [(n, (n + 1) % owners) for n in range(owners)])  1.9 us
    pallas_call x1, Pallas kernels, edges(): pl.pallas_call(edge_kernel, in_specs=[pl.BlockSpec(memory_space=pltpu.HBM...  1.78 us
  transfers between devices with their start and end apart: 9, of which 1 were waited for; matrix products, arithmetic and copies ran while one was open for 1% of the time, Pallas kernels for 22%

profile of v4, /device:TPU:1, one launch (start us, length us, event | category | flops | bytes accessed | tf_op | source)
XLA Modules:
  0.0 54.1 jit_solution(15520997030055873405)
XLA Ops:
  0.0 2.0 %collective-permute-start.1 = (bf16[12,64,256]{2,1,0:T(8,128)(2,1)}, bf16[12,64,256]{2,1,0:T(8,128)(2,1)S(1)}, u32[]{:S(2)}, u32[]{:S(2)}) collective-permute-start(bf16[12,64,256]{2,1,0:T(8,128)(2,1)} %context.3), channel_id=1, source_target_pairs={{2,0},{7,1},{4,2},{1,3},{6,4},{3,5},{0,6},{5,7},{10,8},{15,9},{12,... | collective-permute-start | bytes 1179656 | tf_op jit(solution)/shard_map/ppermute | solution.py:416
  2.0 1.3 %collective-permute-start = (bf16[12,64,256]{2,1,0:T(8,128)(2,1)}, bf16[12,64,256]{2,1,0:T(8,128)(2,1)S(1)}, u32[]{:S(2)}, u32[]{:S(2)}) collective-permute-start(bf16[12,64,256]{2,1,0:T(8,128)(2,1)} %context.3), channel_id=1, source_target_pairs={{0,2},{1,7},{2,4},{3,1},{4,6},{5,3},{6,0},{7,5},{8,10},{9,15},{10,... | collective-permute-start | bytes 1179656 | tf_op jit(solution)/shard_map/ppermute | solution.py:415
  3.3 1.8 %edges.1 = (bf16[2,128,256]{2,1,0:T(8,128)(2,1)S(1)}, bf16[2,128,256]{2,1,0:T(8,128)(2,1)S(1)}) custom-call(bf16[96,64,256]{2,1,0:T(8,128)(2,1)} %bitcast.12, bf16[8,64,256]{2,1,0:T(8,128)(2,1)} %bitcast.20, bf16[12,64,256]{2,1,0:T(8,128)(2,1)} %context.3), custom_call_target="tpu_custom_call" | custom-call | bytes 4000000 | tf_op jit(solution)/shard_map/edges/pallas_call | solution.py:68
  5.1 1.9 %collective-permute-start.2 = (bf16[2,128,256]{2,1,0:T(8,128)(2,1)S(1)}, bf16[2,128,256]{2,1,0:T(8,128)(2,1)S(1)}, u32[]{:S(2)}, u32[]{:S(2)}) collective-permute-start(bf16[2,128,256]{2,1,0:T(8,128)(2,1)S(1)} %get-tuple-element.35), channel_id=1, source_target_pairs={{0,8},{8,16},{16,24},{24,32},{32,40},{40,48},{48,56},{56,64},{64,7... | collective-permute-start | bytes 393224 | tf_op jit(solution)/shard_map/ppermute | solution.py:418
  7.0 4.7 %collective-permute-start.3 = (bf16[2,128,256]{2,1,0:T(8,128)(2,1)S(1)}, bf16[2,128,256]{2,1,0:T(8,128)(2,1)S(1)}, u32[]{:S(2)}, u32[]{:S(2)}) collective-permute-start(bf16[2,128,256]{2,1,0:T(8,128)(2,1)S(1)} %get-tuple-element.40.refs_5_), channel_id=1, source_target_pairs={{8,0},{16,8},{24,16},{32,24},{40,32},{48,40},{56,48},{64,56},{72,6... | collective-permute-start | bytes 393224 | tf_op jit(solution)/shard_map/ppermute | solution.py:419
  11.7 1.2 %copy-done.1 = bf16[192,200,3,3]{1,0,3,2:T(8,128)(2,1)S(1)} copy-done((bf16[192,200,3,3]{1,0,3,2:T(8,128)(2,1)S(1)}, bf16[192,200,3,3]{1,0,3,2:T(8,128)(2,1)}, u32[]{:S(2)}) %copy-start.1) | copy-done | bytes 691224
  12.8 0.1 state_weights.1.refs_2_
  13.0 4.6 %state_part_0.1 = (f32[64,192,256]{2,1,0:T(8,128)S(1)}, bf16[64,96,256]{2,1,0:T(8,128)(2,1)S(1)}) custom-call(bf16[96,64,256]{2,1,0:T(8,128)(2,1)S(1)} %bitcast.13, bf16[96,64,256]{2,1,0:T(8,128)(2,1)S(1)} %bitcast.14, bf16[192,864]{1,0:T(8,128)(2,1)S(1)} %state_weights.1.refs_2_), custom_call_target="tpu_custom_call" | custom-call | flops 6000000000 | bytes 10000000 | tf_op jit(solution)/shard_map/state_part_0/pallas_call | solution.py:181
  17.6 0.0 copy-start.3
  17.6 0.0 collective-permute-done.2.refs_3_.above
  17.6 0.0 collective-permute-done.3.refs_4_.below
  17.6 0.0 collective-permute-done.1.back
  17.6 0.0 collective-permute-done.forth
  17.7 1.6 %collective-permute-start.5 = (bf16[1,64,256]{2,1,0:T(8,128)(2,1)S(1)}, bf16[1,64,256]{2,1,0:T(8,128)(2,1)S(1)}, u32[]{:S(2)}, u32[]{:S(2)}) collective-permute-start(bf16[1,64,256]{2,1,0:T(8,128)(2,1)S(1)} %bitcast.24), channel_id=1, source_target_pairs={{0,4},{1,5},{2,6},{3,7},{4,0},{5,1},{6,2},{7,3},{8,12},{9,13},{10,... | collective-permute-start | bytes 98312 | tf_op jit(solution)/shard_map/ppermute | solution.py:429
  19.3 0.3 collective-permute-start.4
  19.6 2.4 %collective-permute-start.6 = (bf16[13,64,256]{2,1,0:T(8,128)(2,1)S(1)}, bf16[13,64,256]{2,1,0:T(8,128)(2,1)S(1)}, u32[]{:S(2)}, u32[]{:S(2)}) collective-permute-start(bf16[13,64,256]{2,1,0:T(8,128)(2,1)S(1)} %pad_maximum_fusion.2), channel_id=1, source_target_pairs={{0,2},{1,7},{2,4},{3,1},{4,6},{5,3},{6,0},{7,5},{8,10},{9,15},{10,... | collective-permute-start | bytes 1277960 | tf_op jit(solution)/shard_map/ppermute | solution.py:428
  22.1 0.1 pad_maximum_fusion
  22.2 1.2 %collective-permute-start.7 = (bf16[36,64,256]{2,1,0:T(8,128)(2,1)S(1)}, bf16[36,64,256]{2,1,0:T(8,128)(2,1)S(1)}, u32[]{:S(2)}, u32[]{:S(2)}) collective-permute-start(bf16[36,64,256]{2,1,0:T(8,128)(2,1)S(1)} %pad_maximum_fusion), channel_id=1, source_target_pairs={{0,1},{1,0},{2,3},{3,2},{4,5},{5,4},{6,7},{7,6},{8,9},{9,8},{10,11... | collective-permute-start | bytes 3538952 | tf_op jit(solution)/shard_map/ppermute | solution.py:413
  23.4 4.8 %state_part_2.1 = (f32[64,192,256]{2,1,0:T(8,128)S(1)}, bf16[64,96,256]{2,1,0:T(8,128)(2,1)S(1)}, f32[2,192,256]{2,1,0:T(8,128)S(1)}) custom-call(bf16[96,64,256]{2,1,0:T(8,128)(2,1)S(1)} %bitcast.15, bf16[96,64,256]{2,1,0:T(8,128)(2,1)S(1)} %bitcast.16, bf16[192,864]{1,0:T(8,128)(2,1)S(1)} %state_weights.1.refs_2_, ...), custom_call_target="tpu_custom_call", output_to_operand_aliasing={{0}: (6, {}), {1}: (7, {})} | custom-call | flops 6000000000 | bytes 10000000 | tf_op jit(solution)/shard_map/state_part_2/pallas_call | solution.py:181
  28.2 0.0 copy-start.2
  28.3 0.0 collective-permute-done.5
  28.3 0.0 collective-permute-done.4
  28.3 0.0 collective-permute-done.6.far
  28.3 0.0 copy-start.5
  28.3 0.0 copy-start.6
  28.3 0.0 copy-start.7
  28.3 0.1 pad_maximum_fusion.1
  28.4 3.6 %collective-permute-start.8 = (bf16[16,64,256]{2,1,0:T(8,128)(2,1)S(1)}, bf16[16,64,256]{2,1,0:T(8,128)(2,1)S(1)}, u32[]{:S(2)}, u32[]{:S(2)}) collective-permute-start(bf16[16,64,256]{2,1,0:T(8,128)(2,1)S(1)} %pad_maximum_fusion.1), channel_id=1, source_target_pairs={{0,1},{1,0},{2,3},{3,2},{4,5},{5,4},{6,7},{7,6},{8,9},{9,8},{10,11... | collective-permute-start | bytes 1572872 | tf_op jit(solution)/shard_map/ppermute | solution.py:413
  32.0 0.4 side_weights.1
  32.5 1.1 %collective-permute-done.8.other_far = bf16[16,64,256]{2,1,0:T(8,128)(2,1)S(1)} collective-permute-done((bf16[16,64,256]{2,1,0:T(8,128)(2,1)S(1)}, bf16[16,64,256]{2,1,0:T(8,128)(2,1)S(1)}, u32[]{:S(2)}, u32[]{:S(2)}) %collective-permute-start.8) | collective-permute-done | bytes 524320 | tf_op jit(solution)/shard_map/ppermute | solution.py:413
  33.6 0.0 collective-permute-done.7.others
  33.6 20.4 %side_part.1 = bf16[96,64,256]{2,1,0:T(8,128)(2,1)} custom-call(bf16[12,64,256]{2,1,0:T(8,128)(2,1)S(1)} %copy-done.3, bf16[12,64,256]{2,1,0:T(8,128)(2,1)S(1)} %collective-permute-done.forth, bf16[12,64,256]{2,1,0:T(8,128)(2,1)S(1)} %collective-permute-done.1.back, bf16[13,64,256]{2,1,0:T(8,128)(2,1)S(1)} %collective-permute-done.6.far, ...), custom_call_target="tpu_custom_call" | custom-call | flops 16999999488 | bytes 20000000 | tf_op jit(solution)/shard_map/side_part/pallas_call | solution.py:361
  (15 shorter events, 0.1 us)
Async XLA Ops:
  0.0 17.6 %collective-permute-start.1 = (bf16[12,64,256]{2,1,0:T(8,128)(2,1)}, bf16[12,64,256]{2,1,0:T(8,128)(2,1)S(1)}, u32[]{:S(2)}, u32[]{:S(2)}) collective-permute-start(bf16[12,64,256]{2,1,0:T(8,128)(2,1)} %context.3), channel_id=1, source_target_pairs={{2,0},{7,1},{4,2},{1,3},{6,4},{3,5},{0,6},{5,7},{10,8},{15,9},{12,... | collective-permute-start | bytes 1179656 | tf_op jit(solution)/shard_map/ppermute | solution.py:416
  2.0 15.6 %collective-permute-start = (bf16[12,64,256]{2,1,0:T(8,128)(2,1)}, bf16[12,64,256]{2,1,0:T(8,128)(2,1)S(1)}, u32[]{:S(2)}, u32[]{:S(2)}) collective-permute-start(bf16[12,64,256]{2,1,0:T(8,128)(2,1)} %context.3), channel_id=1, source_target_pairs={{0,2},{1,7},{2,4},{3,1},{4,6},{5,3},{6,0},{7,5},{8,10},{9,15},{10,... | collective-permute-start | bytes 1179656 | tf_op jit(solution)/shard_map/ppermute | solution.py:415
  3.3 9.7 %copy-start = (bf16[1,96,64,256]{3,2,1,0:T(8,128)(2,1)S(1)}, bf16[1,96,64,256]{3,2,1,0:T(8,128)(2,1)}, u32[]{:S(2)}) copy-start(bf16[1,96,64,256]{3,2,1,0:T(8,128)(2,1)} %param.7) | copy-start | bytes 9437188
  5.1 12.5 %collective-permute-start.2 = (bf16[2,128,256]{2,1,0:T(8,128)(2,1)S(1)}, bf16[2,128,256]{2,1,0:T(8,128)(2,1)S(1)}, u32[]{:S(2)}, u32[]{:S(2)}) collective-permute-start(bf16[2,128,256]{2,1,0:T(8,128)(2,1)S(1)} %get-tuple-element.35), channel_id=1, source_target_pairs={{0,8},{8,16},{16,24},{24,32},{32,40},{40,48},{48,56},{56,64},{64,7... | collective-permute-start | bytes 393224 | tf_op jit(solution)/shard_map/ppermute | solution.py:418
  7.0 10.6 %collective-permute-start.3 = (bf16[2,128,256]{2,1,0:T(8,128)(2,1)S(1)}, bf16[2,128,256]{2,1,0:T(8,128)(2,1)S(1)}, u32[]{:S(2)}, u32[]{:S(2)}) collective-permute-start(bf16[2,128,256]{2,1,0:T(8,128)(2,1)S(1)} %get-tuple-element.40.refs_5_), channel_id=1, source_target_pairs={{8,0},{16,8},{24,16},{32,24},{40,32},{48,40},{56,48},{64,56},{72,6... | collective-permute-start | bytes 393224 | tf_op jit(solution)/shard_map/ppermute | solution.py:419
  11.7 1.2 %copy-start.1 = (bf16[192,200,3,3]{1,0,3,2:T(8,128)(2,1)S(1)}, bf16[192,200,3,3]{1,0,3,2:T(8,128)(2,1)}, u32[]{:S(2)}) copy-start(bf16[192,200,3,3]{1,0,3,2:T(8,128)(2,1)} %param.10) | copy-start | bytes 2073604
  17.6 4.5 %copy-start.3 = (bf16[12,64,256]{2,1,0:T(8,128)(2,1)S(1)}, bf16[12,64,256]{2,1,0:T(8,128)(2,1)}, u32[]{:S(2)}) copy-start(bf16[12,64,256]{2,1,0:T(8,128)(2,1)} %context.3) | copy-start | bytes 1179652
  17.7 10.6 %collective-permute-start.5 = (bf16[1,64,256]{2,1,0:T(8,128)(2,1)S(1)}, bf16[1,64,256]{2,1,0:T(8,128)(2,1)S(1)}, u32[]{:S(2)}, u32[]{:S(2)}) collective-permute-start(bf16[1,64,256]{2,1,0:T(8,128)(2,1)S(1)} %bitcast.24), channel_id=1, source_target_pairs={{0,4},{1,5},{2,6},{3,7},{4,0},{5,1},{6,2},{7,3},{8,12},{9,13},{10,... | collective-permute-start | bytes 98312 | tf_op jit(solution)/shard_map/ppermute | solution.py:429
  19.3 9.0 %collective-permute-start.4 = (bf16[1,64,256]{2,1,0:T(8,128)(2,1)S(1)}, bf16[1,64,256]{2,1,0:T(8,128)(2,1)S(1)}, u32[]{:S(2)}, u32[]{:S(2)}) collective-permute-start(bf16[1,64,256]{2,1,0:T(8,128)(2,1)S(1)} %bitcast.25), channel_id=1, source_target_pairs={{2,0},{7,1},{4,2},{1,3},{6,4},{3,5},{0,6},{5,7},{10,8},{15,9},{12,... | collective-permute-start | bytes 98312 | tf_op jit(solution)/shard_map/ppermute | solution.py:429
  19.6 8.6 %collective-permute-start.6 = (bf16[13,64,256]{2,1,0:T(8,128)(2,1)S(1)}, bf16[13,64,256]{2,1,0:T(8,128)(2,1)S(1)}, u32[]{:S(2)}, u32[]{:S(2)}) collective-permute-start(bf16[13,64,256]{2,1,0:T(8,128)(2,1)S(1)} %pad_maximum_fusion.2), channel_id=1, source_target_pairs={{0,2},{1,7},{2,4},{3,1},{4,6},{5,3},{6,0},{7,5},{8,10},{9,15},{10,... | collective-permute-start | bytes 1277960 | tf_op jit(solution)/shard_map/ppermute | solution.py:428
  22.2 11.4 %collective-permute-start.7 = (bf16[36,64,256]{2,1,0:T(8,128)(2,1)S(1)}, bf16[36,64,256]{2,1,0:T(8,128)(2,1)S(1)}, u32[]{:S(2)}, u32[]{:S(2)}) collective-permute-start(bf16[36,64,256]{2,1,0:T(8,128)(2,1)S(1)} %pad_maximum_fusion), channel_id=1, source_target_pairs={{0,1},{1,0},{2,3},{3,2},{4,5},{5,4},{6,7},{7,6},{8,9},{9,8},{10,11... | collective-permute-start | bytes 3538952 | tf_op jit(solution)/shard_map/ppermute | solution.py:413
  23.4 8.6 %copy-start.4 = (bf16[96,200,3,3]{1,0,3,2:T(8,128)(2,1)S(1)}, bf16[96,200,3,3]{1,0,3,2:T(8,128)(2,1)}, u32[]{:S(2)}) copy-start(bf16[96,200,3,3]{1,0,3,2:T(8,128)(2,1)} %param.11) | copy-start | bytes 1036804
  28.2 3.8 %copy-start.2 = (bf16[192,200,3,3]{1,0,3,2:T(8,128)(2,1)S(1)}, bf16[192,200,3,3]{1,0,3,2:T(8,128)(2,1)}, u32[]{:S(2)}) copy-start(bf16[192,200,3,3]{1,0,3,2:T(8,128)(2,1)} %param.10) | copy-start | bytes 2073604
  28.3 5.3 %copy-start.5 = (bf16[1,1,8,64,256]{4,3,2,1,0:T(8,128)(2,1)S(1)}, bf16[1,1,8,64,256]{4,3,2,1,0:T(8,128)(2,1)}, u32[]{:S(2)}) copy-start(bf16[1,1,8,64,256]{4,3,2,1,0:T(8,128)(2,1)} %param.9) | copy-start | bytes 786436
  28.3 5.3 %copy-start.6 = (s32[16,4]{0,1:T(4,128)S(1)}, s32[16,4]{0,1:T(4,128)}, u32[]{:S(2)}) copy-start(s32[16,4]{0,1:T(4,128)} %param.12) | copy-start | bytes 772
  28.3 5.3 %copy-start.7 = (s32[16,4]{0,1:T(4,128)S(1)}, s32[16,4]{0,1:T(4,128)}, u32[]{:S(2)}) copy-start(s32[16,4]{0,1:T(4,128)} %param.13) | copy-start | bytes 772
  28.4 5.1 %collective-permute-start.8 = (bf16[16,64,256]{2,1,0:T(8,128)(2,1)S(1)}, bf16[16,64,256]{2,1,0:T(8,128)(2,1)S(1)}, u32[]{:S(2)}, u32[]{:S(2)}) collective-permute-start(bf16[16,64,256]{2,1,0:T(8,128)(2,1)S(1)} %pad_maximum_fusion.1), channel_id=1, source_target_pairs={{0,1},{1,0},{2,3},{3,2},{4,5},{5,4},{6,7},{7,6},{8,9},{9,8},{10,11... | collective-permute-start | bytes 1572872 | tf_op jit(solution)/shard_map/ppermute | solution.py:413

commit v5 on v4

--- a/solution.py
+++ b/solution.py
@@ -426,9 +426,12 @@
     side = slice(STATE_CH + 16, STATE_CH + 16 + RIM_CH)
     rim = jnp.concatenate([above[:, side], below[:, side]], axis=0).reshape(1, 2 * HALO * RIM_CH, COLS)
     far = lax.ppermute(jnp.concatenate([forth, rim], axis=0), "member", FORTH)
+    others = to_core(jnp.concatenate([context_field, forth, back], axis=0))
+    before = state_part(2, 1, state, state_weights, before)
+
+    before, rim = lax.optimization_barrier((before, rim))
     rims = [rim, lax.ppermute(rim, "member", BACK), lax.ppermute(rim, "member", along_x(2))]
-    others = to_core(jnp.concatenate([context_field, forth, back], axis=0))
-    sums, by_row, rim_sums = state_part(2, 2, state, state_weights, before, (above, below, top))
+    sums, by_row, rim_sums = state_part(3, 1, state, state_weights, before, (above, below, top))
 
     sums, rims, far = lax.optimization_barrier((sums, rims, far))
     rims = jnp.concatenate(rims, axis=0)

time: 54.3 us -> 53.2 us (0.980)
  starting transfers between devices: 19 us -> 16.7 us
  waiting for transfers between devices: 1.11 us -> 3.22 us
  Pallas kernels: 32.1 us -> 31.3 us
    ppermute x2, starting transfers between devices: 4.83 us -> 1.71 us  [to_core(): return lax.ppermute(a, 'member', CORES)]
    ppermute x1, starting transfers between devices: 1.61 us -> 3.74 us  [shards(): lax.ppermute(rim, 'member', along_x(2))]
    ppermute x1, waiting for transfers between devices: 0.01 us -> 2.12 us  [shards(): lax.ppermute(rim, 'member', BACK)]
    ppermute x1, starting transfers between devices: 2.43 us -> 1.34 us  [shards(): far = lax.ppermute(jnp.concatenate([forth, rim], axis=0), 'member', FORTH)]
    pallas_call x2 -> x3, Pallas kernels: 9.39 us -> 8.68 us  [state_part(): pl.pallas_call(functools.partial(state_kernel, first, count), grid=(count...]
  transfers between devices with their start and end apart: 9 -> 9, of which waited for: 1 -> 2; matrix products, arithmetic and copies ran while one was open for 1% -> 0% of each run, Pallas kernels for 22% -> 21%
where the time goes in v5:
time: 53.2 us; the launch traced here: 53 us
  Pallas kernels  31.3 us (59%)
  starting transfers between devices  16.7 us (31%)
  waiting for transfers between devices  3.22 us (6%)
  local copies, waits for them, and re-layouts  1.21 us (2%)
    pallas_call x1, Pallas kernels, side_part(): pl.pallas_call(side_kernel, grid=(STEPS,), in_specs=[any_space] * (len(pi...  20.4 us
    pallas_call x3, Pallas kernels, state_part(): pl.pallas_call(functools.partial(state_kernel, first, count), grid=(count...  8.68 us
    ppermute x1, starting transfers between devices, shards(): lax.ppermute(top, 'space', [((n + 1) % owners, n) for n in range(owners)])  4.65 us
    ppermute x1, starting transfers between devices, shards(): lax.ppermute(rim, 'member', along_x(2))  3.74 us
    ppermute x1, waiting for transfers between devices, shards(): lax.ppermute(rim, 'member', BACK)  2.12 us
    ppermute x1, starting transfers between devices, shards(): back = lax.ppermute(context_field, 'member', BACK)  2.04 us
    ppermute x1, starting transfers between devices, shards(): lax.ppermute(low, 'space', [(n, (n + 1) % owners) for n in range(owners)])  1.84 us
    ppermute x2, starting transfers between devices, to_core(): return lax.ppermute(a, 'member', CORES)  1.71 us
  transfers between devices with their start and end apart: 9, of which 2 were waited for; matrix products, arithmetic and copies ran while one was open for 0% of the time, Pallas kernels for 21%

profile of v5, /device:TPU:1, one launch (start us, length us, event | category | flops | bytes accessed | tf_op | source)
XLA Modules:
  0.0 53.0 jit_solution(14806088634942079567)
XLA Ops:
  0.0 2.0 %collective-permute-start.1 = (bf16[12,64,256]{2,1,0:T(8,128)(2,1)}, bf16[12,64,256]{2,1,0:T(8,128)(2,1)S(1)}, u32[]{:S(2)}, u32[]{:S(2)}) collective-permute-start(bf16[12,64,256]{2,1,0:T(8,128)(2,1)} %context.3), channel_id=1, source_target_pairs={{2,0},{7,1},{4,2},{1,3},{6,4},{3,5},{0,6},{5,7},{10,8},{15,9},{12,... | collective-permute-start | bytes 1179656 | tf_op jit(solution)/shard_map/ppermute | solution.py:416
  2.0 1.3 %collective-permute-start = (bf16[12,64,256]{2,1,0:T(8,128)(2,1)}, bf16[12,64,256]{2,1,0:T(8,128)(2,1)S(1)}, u32[]{:S(2)}, u32[]{:S(2)}) collective-permute-start(bf16[12,64,256]{2,1,0:T(8,128)(2,1)} %context.3), channel_id=1, source_target_pairs={{0,2},{1,7},{2,4},{3,1},{4,6},{5,3},{6,0},{7,5},{8,10},{9,15},{10,... | collective-permute-start | bytes 1179656 | tf_op jit(solution)/shard_map/ppermute | solution.py:415
  3.4 1.6 %edges.1 = (bf16[2,128,256]{2,1,0:T(8,128)(2,1)S(1)}, bf16[2,128,256]{2,1,0:T(8,128)(2,1)S(1)}) custom-call(bf16[96,64,256]{2,1,0:T(8,128)(2,1)} %bitcast.12, bf16[8,64,256]{2,1,0:T(8,128)(2,1)} %bitcast.22, bf16[12,64,256]{2,1,0:T(8,128)(2,1)} %context.3), custom_call_target="tpu_custom_call" | custom-call | bytes 4000000 | tf_op jit(solution)/shard_map/edges/pallas_call | solution.py:68
  5.0 1.8 %collective-permute-start.2 = (bf16[2,128,256]{2,1,0:T(8,128)(2,1)S(1)}, bf16[2,128,256]{2,1,0:T(8,128)(2,1)S(1)}, u32[]{:S(2)}, u32[]{:S(2)}) collective-permute-start(bf16[2,128,256]{2,1,0:T(8,128)(2,1)S(1)} %get-tuple-element.40), channel_id=1, source_target_pairs={{0,8},{8,16},{16,24},{24,32},{32,40},{40,48},{48,56},{56,64},{64,7... | collective-permute-start | bytes 393224 | tf_op jit(solution)/shard_map/ppermute | solution.py:418
  6.9 4.7 %collective-permute-start.3 = (bf16[2,128,256]{2,1,0:T(8,128)(2,1)S(1)}, bf16[2,128,256]{2,1,0:T(8,128)(2,1)S(1)}, u32[]{:S(2)}, u32[]{:S(2)}) collective-permute-start(bf16[2,128,256]{2,1,0:T(8,128)(2,1)S(1)} %get-tuple-element.45.refs_5_), channel_id=1, source_target_pairs={{8,0},{16,8},{24,16},{32,24},{40,32},{48,40},{56,48},{64,56},{72,6... | collective-permute-start | bytes 393224 | tf_op jit(solution)/shard_map/ppermute | solution.py:419
  11.5 1.2 %copy-done.1 = bf16[192,200,3,3]{1,0,3,2:T(8,128)(2,1)S(1)} copy-done((bf16[192,200,3,3]{1,0,3,2:T(8,128)(2,1)S(1)}, bf16[192,200,3,3]{1,0,3,2:T(8,128)(2,1)}, u32[]{:S(2)}) %copy-start.1) | copy-done | bytes 691224
  12.7 0.1 state_weights.1.refs_2_
  12.8 0.0 copy-start.3
  12.8 4.6 %state_part_0.1 = (f32[64,192,256]{2,1,0:T(8,128)S(1)}, bf16[64,96,256]{2,1,0:T(8,128)(2,1)S(1)}) custom-call(bf16[96,64,256]{2,1,0:T(8,128)(2,1)S(1)} %bitcast.13, bf16[96,64,256]{2,1,0:T(8,128)(2,1)S(1)} %bitcast.14, bf16[192,864]{1,0:T(8,128)(2,1)S(1)} %state_weights.1.refs_2_), custom_call_target="tpu_custom_call" | custom-call | flops 6000000000 | bytes 10000000 | tf_op jit(solution)/shard_map/state_part_0/pallas_call | solution.py:181
  17.4 0.0 collective-permute-done.2.refs_3_.above
  17.4 0.0 collective-permute-done.3.refs_4_.below
  17.5 0.0 collective-permute-done.1.back
  17.5 0.0 collective-permute-done.forth
  17.6 1.3 %collective-permute-start.6 = (bf16[13,64,256]{2,1,0:T(8,128)(2,1)S(1)}, bf16[13,64,256]{2,1,0:T(8,128)(2,1)S(1)}, u32[]{:S(2)}, u32[]{:S(2)}) collective-permute-start(bf16[13,64,256]{2,1,0:T(8,128)(2,1)S(1)} %pad_maximum_fusion.2), channel_id=1, source_target_pairs={{0,2},{1,7},{2,4},{3,1},{4,6},{5,3},{6,0},{7,5},{8,10},{9,15},{10,... | collective-permute-start | bytes 1277960 | tf_op jit(solution)/shard_map/ppermute | solution.py:428
  18.9 0.1 pad_maximum_fusion
  19.0 0.6 %collective-permute-start.7 = (bf16[36,64,256]{2,1,0:T(8,128)(2,1)S(1)}, bf16[36,64,256]{2,1,0:T(8,128)(2,1)S(1)}, u32[]{:S(2)}, u32[]{:S(2)}) collective-permute-start(bf16[36,64,256]{2,1,0:T(8,128)(2,1)S(1)} %pad_maximum_fusion), channel_id=1, source_target_pairs={{0,1},{1,0},{2,3},{3,2},{4,5},{5,4},{6,7},{7,6},{8,9},{9,8},{10,11... | collective-permute-start | bytes 3538952 | tf_op jit(solution)/shard_map/ppermute | solution.py:413
  19.6 2.0 %state_part_2.1 = (f32[64,192,256]{2,1,0:T(8,128)S(1)}, bf16[64,96,256]{2,1,0:T(8,128)(2,1)S(1)}) custom-call(bf16[96,64,256]{2,1,0:T(8,128)(2,1)S(1)} %bitcast.15, bf16[96,64,256]{2,1,0:T(8,128)(2,1)S(1)} %bitcast.16, bf16[192,864]{1,0:T(8,128)(2,1)S(1)} %state_weights.1.refs_2_, ...), custom_call_target="tpu_custom_call", output_to_operand_aliasing={{0}: (3, {}), {1}: (4, {})} | custom-call | flops 3000000000 | bytes 5000000 | tf_op jit(solution)/shard_map/state_part_2/pallas_call | solution.py:181
  21.6 0.0 copy-start.2
  21.6 0.0 copy-start.4
  21.6 0.0 copy-start.5
  21.7 0.0 copy-start.6
  21.7 0.0 copy-start.7
  21.7 3.7 %collective-permute-start.5 = (bf16[1,64,256]{2,1,0:T(8,128)(2,1)S(1)}, bf16[1,64,256]{2,1,0:T(8,128)(2,1)S(1)}, u32[]{:S(2)}, u32[]{:S(2)}) collective-permute-start(bf16[1,64,256]{2,1,0:T(8,128)(2,1)S(1)} %bitcast.27), channel_id=1, source_target_pairs={{0,4},{1,5},{2,6},{3,7},{4,0},{5,1},{6,2},{7,3},{8,12},{9,13},{10,... | collective-permute-start | bytes 98312 | tf_op jit(solution)/shard_map/ppermute | solution.py:433
  25.4 0.0 collective-permute-start.4
  25.4 2.1 %state_part_3.1 = (f32[64,192,256]{2,1,0:T(8,128)S(1)}, bf16[64,96,256]{2,1,0:T(8,128)(2,1)S(1)}, f32[2,192,256]{2,1,0:T(8,128)S(1)}) custom-call(bf16[96,64,256]{2,1,0:T(8,128)(2,1)S(1)} %bitcast.17, bf16[96,64,256]{2,1,0:T(8,128)(2,1)S(1)} %bitcast.18, bf16[192,864]{1,0:T(8,128)(2,1)S(1)} %state_weights.1.refs_2_, ...), custom_call_target="tpu_custom_call", output_to_operand_aliasing={{0}: (6, {}), {1}: (7, {})} | custom-call | flops 3000000000 | bytes 5000000 | tf_op jit(solution)/shard_map/state_part_3/pallas_call | solution.py:181
  27.6 0.0 collective-permute-done.5
  27.6 2.1 %collective-permute-done.4 = bf16[1,64,256]{2,1,0:T(8,128)(2,1)S(1)} collective-permute-done((bf16[1,64,256]{2,1,0:T(8,128)(2,1)S(1)}, bf16[1,64,256]{2,1,0:T(8,128)(2,1)S(1)}, u32[]{:S(2)}, u32[]{:S(2)}) %collective-permute-start.4) | collective-permute-done | bytes 32800 | tf_op jit(solution)/shard_map/ppermute | solution.py:433
  29.7 0.1 pad_maximum_fusion.1
  29.8 1.1 %collective-permute-start.8 = (bf16[16,64,256]{2,1,0:T(8,128)(2,1)S(1)}, bf16[16,64,256]{2,1,0:T(8,128)(2,1)S(1)}, u32[]{:S(2)}, u32[]{:S(2)}) collective-permute-start(bf16[16,64,256]{2,1,0:T(8,128)(2,1)S(1)} %pad_maximum_fusion.1), channel_id=1, source_target_pairs={{0,1},{1,0},{2,3},{3,2},{4,5},{5,4},{6,7},{7,6},{8,9},{9,8},{10,11... | collective-permute-start | bytes 1572872 | tf_op jit(solution)/shard_map/ppermute | solution.py:413
  30.9 0.4 side_weights.1
  31.3 1.1 %collective-permute-done.8.other_far = bf16[16,64,256]{2,1,0:T(8,128)(2,1)S(1)} collective-permute-done((bf16[16,64,256]{2,1,0:T(8,128)(2,1)S(1)}, bf16[16,64,256]{2,1,0:T(8,128)(2,1)S(1)}, u32[]{:S(2)}, u32[]{:S(2)}) %collective-permute-start.8) | collective-permute-done | bytes 524320 | tf_op jit(solution)/shard_map/ppermute | solution.py:413
  32.4 20.4 %side_part.1 = bf16[96,64,256]{2,1,0:T(8,128)(2,1)} custom-call(bf16[12,64,256]{2,1,0:T(8,128)(2,1)S(1)} %copy-done.3, bf16[12,64,256]{2,1,0:T(8,128)(2,1)S(1)} %collective-permute-done.forth, bf16[12,64,256]{2,1,0:T(8,128)(2,1)S(1)} %collective-permute-done.1.back, bf16[13,64,256]{2,1,0:T(8,128)(2,1)S(1)} %collective-permute-done.6.far, ...), custom_call_target="tpu_custom_call" | custom-call | flops 16999999488 | bytes 20000000 | tf_op jit(solution)/shard_map/side_part/pallas_call | solution.py:361
  (16 shorter events, 0.1 us)
Async XLA Ops:
  0.0 12.8 %copy-start = (bf16[1,96,64,256]{3,2,1,0:T(8,128)(2,1)S(1)}, bf16[1,96,64,256]{3,2,1,0:T(8,128)(2,1)}, u32[]{:S(2)}) copy-start(bf16[1,96,64,256]{3,2,1,0:T(8,128)(2,1)} %param.7) | copy-start | bytes 9437188
  0.0 17.5 %collective-permute-start.1 = (bf16[12,64,256]{2,1,0:T(8,128)(2,1)}, bf16[12,64,256]{2,1,0:T(8,128)(2,1)S(1)}, u32[]{:S(2)}, u32[]{:S(2)}) collective-permute-start(bf16[12,64,256]{2,1,0:T(8,128)(2,1)} %context.3), channel_id=1, source_target_pairs={{2,0},{7,1},{4,2},{1,3},{6,4},{3,5},{0,6},{5,7},{10,8},{15,9},{12,... | collective-permute-start | bytes 1179656 | tf_op jit(solution)/shard_map/ppermute | solution.py:416
  2.0 15.4 %collective-permute-start = (bf16[12,64,256]{2,1,0:T(8,128)(2,1)}, bf16[12,64,256]{2,1,0:T(8,128)(2,1)S(1)}, u32[]{:S(2)}, u32[]{:S(2)}) collective-permute-start(bf16[12,64,256]{2,1,0:T(8,128)(2,1)} %context.3), channel_id=1, source_target_pairs={{0,2},{1,7},{2,4},{3,1},{4,6},{5,3},{6,0},{7,5},{8,10},{9,15},{10,... | collective-permute-start | bytes 1179656 | tf_op jit(solution)/shard_map/ppermute | solution.py:415
  5.0 12.4 %collective-permute-start.2 = (bf16[2,128,256]{2,1,0:T(8,128)(2,1)S(1)}, bf16[2,128,256]{2,1,0:T(8,128)(2,1)S(1)}, u32[]{:S(2)}, u32[]{:S(2)}) collective-permute-start(bf16[2,128,256]{2,1,0:T(8,128)(2,1)S(1)} %get-tuple-element.40), channel_id=1, source_target_pairs={{0,8},{8,16},{16,24},{24,32},{32,40},{40,48},{48,56},{56,64},{64,7... | collective-permute-start | bytes 393224 | tf_op jit(solution)/shard_map/ppermute | solution.py:418
  6.9 10.6 %collective-permute-start.3 = (bf16[2,128,256]{2,1,0:T(8,128)(2,1)S(1)}, bf16[2,128,256]{2,1,0:T(8,128)(2,1)S(1)}, u32[]{:S(2)}, u32[]{:S(2)}) collective-permute-start(bf16[2,128,256]{2,1,0:T(8,128)(2,1)S(1)} %get-tuple-element.45.refs_5_), channel_id=1, source_target_pairs={{8,0},{16,8},{24,16},{32,24},{40,32},{48,40},{56,48},{64,56},{72,6... | collective-permute-start | bytes 393224 | tf_op jit(solution)/shard_map/ppermute | solution.py:419
  11.5 1.2 %copy-start.1 = (bf16[192,200,3,3]{1,0,3,2:T(8,128)(2,1)S(1)}, bf16[192,200,3,3]{1,0,3,2:T(8,128)(2,1)}, u32[]{:S(2)}) copy-start(bf16[192,200,3,3]{1,0,3,2:T(8,128)(2,1)} %param.10) | copy-start | bytes 2073604
  12.8 6.1 %copy-start.3 = (bf16[12,64,256]{2,1,0:T(8,128)(2,1)S(1)}, bf16[12,64,256]{2,1,0:T(8,128)(2,1)}, u32[]{:S(2)}) copy-start(bf16[12,64,256]{2,1,0:T(8,128)(2,1)} %context.3) | copy-start | bytes 1179652
  17.6 12.1 %collective-permute-start.6 = (bf16[13,64,256]{2,1,0:T(8,128)(2,1)S(1)}, bf16[13,64,256]{2,1,0:T(8,128)(2,1)S(1)}, u32[]{:S(2)}, u32[]{:S(2)}) collective-permute-start(bf16[13,64,256]{2,1,0:T(8,128)(2,1)S(1)} %pad_maximum_fusion.2), channel_id=1, source_target_pairs={{0,2},{1,7},{2,4},{3,1},{4,6},{5,3},{6,0},{7,5},{8,10},{9,15},{10,... | collective-permute-start | bytes 1277960 | tf_op jit(solution)/shard_map/ppermute | solution.py:428
  19.0 13.4 %collective-permute-start.7 = (bf16[36,64,256]{2,1,0:T(8,128)(2,1)S(1)}, bf16[36,64,256]{2,1,0:T(8,128)(2,1)S(1)}, u32[]{:S(2)}, u32[]{:S(2)}) collective-permute-start(bf16[36,64,256]{2,1,0:T(8,128)(2,1)S(1)} %pad_maximum_fusion), channel_id=1, source_target_pairs={{0,1},{1,0},{2,3},{3,2},{4,5},{5,4},{6,7},{7,6},{8,9},{9,8},{10,11... | collective-permute-start | bytes 3538952 | tf_op jit(solution)/shard_map/ppermute | solution.py:413
  21.6 9.3 %copy-start.2 = (bf16[192,200,3,3]{1,0,3,2:T(8,128)(2,1)S(1)}, bf16[192,200,3,3]{1,0,3,2:T(8,128)(2,1)}, u32[]{:S(2)}) copy-start(bf16[192,200,3,3]{1,0,3,2:T(8,128)(2,1)} %param.10) | copy-start | bytes 2073604
  21.6 9.3 %copy-start.4 = (bf16[96,200,3,3]{1,0,3,2:T(8,128)(2,1)S(1)}, bf16[96,200,3,3]{1,0,3,2:T(8,128)(2,1)}, u32[]{:S(2)}) copy-start(bf16[96,200,3,3]{1,0,3,2:T(8,128)(2,1)} %param.11) | copy-start | bytes 1036804
  21.6 10.8 %copy-start.5 = (bf16[1,1,8,64,256]{4,3,2,1,0:T(8,128)(2,1)S(1)}, bf16[1,1,8,64,256]{4,3,2,1,0:T(8,128)(2,1)}, u32[]{:S(2)}) copy-start(bf16[1,1,8,64,256]{4,3,2,1,0:T(8,128)(2,1)} %param.9) | copy-start | bytes 786436
  21.7 10.8 %copy-start.6 = (s32[16,4]{0,1:T(4,128)S(1)}, s32[16,4]{0,1:T(4,128)}, u32[]{:S(2)}) copy-start(s32[16,4]{0,1:T(4,128)} %param.12) | copy-start | bytes 772
  21.7 10.8 %copy-start.7 = (s32[16,4]{0,1:T(4,128)S(1)}, s32[16,4]{0,1:T(4,128)}, u32[]{:S(2)}) copy-start(s32[16,4]{0,1:T(4,128)} %param.13) | copy-start | bytes 772
  21.7 5.9 %collective-permute-start.5 = (bf16[1,64,256]{2,1,0:T(8,128)(2,1)S(1)}, bf16[1,64,256]{2,1,0:T(8,128)(2,1)S(1)}, u32[]{:S(2)}, u32[]{:S(2)}) collective-permute-start(bf16[1,64,256]{2,1,0:T(8,128)(2,1)S(1)} %bitcast.27), channel_id=1, source_target_pairs={{0,4},{1,5},{2,6},{3,7},{4,0},{5,1},{6,2},{7,3},{8,12},{9,13},{10,... | collective-permute-start | bytes 98312 | tf_op jit(solution)/shard_map/ppermute | solution.py:433
  25.4 4.3 %collective-permute-start.4 = (bf16[1,64,256]{2,1,0:T(8,128)(2,1)S(1)}, bf16[1,64,256]{2,1,0:T(8,128)(2,1)S(1)}, u32[]{:S(2)}, u32[]{:S(2)}) collective-permute-start(bf16[1,64,256]{2,1,0:T(8,128)(2,1)S(1)} %bitcast.28), channel_id=1, source_target_pairs={{2,0},{7,1},{4,2},{1,3},{6,4},{3,5},{0,6},{5,7},{10,8},{15,9},{12,... | collective-permute-start | bytes 98312 | tf_op jit(solution)/shard_map/ppermute | solution.py:433
  29.8 2.6 %collective-permute-start.8 = (bf16[16,64,256]{2,1,0:T(8,128)(2,1)S(1)}, bf16[16,64,256]{2,1,0:T(8,128)(2,1)S(1)}, u32[]{:S(2)}, u32[]{:S(2)}) collective-permute-start(bf16[16,64,256]{2,1,0:T(8,128)(2,1)S(1)} %pad_maximum_fusion.1), channel_id=1, source_target_pairs={{0,1},{1,0},{2,3},{3,2},{4,5},{5,4},{6,7},{7,6},{8,9},{9,8},{10,11... | collective-permute-start | bytes 1572872 | tf_op jit(solution)/shard_map/ppermute | solution.py:413

commit v6 on v5

--- a/solution.py
+++ b/solution.py
@@ -206,7 +206,7 @@
 def side_kernel(
     context, forth, back, far, rims, others, other_far, noise, above, below, sums, by_row, rim_sums, w_side, w_reset, w_rest,
     active, offset, out, raw, taps, rim_taps, reset_taps,
-    rest_taps, update, partial, rows_done, rims_buf, context_rim, piece_sems, rim_sems,
+    rest_taps, update, partial, rows_done, rims_buf, context_rim, chunk, piece_sems, rim_sems,
 ):
     step = pl.program_id(0)
     parts = ((0, CHUNK), (CHUNK, CHUNK), (2 * CHUNK, ROWS - 2 * CHUNK))
@@ -283,7 +283,7 @@
             context_rim[n] = inside(joined, not_first if n < HALO else not_last).astype(BF16)
         for copy in first_half:
             copy.wait()
-        chunk = jnp.transpose(raw[:, :CHUNK, :], (1, 0, 2))[:AHEAD]
+        chunk[...] = jnp.transpose(raw[:, :CHUNK, :], (1, 0, 2))
         for n in range(HALO):
             noise_rim = inside(above[n, STATE_CH : STATE_CH + 16], not_first)
             put_taps(rim_taps, n * C3, jnp.concatenate([context_rim[n], noise_rim], axis=0))
@@ -311,8 +311,6 @@
         used = (active[n, owner] == 1) & (offset[n, owner] < REACH)
         chosen = chosen | ((tile == n) & used)
     later = pl.multiple_of(jnp.minimum(step + 1, STEPS - 1) * CHUNK, CHUNK)
-    chunk = jnp.transpose(raw[:, pl.ds(here, CHUNK), :], (1, 0, 2))
-    following = jnp.transpose(raw[:, pl.ds(later, CHUNK), :], (1, 0, 2))
 
     def candidate(n, side_terms):
         slot = n + 1
@@ -337,6 +335,9 @@
         if place < CHUNK:
             put_taps(taps, place * C3, chunk[place])
             continue
+        if place == CHUNK:
+            following = jnp.transpose(raw[:, pl.ds(later, CHUNK), :], (1, 0, 2))
+            chunk[...] = following
         row = following[place - CHUNK]
         if place < CHUNK + HALO:
             noise_rim = inside(below[place - CHUNK, STATE_CH : STATE_CH + 16], not_last)
@@ -379,6 +380,7 @@
             pltpu.VMEM((CHUNK, STATE_CH, COLS), BF16),
             pltpu.VMEM((8, 2 * HALO * RIM_CH, COLS), BF16),
             pltpu.VMEM((2 * HALO, CONTEXT_CH, COLS), BF16),
+            pltpu.VMEM((CHUNK, SIDE_CH, COLS), BF16),
             pltpu.SemaphoreType.DMA((3, 9)),
             pltpu.SemaphoreType.DMA((8,)),
         ],
@@ -418,7 +420,7 @@
     above = lax.ppermute(low, "space", [(n, (n + 1) % owners) for n in range(owners)])
     below = lax.ppermute(top, "space", [((n + 1) % owners, n) for n in range(owners)])
     gate_kernel, candidate_kernel = by_tap(gate_kernel), by_tap(candidate_kernel)
-    state, top = lax.optimization_barrier((state, top))
+    gate_kernel, top = lax.optimization_barrier((gate_kernel, top))
     (state_weights,) = laid_out(state_weights_kernel, "state_weights", [(2 * STATE_CH, 3 * S3)], gate_kernel)
     before = state_part(0, 2, state, state_weights)
 

time: 53.2 us -> 53.5 us (level)
  transfers between devices with their start and end apart: 9 -> 9, of which waited for: 2 -> 2; matrix products, arithmetic and copies ran while one was open for 0% -> 0% of each run, Pallas kernels for 21% -> 20%
where the time goes in v6:
time: 53.5 us; the launch traced here: 53.4 us
  Pallas kernels  31.6 us (59%)
  starting transfers between devices  16.7 us (31%)
  waiting for transfers between devices  3.22 us (6%)
  local copies, waits for them, and re-layouts  1.21 us (2%)
    pallas_call x1, Pallas kernels, side_part(): pl.pallas_call(side_kernel, grid=(STEPS,), in_specs=[any_space] * (len(pi...  20.8 us
    pallas_call x3, Pallas kernels, state_part(): pl.pallas_call(functools.partial(state_kernel, first, count), grid=(count...  8.68 us
    ppermute x1, starting transfers between devices, shards(): lax.ppermute(top, 'space', [((n + 1) % owners, n) for n in range(owners)])  4.65 us
    ppermute x1, starting transfers between devices, shards(): lax.ppermute(rim, 'member', along_x(2))  3.74 us
    ppermute x1, waiting for transfers between devices, shards(): lax.ppermute(rim, 'member', BACK)  2.12 us
    ppermute x1, starting transfers between devices, shards(): back = lax.ppermute(context_field, 'member', BACK)  2.04 us
    ppermute x1, starting transfers between devices, shards(): lax.ppermute(low, 'space', [(n, (n + 1) % owners) for n in range(owners)])  1.84 us
    ppermute x2, starting transfers between devices, to_core(): return lax.ppermute(a, 'member', CORES)  1.71 us
  transfers between devices with their start and end apart: 9, of which 2 were waited for; matrix products, arithmetic and copies ran while one was open for 0% of the time, Pallas kernels for 20%

profile of v6, /device:TPU:1, one launch (start us, length us, event | category | flops | bytes accessed | tf_op | source)
XLA Modules:
  0.0 53.4 jit_solution(5593950043913496640)
XLA Ops:
  0.0 2.0 %collective-permute-start.1 = (bf16[12,64,256]{2,1,0:T(8,128)(2,1)}, bf16[12,64,256]{2,1,0:T(8,128)(2,1)S(1)}, u32[]{:S(2)}, u32[]{:S(2)}) collective-permute-start(bf16[12,64,256]{2,1,0:T(8,128)(2,1)} %context.3), channel_id=1, source_target_pairs={{2,0},{7,1},{4,2},{1,3},{6,4},{3,5},{0,6},{5,7},{10,8},{15,9},{12,... | collective-permute-start | bytes 1179656 | tf_op jit(solution)/shard_map/ppermute | solution.py:418
  2.0 1.3 %collective-permute-start = (bf16[12,64,256]{2,1,0:T(8,128)(2,1)}, bf16[12,64,256]{2,1,0:T(8,128)(2,1)S(1)}, u32[]{:S(2)}, u32[]{:S(2)}) collective-permute-start(bf16[12,64,256]{2,1,0:T(8,128)(2,1)} %context.3), channel_id=1, source_target_pairs={{0,2},{1,7},{2,4},{3,1},{4,6},{5,3},{6,0},{7,5},{8,10},{9,15},{10,... | collective-permute-start | bytes 1179656 | tf_op jit(solution)/shard_map/ppermute | solution.py:417
  3.4 1.6 %edges.1 = (bf16[2,128,256]{2,1,0:T(8,128)(2,1)S(1)}, bf16[2,128,256]{2,1,0:T(8,128)(2,1)S(1)}) custom-call(bf16[96,64,256]{2,1,0:T(8,128)(2,1)} %bitcast.12, bf16[8,64,256]{2,1,0:T(8,128)(2,1)} %bitcast.22, bf16[12,64,256]{2,1,0:T(8,128)(2,1)} %context.3), custom_call_target="tpu_custom_call" | custom-call | bytes 4000000 | tf_op jit(solution)/shard_map/edges/pallas_call | solution.py:68
  5.0 1.8 %collective-permute-start.2 = (bf16[2,128,256]{2,1,0:T(8,128)(2,1)S(1)}, bf16[2,128,256]{2,1,0:T(8,128)(2,1)S(1)}, u32[]{:S(2)}, u32[]{:S(2)}) collective-permute-start(bf16[2,128,256]{2,1,0:T(8,128)(2,1)S(1)} %get-tuple-element.40), channel_id=1, source_target_pairs={{0,8},{8,16},{16,24},{24,32},{32,40},{40,48},{48,56},{56,64},{64,7... | collective-permute-start | bytes 393224 | tf_op jit(solution)/shard_map/ppermute | solution.py:420
  6.9 4.7 %collective-permute-start.3 = (bf16[2,128,256]{2,1,0:T(8,128)(2,1)S(1)}, bf16[2,128,256]{2,1,0:T(8,128)(2,1)S(1)}, u32[]{:S(2)}, u32[]{:S(2)}) collective-permute-start(bf16[2,128,256]{2,1,0:T(8,128)(2,1)S(1)} %get-tuple-element.45.refs_5_), channel_id=1, source_target_pairs={{8,0},{16,8},{24,16},{32,24},{40,32},{48,40},{56,48},{64,56},{72,6... | collective-permute-start | bytes 393224 | tf_op jit(solution)/shard_map/ppermute | solution.py:421
  11.5 1.2 %copy-done.1 = bf16[192,200,3,3]{1,0,3,2:T(8,128)(2,1)S(1)} copy-done((bf16[192,200,3,3]{1,0,3,2:T(8,128)(2,1)S(1)}, bf16[192,200,3,3]{1,0,3,2:T(8,128)(2,1)}, u32[]{:S(2)}) %copy-start.1) | copy-done | bytes 691224
  12.7 0.1 state_weights.1.refs_2_
  12.8 0.0 copy-start.3
  12.8 4.6 %state_part_0.1 = (f32[64,192,256]{2,1,0:T(8,128)S(1)}, bf16[64,96,256]{2,1,0:T(8,128)(2,1)S(1)}) custom-call(bf16[96,64,256]{2,1,0:T(8,128)(2,1)S(1)} %bitcast.13, bf16[96,64,256]{2,1,0:T(8,128)(2,1)S(1)} %bitcast.14, bf16[192,864]{1,0:T(8,128)(2,1)S(1)} %state_weights.1.refs_2_), custom_call_target="tpu_custom_call" | custom-call | flops 6000000000 | bytes 10000000 | tf_op jit(solution)/shard_map/state_part_0/pallas_call | solution.py:181
  17.4 0.0 collective-permute-done.2.refs_3_.above
  17.4 0.0 collective-permute-done.3.refs_4_.below
  17.5 0.0 collective-permute-done.1.back
  17.5 0.0 collective-permute-done.forth
  17.6 1.3 %collective-permute-start.6 = (bf16[13,64,256]{2,1,0:T(8,128)(2,1)S(1)}, bf16[13,64,256]{2,1,0:T(8,128)(2,1)S(1)}, u32[]{:S(2)}, u32[]{:S(2)}) collective-permute-start(bf16[13,64,256]{2,1,0:T(8,128)(2,1)S(1)} %pad_maximum_fusion.2), channel_id=1, source_target_pairs={{0,2},{1,7},{2,4},{3,1},{4,6},{5,3},{6,0},{7,5},{8,10},{9,15},{10,... | collective-permute-start | bytes 1277960 | tf_op jit(solution)/shard_map/ppermute | solution.py:430
  18.9 0.1 pad_maximum_fusion
  19.0 0.6 %collective-permute-start.7 = (bf16[36,64,256]{2,1,0:T(8,128)(2,1)S(1)}, bf16[36,64,256]{2,1,0:T(8,128)(2,1)S(1)}, u32[]{:S(2)}, u32[]{:S(2)}) collective-permute-start(bf16[36,64,256]{2,1,0:T(8,128)(2,1)S(1)} %pad_maximum_fusion), channel_id=1, source_target_pairs={{0,1},{1,0},{2,3},{3,2},{4,5},{5,4},{6,7},{7,6},{8,9},{9,8},{10,11... | collective-permute-start | bytes 3538952 | tf_op jit(solution)/shard_map/ppermute | solution.py:415
  19.6 2.0 %state_part_2.1 = (f32[64,192,256]{2,1,0:T(8,128)S(1)}, bf16[64,96,256]{2,1,0:T(8,128)(2,1)S(1)}) custom-call(bf16[96,64,256]{2,1,0:T(8,128)(2,1)S(1)} %bitcast.15, bf16[96,64,256]{2,1,0:T(8,128)(2,1)S(1)} %bitcast.16, bf16[192,864]{1,0:T(8,128)(2,1)S(1)} %state_weights.1.refs_2_, ...), custom_call_target="tpu_custom_call", output_to_operand_aliasing={{0}: (3, {}), {1}: (4, {})} | custom-call | flops 3000000000 | bytes 5000000 | tf_op jit(solution)/shard_map/state_part_2/pallas_call | solution.py:181
  21.6 0.0 copy-start.2
  21.6 0.0 copy-start.4
  21.6 0.0 copy-start.5
  21.7 0.0 copy-start.6
  21.7 0.0 copy-start.7
  21.7 3.7 %collective-permute-start.5 = (bf16[1,64,256]{2,1,0:T(8,128)(2,1)S(1)}, bf16[1,64,256]{2,1,0:T(8,128)(2,1)S(1)}, u32[]{:S(2)}, u32[]{:S(2)}) collective-permute-start(bf16[1,64,256]{2,1,0:T(8,128)(2,1)S(1)} %bitcast.27), channel_id=1, source_target_pairs={{0,4},{1,5},{2,6},{3,7},{4,0},{5,1},{6,2},{7,3},{8,12},{9,13},{10,... | collective-permute-start | bytes 98312 | tf_op jit(solution)/shard_map/ppermute | solution.py:435
  25.4 0.0 collective-permute-start.4
  25.4 2.1 %state_part_3.1 = (f32[64,192,256]{2,1,0:T(8,128)S(1)}, bf16[64,96,256]{2,1,0:T(8,128)(2,1)S(1)}, f32[2,192,256]{2,1,0:T(8,128)S(1)}) custom-call(bf16[96,64,256]{2,1,0:T(8,128)(2,1)S(1)} %bitcast.17, bf16[96,64,256]{2,1,0:T(8,128)(2,1)S(1)} %bitcast.18, bf16[192,864]{1,0:T(8,128)(2,1)S(1)} %state_weights.1.refs_2_, ...), custom_call_target="tpu_custom_call", output_to_operand_aliasing={{0}: (6, {}), {1}: (7, {})} | custom-call | flops 3000000000 | bytes 5000000 | tf_op jit(solution)/shard_map/state_part_3/pallas_call | solution.py:181
  27.6 0.0 collective-permute-done.5
  27.6 2.1 %collective-permute-done.4 = bf16[1,64,256]{2,1,0:T(8,128)(2,1)S(1)} collective-permute-done((bf16[1,64,256]{2,1,0:T(8,128)(2,1)S(1)}, bf16[1,64,256]{2,1,0:T(8,128)(2,1)S(1)}, u32[]{:S(2)}, u32[]{:S(2)}) %collective-permute-start.4) | collective-permute-done | bytes 32800 | tf_op jit(solution)/shard_map/ppermute | solution.py:435
  29.7 0.1 pad_maximum_fusion.1
  29.8 1.1 %collective-permute-start.8 = (bf16[16,64,256]{2,1,0:T(8,128)(2,1)S(1)}, bf16[16,64,256]{2,1,0:T(8,128)(2,1)S(1)}, u32[]{:S(2)}, u32[]{:S(2)}) collective-permute-start(bf16[16,64,256]{2,1,0:T(8,128)(2,1)S(1)} %pad_maximum_fusion.1), channel_id=1, source_target_pairs={{0,1},{1,0},{2,3},{3,2},{4,5},{5,4},{6,7},{7,6},{8,9},{9,8},{10,11... | collective-permute-start | bytes 1572872 | tf_op jit(solution)/shard_map/ppermute | solution.py:415
  30.9 0.4 side_weights.1
  31.3 1.1 %collective-permute-done.8.other_far = bf16[16,64,256]{2,1,0:T(8,128)(2,1)S(1)} collective-permute-done((bf16[16,64,256]{2,1,0:T(8,128)(2,1)S(1)}, bf16[16,64,256]{2,1,0:T(8,128)(2,1)S(1)}, u32[]{:S(2)}, u32[]{:S(2)}) %collective-permute-start.8) | collective-permute-done | bytes 524320 | tf_op jit(solution)/shard_map/ppermute | solution.py:415
  32.4 20.8 %side_part.1 = bf16[96,64,256]{2,1,0:T(8,128)(2,1)} custom-call(bf16[12,64,256]{2,1,0:T(8,128)(2,1)S(1)} %copy-done.3, bf16[12,64,256]{2,1,0:T(8,128)(2,1)S(1)} %collective-permute-done.forth, bf16[12,64,256]{2,1,0:T(8,128)(2,1)S(1)} %collective-permute-done.1.back, bf16[13,64,256]{2,1,0:T(8,128)(2,1)S(1)} %collective-permute-done.6.far, ...), custom_call_target="tpu_custom_call" | custom-call | flops 16999999488 | bytes 20000000 | tf_op jit(solution)/shard_map/side_part/pallas_call | solution.py:362
  (16 shorter events, 0.1 us)
Async XLA Ops:
  0.0 12.8 %copy-start = (bf16[1,96,64,256]{3,2,1,0:T(8,128)(2,1)S(1)}, bf16[1,96,64,256]{3,2,1,0:T(8,128)(2,1)}, u32[]{:S(2)}) copy-start(bf16[1,96,64,256]{3,2,1,0:T(8,128)(2,1)} %param.7) | copy-start | bytes 9437188
  0.0 17.5 %collective-permute-start.1 = (bf16[12,64,256]{2,1,0:T(8,128)(2,1)}, bf16[12,64,256]{2,1,0:T(8,128)(2,1)S(1)}, u32[]{:S(2)}, u32[]{:S(2)}) collective-permute-start(bf16[12,64,256]{2,1,0:T(8,128)(2,1)} %context.3), channel_id=1, source_target_pairs={{2,0},{7,1},{4,2},{1,3},{6,4},{3,5},{0,6},{5,7},{10,8},{15,9},{12,... | collective-permute-start | bytes 1179656 | tf_op jit(solution)/shard_map/ppermute | solution.py:418
  2.0 15.4 %collective-permute-start = (bf16[12,64,256]{2,1,0:T(8,128)(2,1)}, bf16[12,64,256]{2,1,0:T(8,128)(2,1)S(1)}, u32[]{:S(2)}, u32[]{:S(2)}) collective-permute-start(bf16[12,64,256]{2,1,0:T(8,128)(2,1)} %context.3), channel_id=1, source_target_pairs={{0,2},{1,7},{2,4},{3,1},{4,6},{5,3},{6,0},{7,5},{8,10},{9,15},{10,... | collective-permute-start | bytes 1179656 | tf_op jit(solution)/shard_map/ppermute | solution.py:417
  5.0 12.4 %collective-permute-start.2 = (bf16[2,128,256]{2,1,0:T(8,128)(2,1)S(1)}, bf16[2,128,256]{2,1,0:T(8,128)(2,1)S(1)}, u32[]{:S(2)}, u32[]{:S(2)}) collective-permute-start(bf16[2,128,256]{2,1,0:T(8,128)(2,1)S(1)} %get-tuple-element.40), channel_id=1, source_target_pairs={{0,8},{8,16},{16,24},{24,32},{32,40},{40,48},{48,56},{56,64},{64,7... | collective-permute-start | bytes 393224 | tf_op jit(solution)/shard_map/ppermute | solution.py:420
  6.9 10.6 %collective-permute-start.3 = (bf16[2,128,256]{2,1,0:T(8,128)(2,1)S(1)}, bf16[2,128,256]{2,1,0:T(8,128)(2,1)S(1)}, u32[]{:S(2)}, u32[]{:S(2)}) collective-permute-start(bf16[2,128,256]{2,1,0:T(8,128)(2,1)S(1)} %get-tuple-element.45.refs_5_), channel_id=1, source_target_pairs={{8,0},{16,8},{24,16},{32,24},{40,32},{48,40},{56,48},{64,56},{72,6... | collective-permute-start | bytes 393224 | tf_op jit(solution)/shard_map/ppermute | solution.py:421
  11.5 1.2 %copy-start.1 = (bf16[192,200,3,3]{1,0,3,2:T(8,128)(2,1)S(1)}, bf16[192,200,3,3]{1,0,3,2:T(8,128)(2,1)}, u32[]{:S(2)}) copy-start(bf16[192,200,3,3]{1,0,3,2:T(8,128)(2,1)} %param.10) | copy-start | bytes 2073604
  12.8 6.1 %copy-start.3 = (bf16[12,64,256]{2,1,0:T(8,128)(2,1)S(1)}, bf16[12,64,256]{2,1,0:T(8,128)(2,1)}, u32[]{:S(2)}) copy-start(bf16[12,64,256]{2,1,0:T(8,128)(2,1)} %context.3) | copy-start | bytes 1179652
  17.6 12.1 %collective-permute-start.6 = (bf16[13,64,256]{2,1,0:T(8,128)(2,1)S(1)}, bf16[13,64,256]{2,1,0:T(8,128)(2,1)S(1)}, u32[]{:S(2)}, u32[]{:S(2)}) collective-permute-start(bf16[13,64,256]{2,1,0:T(8,128)(2,1)S(1)} %pad_maximum_fusion.2), channel_id=1, source_target_pairs={{0,2},{1,7},{2,4},{3,1},{4,6},{5,3},{6,0},{7,5},{8,10},{9,15},{10,... | collective-permute-start | bytes 1277960 | tf_op jit(solution)/shard_map/ppermute | solution.py:430
  19.0 13.4 %collective-permute-start.7 = (bf16[36,64,256]{2,1,0:T(8,128)(2,1)S(1)}, bf16[36,64,256]{2,1,0:T(8,128)(2,1)S(1)}, u32[]{:S(2)}, u32[]{:S(2)}) collective-permute-start(bf16[36,64,256]{2,1,0:T(8,128)(2,1)S(1)} %pad_maximum_fusion), channel_id=1, source_target_pairs={{0,1},{1,0},{2,3},{3,2},{4,5},{5,4},{6,7},{7,6},{8,9},{9,8},{10,11... | collective-permute-start | bytes 3538952 | tf_op jit(solution)/shard_map/ppermute | solution.py:415
  21.6 9.3 %copy-start.2 = (bf16[192,200,3,3]{1,0,3,2:T(8,128)(2,1)S(1)}, bf16[192,200,3,3]{1,0,3,2:T(8,128)(2,1)}, u32[]{:S(2)}) copy-start(bf16[192,200,3,3]{1,0,3,2:T(8,128)(2,1)} %param.10) | copy-start | bytes 2073604
  21.6 9.3 %copy-start.4 = (bf16[96,200,3,3]{1,0,3,2:T(8,128)(2,1)S(1)}, bf16[96,200,3,3]{1,0,3,2:T(8,128)(2,1)}, u32[]{:S(2)}) copy-start(bf16[96,200,3,3]{1,0,3,2:T(8,128)(2,1)} %param.11) | copy-start | bytes 1036804
  21.6 10.8 %copy-start.5 = (bf16[1,1,8,64,256]{4,3,2,1,0:T(8,128)(2,1)S(1)}, bf16[1,1,8,64,256]{4,3,2,1,0:T(8,128)(2,1)}, u32[]{:S(2)}) copy-start(bf16[1,1,8,64,256]{4,3,2,1,0:T(8,128)(2,1)} %param.9) | copy-start | bytes 786436
  21.7 10.8 %copy-start.6 = (s32[16,4]{0,1:T(4,128)S(1)}, s32[16,4]{0,1:T(4,128)}, u32[]{:S(2)}) copy-start(s32[16,4]{0,1:T(4,128)} %param.12) | copy-start | bytes 772
  21.7 10.8 %copy-start.7 = (s32[16,4]{0,1:T(4,128)S(1)}, s32[16,4]{0,1:T(4,128)}, u32[]{:S(2)}) copy-start(s32[16,4]{0,1:T(4,128)} %param.13) | copy-start | bytes 772
  21.7 5.9 %collective-permute-start.5 = (bf16[1,64,256]{2,1,0:T(8,128)(2,1)S(1)}, bf16[1,64,256]{2,1,0:T(8,128)(2,1)S(1)}, u32[]{:S(2)}, u32[]{:S(2)}) collective-permute-start(bf16[1,64,256]{2,1,0:T(8,128)(2,1)S(1)} %bitcast.27), channel_id=1, source_target_pairs={{0,4},{1,5},{2,6},{3,7},{4,0},{5,1},{6,2},{7,3},{8,12},{9,13},{10,... | collective-permute-start | bytes 98312 | tf_op jit(solution)/shard_map/ppermute | solution.py:435
  25.4 4.3 %collective-permute-start.4 = (bf16[1,64,256]{2,1,0:T(8,128)(2,1)S(1)}, bf16[1,64,256]{2,1,0:T(8,128)(2,1)S(1)}, u32[]{:S(2)}, u32[]{:S(2)}) collective-permute-start(bf16[1,64,256]{2,1,0:T(8,128)(2,1)S(1)} %bitcast.28), channel_id=1, source_target_pairs={{2,0},{7,1},{4,2},{1,3},{6,4},{3,5},{0,6},{5,7},{10,8},{15,9},{12,... | collective-permute-start | bytes 98312 | tf_op jit(solution)/shard_map/ppermute | solution.py:435
  29.8 2.6 %collective-permute-start.8 = (bf16[16,64,256]{2,1,0:T(8,128)(2,1)S(1)}, bf16[16,64,256]{2,1,0:T(8,128)(2,1)S(1)}, u32[]{:S(2)}, u32[]{:S(2)}) collective-permute-start(bf16[16,64,256]{2,1,0:T(8,128)(2,1)S(1)} %pad_maximum_fusion.1), channel_id=1, source_target_pairs={{0,1},{1,0},{2,3},{3,2},{4,5},{5,4},{6,7},{7,6},{8,9},{9,8},{10,11... | collective-permute-start | bytes 1572872 | tf_op jit(solution)/shard_map/ppermute | solution.py:415
